TPU v7x, 32 devices: a whole 2x2x4 slice. The times are simulated.
32 devices in a mesh: rep: 2 (over x), tp: 16 (over z, y, core).
Axes of the slice: x: 2, y: 2, z: 4, core: 2. Of those that a mesh axis runs over, the one named last changes fastest.
Arguments:
- tokens: bfloat16 [512, 8192], P(('rep', 'tp')), parts along dimension 0, may hold values from -6 to 6
- cotangent: bfloat16 [10240, 512], P('tp', 'rep'), parts along dimension 1, may hold values from -6 to 6
- joined_weight: bfloat16 [10240, 8192], P('tp'), may hold values from -0.0625 to 0.0625
- adapter_down_maps: bfloat16 [64, 16, 8192], P(None, None, 'tp'), may hold values from -0.0625 to 0.0625
- adapter_up_maps: bfloat16 [10240, 1024], P('tp'), may hold values from -0.0625 to 0.0625
- adapter_token_lengths: int32 [128], P('rep'), parts along dimension 0, may hold values from 1 to 16, 256 in all
- adapter_storage_slot: int32 [64], replicated, may hold values from 0 to 63, each once
Outputs:
- grad_tokens: bfloat16 [512, 8192], P(('rep', 'tp')), parts along dimension 0
- down_map_gradient: float32 [128, 16, 8192], P('rep', None, 'tp'), parts along dimension 0
- up_map_gradient: float32 [10240, 2048], P('tp', 'rep'), parts along dimension 1
There are 2 independent parts, one for each index of `rep`. A program takes and returns all parts, laid end to end along the dimension named above; an argument that names none is the same for every part. Nothing has to cross between parts.
Inputs may be any that keep to these rules, and one draw needn't show every extreme that they name: `adapter_token_lengths`: they sum to 256; tokens are ordered by adapter. `adapter_storage_slot`: A permutation.
All inputs are finite; a program needn't handle non-finite values.
Results may differ from a plain program's by a relative error of at most 0.0051.
Values may be sent and summed in bfloat16 or wider, within the bound.
No kernel may reach another device: no remote copies, remote signals or barrier semaphores. Data moves between devices by JAX's collectives and lax.ppermute only.
A program may use at most 128 MiB of HBM per device.

v0:
```python
import jax
import jax.numpy as jnp
from jax import lax
from jax.sharding import PartitionSpec as P

ADAPTER_SCALE = 2.0
eps = 1e-06


def body(
    tokens,
    cotangent,
    joined_weight,
    adapter_down_maps,
    adapter_up_maps,
    adapter_token_lengths,
    adapter_storage_slot,
):
    tp_count = lax.axis_size("tp")
    my_index = lax.axis_index("tp")
    tok_dev = tokens.shape[0]
    all_rows = tok_dev * tp_count
    most_rows = all_rows // 16
    adapter_list = adapter_down_maps.shape[0]
    rank_width = adapter_down_maps.shape[1]
    feature_share = adapter_down_maps.shape[2]
    column_share = cotangent.shape[0]
    contract_token_rows = (((0,), (0,)), ((), ()))
    seg_ends = jnp.cumsum(adapter_token_lengths)
    starts = seg_ends - adapter_token_lengths
    position = jnp.arange(all_rows, dtype=jnp.int32)[:, None]
    adapter_of = jnp.sum((position >= seg_ends[None, :]).astype(jnp.int32), axis=1)
    token_slot = jnp.take(adapter_storage_slot, adapter_of, axis=0)
    permuted = (
        adapter_storage_slot[:, None] == jnp.arange(adapter_list, dtype=jnp.int32)[None, :]
    ).astype(jnp.float32)
    as_float = tokens.astype(jnp.float32)
    inv_rms = lax.rsqrt(jnp.mean(as_float * as_float, axis=1, keepdims=True) + eps)
    normed = as_float * inv_rms
    normed_halfwidth = normed.astype(jnp.bfloat16)
    normed_cols = lax.all_to_all(normed_halfwidth, "tp", split_axis=1, concat_axis=0, tiled=True)
    down_per_token = jnp.take(adapter_down_maps, token_slot, axis=0)
    up_per_token = jnp.take(
        adapter_up_maps.reshape(column_share, adapter_list, rank_width), token_slot, axis=1
    )
    low_part = jnp.einsum(
        "td,trd->tr", normed_cols, down_per_token, preferred_element_type=jnp.float32
    )
    back_part = jnp.einsum(
        "ct,ctr->tr", cotangent, up_per_token, preferred_element_type=jnp.float32
    )
    low_sum, back_sum = lax.psum((low_part, back_part), "tp")
    low_bf = low_sum.astype(jnp.bfloat16)
    back_bf = back_sum.astype(jnp.bfloat16)
    adapter_term = ADAPTER_SCALE * jnp.einsum(
        "tr,trd->td", back_bf, down_per_token, preferred_element_type=jnp.float32
    )
    padded_cot = jnp.pad(cotangent, ((0, 0), (0, most_rows)))
    padded_low = jnp.pad(low_bf, ((0, most_rows), (0, 0)))
    padded_back = jnp.pad(back_bf, ((0, most_rows), (0, 0)))
    padded_norm = jnp.pad(normed_cols, ((0, most_rows), (0, 0)))
    offsets = jnp.arange(most_rows, dtype=jnp.int32)[:, None]

    def one_segment(which):
        begin = starts[which]
        keep = offsets < adapter_token_lengths[which]
        low_seg = jnp.where(
            keep,
            lax.dynamic_slice_in_dim(padded_low, begin, most_rows, 0),
            jnp.zeros((), jnp.bfloat16),
        )
        back_seg = jnp.where(
            keep,
            lax.dynamic_slice_in_dim(padded_back, begin, most_rows, 0),
            jnp.zeros((), jnp.bfloat16),
        )
        cot_seg = lax.dynamic_slice_in_dim(padded_cot, begin, most_rows, 1)
        norm_seg = lax.dynamic_slice_in_dim(padded_norm, begin, most_rows, 0)
        up_grad = jnp.dot(cot_seg, low_seg, preferred_element_type=jnp.float32)
        down_grad = lax.dot_general(
            back_seg, norm_seg, contract_token_rows, preferred_element_type=jnp.float32
        )
        return (up_grad, down_grad)

    up_each, down_each = lax.map(one_segment, jnp.arange(adapter_list, dtype=jnp.int32))
    up_map_gradient = ADAPTER_SCALE * jnp.einsum(
        "as,acr->csr", permuted, up_each, precision=lax.Precision.HIGHEST
    )
    up_map_gradient = up_map_gradient.reshape(column_share, adapter_list * rank_width)
    down_map_gradient = ADAPTER_SCALE * jnp.einsum(
        "as,ard->srd", permuted, down_each, precision=lax.Precision.HIGHEST
    )
    matrix_product = lax.dot_general(
        cotangent, joined_weight, contract_token_rows, preferred_element_type=jnp.float32
    )
    column_offset = my_index * feature_share
    current_adapter = lax.dynamic_slice_in_dim(matrix_product, column_offset, feature_share, 1)
    normed_gradient = lax.psum_scatter(
        lax.dynamic_update_slice_in_dim(
            matrix_product, current_adapter + adapter_term, column_offset, 1
        ),
        "tp",
        scatter_dimension=0,
        tiled=True,
    )
    mean_term = jnp.mean(normed_gradient * normed, axis=1, keepdims=True)
    grad_tokens = (inv_rms * (normed_gradient - normed * mean_term)).astype(jnp.bfloat16)
    return (grad_tokens, down_map_gradient, up_map_gradient)


def solution(mesh):
    in_specs = (
        P(("rep", "tp"), None),
        P("tp", "rep"),
        P("tp", None),
        P(None, None, "tp"),
        P("tp", None),
        P("rep"),
        P(),
    )
    out_specs = (P(("rep", "tp"), None), P("rep", None, "tp"), P("tp", "rep"))
    return jax.shard_map(body, mesh=mesh, in_specs=in_specs, out_specs=out_specs, check_vma=False)
```

profile of v0, /device:TPU:0, one launch (start us, length us, event | category | flops | bytes accessed | tf_op | source)
XLA Modules:
  0.0 817.5 jit_solution(18338151603721491715)
XLA Ops:
  10.2 7.4 all-to-all-start
  23.1 2.8 gather_fusion.2
  25.9 3.5 gather_fusion.1
  29.6 5.6 multiply_reduce_fusion
  35.4 9.7 %fusion.36 = f32[256,8192]{1,0:T(8,128)} fusion(bf16[640,256]{1,0:T(8,128)(2,1)S(1)} %copy-done.3, bf16[640,8192]{1,0:T(8,128)(2,1)} %param.11), kind=kOutput, calls=%fused_computation.62 | convolution fusion | flops 2684354560 | bytes 19202048 | tf_op jit(solution)/shard_map/dot_general | solution.py:93
  45.1 4.0 fusion.16
  49.2 61.9 %all-reduce.4 = (bf16[256,16]{0,1:T(8,128)(2,1)S(1)}, bf16[256,16]{0,1:T(8,128)(2,1)S(1)}) all-reduce(f32[256,16]{0,1:T(8,128)S(1)} %copy.44, f32[256,16]{0,1:T(8,128)S(1)} %bitcast.66), channel_id=1, replica_groups=mesh['rep'=2,'tp'=16] {'tp'}, use_global_device_ids=true, to_apply=%region_3.4 | all-reduce | flops 8192 | bytes 49152 | tf_op jit(solution)/shard_map/psum | solution.py:52
  111.2 3.0 fusion.17
  114.2 2.0 fusion.27
  116.9 677.0 %while.13 = (s32[]{:T(128)}, f32[64,640,16]{1,0,2:T(8,128)}, f32[64,16,512]{2,0,1:T(8,128)}, s32[64]{0:T(128)S(1)}, s32[64]{0:T(128)S(1)}, /*index=5*/bf16[640,2...) while((s32[]{:T(128)}, f32[64,640,16]{1,0,2:T(8,128)}, ...), condition=%wide.region_8.9_spmd.clone, body=%wide.region_7.8_spmd.clone.sunk | while | flops 590360 | bytes 560393 | solution.py:85
  123.5 2.0 dynamic_update_slice.17
  134.2 2.0 dynamic_update_slice.17
  144.8 2.0 dynamic_update_slice.17
  155.4 2.0 dynamic_update_slice.17
  166.0 2.0 dynamic_update_slice.17
  176.6 2.0 dynamic_update_slice.17
  187.2 2.0 dynamic_update_slice.17
  197.7 2.0 dynamic_update_slice.17
  208.3 2.0 dynamic_update_slice.17
  218.9 2.0 dynamic_update_slice.17
  229.5 2.0 dynamic_update_slice.17
  240.1 2.0 dynamic_update_slice.17
  250.7 2.0 dynamic_update_slice.17
  261.2 2.0 dynamic_update_slice.17
  271.8 2.0 dynamic_update_slice.17
  282.4 2.0 dynamic_update_slice.17
  292.9 2.0 dynamic_update_slice.17
  303.5 2.0 dynamic_update_slice.17
  314.1 2.0 dynamic_update_slice.17
  324.7 2.0 dynamic_update_slice.17
  335.2 2.0 dynamic_update_slice.17
  345.8 2.0 dynamic_update_slice.17
  356.4 2.0 dynamic_update_slice.17
  367.0 2.0 dynamic_update_slice.17
  377.5 2.0 dynamic_update_slice.17
  388.1 2.0 dynamic_update_slice.17
  398.7 2.0 dynamic_update_slice.17
  409.3 2.0 dynamic_update_slice.17
  419.8 2.0 dynamic_update_slice.17
  430.4 2.0 dynamic_update_slice.17
  441.0 2.0 dynamic_update_slice.17
  451.6 2.0 dynamic_update_slice.17
  462.1 2.0 dynamic_update_slice.17
  472.7 2.0 dynamic_update_slice.17
  483.3 2.0 dynamic_update_slice.17
  493.9 2.0 dynamic_update_slice.17
  504.4 2.0 dynamic_update_slice.17
  515.0 2.0 dynamic_update_slice.17
  525.6 2.0 dynamic_update_slice.17
  536.2 2.0 dynamic_update_slice.17
  546.7 2.0 dynamic_update_slice.17
  557.3 2.0 dynamic_update_slice.17
  567.9 2.0 dynamic_update_slice.17
  578.5 2.0 dynamic_update_slice.17
  589.0 2.0 dynamic_update_slice.17
  599.6 2.0 dynamic_update_slice.17
  610.2 2.0 dynamic_update_slice.17
  663.0 2.0 dynamic_update_slice.17
  684.2 2.0 dynamic_update_slice.17
  705.3 2.0 dynamic_update_slice.17
  793.9 3.4 multiply_bitcast_fusion
  797.3 3.1 copy.36
  800.4 3.2 copy.38
  804.9 2.5 copy.37
  (638 shorter events, 343.0 us)
Async XLA Ops:
  7.2 15.9 %copy-start = (bf16[64,16,512]{2,1,0:T(8,128)(2,1)S(1)}, bf16[64,16,512]{2,1,0:T(8,128)(2,1)}, u32[]{:S(2)}) copy-start(bf16[64,16,512]{2,1,0:T(8,128)(2,1)} %param.12) | copy-start | bytes 3145732
  10.2 34.9 %all-to-all-start = ((bf16[16,16,512]{2,0,1:T(8,128)(2,1)}), bf16[16,16,512]{2,0,1:T(8,128)(2,1)S(1)}, u32[]{:S(2)}, u32[]{:S(2)}) async-start(bf16[16,16,512]{2,0,1:T(8,128)(2,1)} %bitcast.48), calls=%async_computation.1 | async-start | bytes 524288 | tf_op jit(solution)/shard_map/all_to_all | solution.py:41
  17.6 789.8 %reduce-scatter.2.cloned.1.call-start = ((), (), s32[]{:S(2)}) async-start(), calls=%async_computation.2 | async-start | bytes 8912896 | tf_op jit(solution)/shard_map/reduce_scatter | solution.py:98
  25.9 3.5 copy-start.3
  116.2 0.7 copy-start.5
  116.2 677.7 %copy-start.1 = (s32[64]{0:T(128)S(1)}, s32[64]{0:T(128)}, u32[]{:S(2)}) copy-start(s32[64]{0:T(128)} %param.15) | copy-start | bytes 772
  797.3 6.3 copy-start.4
  803.6 3.9 copy-start.2
Sparse Core Ops, SparseCore 0:
  116.4 101.8 reduce-scatter.1
where the time goes:
time: 825 us; the launch traced here: 817 us
  local copies, waits for them, and re-layouts  378 us (46%)
  loops' own time  250 us (30%)
  blocking collectives  61.9 us (8%)
  other arithmetic  55.8 us (7%)
  matrix products  49.9 us (6%)
  between operations  14.2 us (2%)
    another operation x1, loops' own time, body(): lax.map(one_segment, jnp.arange(adapter_list, dtype=jnp.int32))  250 us
    dynamic_update_slice x256, local copies, waits for them, and re-layouts, body(): lax.map(one_segment, jnp.arange(adapter_list, dtype=jnp.int32))  244 us
    psum x1, blocking collectives, body(): low_sum, back_sum = lax.psum((low_part, back_part), 'tp')  61.9 us
    lt x64, other arithmetic, one_segment(): keep = offsets < adapter_token_lengths[which]  41.6 us
    dynamic_slice x64, local copies, waits for them, and re-layouts, one_segment(): keep = offsets < adapter_token_lengths[which]  37.7 us
    dynamic_slice x64, local copies, waits for them, and re-layouts, one_segment(): begin = starts[which]  37.5 us
    dynamic_slice x64, local copies, waits for them, and re-layouts, body(): lax.map(one_segment, jnp.arange(adapter_list, dtype=jnp.int32))  37.3 us
  transfers between devices with their start and end apart: 2, of which 0 were waited for; matrix products, arithmetic and copies ran while one was open for 57% of the time, Pallas kernels for 0%

commit v1 on v0

v1 whole, which is shorter than its diff:
```python
import functools

import jax
import jax.numpy as jnp
from jax import lax
from jax.experimental import pallas as pl
from jax.experimental.pallas import tpu as pltpu
from jax.sharding import PartitionSpec as P

SCALE = 2.0
EPS = 1e-06
BF = jnp.bfloat16
F32 = jnp.float32
NT = (((1,), (1,)), ((), ()))
TN = (((0,), (0,)), ((), ()))
VMEM = pl.BlockSpec(memory_space=pltpu.VMEM)
SMEM = pl.BlockSpec(memory_space=pltpu.SMEM)


def stages_of(tp):
    bits = [1 << b for b in range(tp.bit_length() - 1)]
    groups = [bits[:1], bits[1:2]]
    rest = bits[2:]
    groups += [rest[i : i + 2] for i in range(0, len(rest), 2)]
    stages = []
    for group in groups:
        masks = [0]
        for b in group:
            masks = masks + [m | b for m in masks]
        if len(masks) > 1:
            stages.append(masks)
    return stages


def block_order(stages):
    order = [0]
    for masks in stages:
        order = [o | m for o in order for m in masks]
    return order


def iota(shape, dim):
    return lax.broadcasted_iota(jnp.int32, shape, dim)


def membership(lens_ref, slots_ref, rows):
    count = lens_ref.shape[1]
    lens = jnp.broadcast_to(lens_ref[...].astype(F32), (8, count)).astype(BF)
    upto = (iota((count, count), 0) <= iota((count, count), 1)).astype(F32).astype(BF)
    ends = jnp.dot(lens, upto, preferred_element_type=F32)[:1].astype(jnp.int32)
    starts = ends - lens_ref[...]
    position = iota((rows, count), 0)
    member = ((position >= starts) & (position < ends)).astype(F32).astype(BF)
    match = (iota((count, count), 0) == slots_ref[...]).astype(F32).astype(BF)
    return member, match


def mask_by_column(lens_ref, slots_ref, rows, rank):
    member, match = membership(lens_ref, slots_ref, rows)
    chosen = lax.dot_general(match, member, NT, preferred_element_type=F32).astype(BF)
    slots = match.shape[0]
    wide = (iota((slots * rank, slots), 0) // rank == iota((slots * rank, slots), 1)).astype(F32).astype(BF)
    return jnp.dot(wide, chosen, preferred_element_type=F32)


def prep_kernel(order, rank, me_ref, lens_ref, slots_ref, tok_ref, cot_ref, up_ref, send_ref, cotp_ref, cott):
    tp, own, _ = send_ref.shape
    width = tok_ref.shape[1]
    share = width // tp
    rows, _ = cott.shape
    cott[...] = cot_ref[...].astype(F32).T.astype(BF)
    tok = tok_ref[...].astype(F32)
    inv = lax.rsqrt(jnp.mean(tok * tok, axis=1, keepdims=True) + EPS)
    normed = (tok * inv).astype(BF)
    member, match = membership(lens_ref, slots_ref, rows)
    chosen = lax.dot_general(member, match, NT, preferred_element_type=F32).astype(BF)
    slots = match.shape[0]
    wide = (iota((slots, slots * rank), 1) // rank == iota((slots, slots * rank), 0)).astype(F32).astype(BF)
    mask = jnp.dot(chosen, wide, preferred_element_type=F32)
    every = jnp.dot(cott[...], up_ref[...], preferred_element_type=F32) * mask
    lanes = every[:, :128]
    for i in range(1, slots * rank // 128):
        lanes = lanes + every[:, i * 128 : (i + 1) * 128]
    turned = lanes.T
    back = turned[:rank]
    for i in range(1, 128 // rank):
        back = back + turned[i * rank : (i + 1) * rank]
    back = back.astype(BF)
    for q in range(tp):
        send_ref[q, :, :share] = normed[:, q * share : (q + 1) * share]
        send_ref[q, :, share:] = back
    me = me_ref[0]
    for i, mask_bits in enumerate(order):
        source = pl.multiple_of((me ^ mask_bits) * own, own)
        cotp_ref[pl.ds(i * own, own), :] = cott[pl.ds(source, own), :]


def product_kernel(cotp_ref, weight_ref, *parts):
    out = jnp.dot(cotp_ref[...], weight_ref[...], preferred_element_type=F32)
    each = parts[0].shape[0]
    for i, part in enumerate(parts):
        part[...] = out[i * each : (i + 1) * each].astype(BF)


def middle_kernel(rank, lens_ref, slots_ref, recv_ref, down_ref, send_ref, left_ref):
    tp, own, wide = recv_ref.shape
    rows = tp * own
    share = wide - rows
    mask = mask_by_column(lens_ref, slots_ref, rows, rank)
    normed = recv_ref[:, :, :share].reshape(rows, share)
    every = lax.dot_general(down_ref[...], normed, NT, preferred_element_type=F32) * mask
    slots = every.shape[0] // rank
    low = jnp.sum(every.reshape(slots, rank, rows), axis=0).astype(BF)
    back = jnp.sum(recv_ref[:, :, share:].astype(F32), axis=0).astype(BF).astype(F32)
    left = (mask.reshape(slots, rank, rows) * back[None]).reshape(slots * rank, rows).astype(BF)
    left_ref[...] = left
    term = SCALE * lax.dot_general(left, down_ref[...], TN, preferred_element_type=F32)
    send_ref[:, :, :share] = term.astype(BF).reshape(tp, own, share)
    for q in range(tp):
        send_ref[q, :, share:] = low


def down_kernel(left_ref, recv_ref, out_ref):
    tp, own, wide = recv_ref.shape
    rows = tp * own
    share = wide - rows
    normed = recv_ref[:, :, :share].reshape(rows, share)
    out_ref[...] = SCALE * jnp.dot(left_ref[...], normed, preferred_element_type=F32)


def up_kernel(rank, lens_ref, slots_ref, recv_ref, cot_ref, out_ref):
    tp, own, wide = recv_ref.shape
    rows = tp * own
    share = wide - rows
    mask = mask_by_column(lens_ref, slots_ref, rows, rank)
    slots = mask.shape[0] // rank
    low = jnp.sum(recv_ref[:, :, share:].astype(F32), axis=0).astype(BF).astype(F32)
    left = (mask.reshape(slots, rank, rows) * low[None]).reshape(slots * rank, rows).astype(BF)
    out_ref[...] = SCALE * lax.dot_general(cot_ref[...], left, NT, preferred_element_type=F32)


def final_kernel(pieces, recv_ref, tok_ref, *refs):
    out_ref = refs[-1]
    tp, own, _ = recv_ref.shape
    width = tok_ref.shape[1]
    share = width // tp
    chunks = []
    at = 0
    for n in pieces:
        total = refs[at][...].astype(F32)
        for r in refs[at + 1 : at + n]:
            total = total + r[...].astype(F32)
        at += n
        chunks.append(total)
    term = jnp.concatenate([recv_ref[q, :, :share].astype(F32) for q in range(tp)], axis=1)
    grad = jnp.concatenate(chunks, axis=1) + term
    tok = tok_ref[...].astype(F32)
    inv = lax.rsqrt(jnp.mean(tok * tok, axis=1, keepdims=True) + EPS)
    normed = tok * inv
    mean = jnp.mean(grad * normed, axis=1, keepdims=True)
    out_ref[...] = (inv * (grad - normed * mean)).astype(BF)


def call(kernel, out, n_in, smem=(), scratch=(), flops=0, nbytes=0, vmem=48):
    return pl.pallas_call(
        kernel,
        out_shape=out,
        in_specs=[SMEM if i in smem else VMEM for i in range(n_in)],
        out_specs=jax.tree.map(lambda _: VMEM, out),
        scratch_shapes=list(scratch),
        cost_estimate=pl.CostEstimate(flops=int(flops), bytes_accessed=int(nbytes), transcendentals=0),
        compiler_params=pltpu.CompilerParams(vmem_limit_bytes=vmem << 20),
    )


def shape(dims, dtype=BF):
    return jax.ShapeDtypeStruct(dims, dtype)


def body(tokens, cotangent, weight, down_maps, up_maps, lengths, slots):
    tp = lax.axis_size("tp")
    me = lax.axis_index("tp").reshape(1)
    own, width = tokens.shape
    rows = own * tp
    count, rank, share = down_maps.shape
    columns = cotangent.shape[0]
    stages = stages_of(tp)
    order = block_order(stages)
    lens = lengths.reshape(1, count)
    slot = slots.reshape(1, count)
    down_flat = down_maps.reshape(count * rank, share)

    send, cotp = call(
        functools.partial(prep_kernel, order, rank),
        (shape((tp, own, share + rows)), shape((rows, columns))),
        6,
        smem=(0,),
        scratch=[pltpu.VMEM((rows, columns), BF)],
        flops=2 * rows * columns * count * rank,
        nbytes=3 << 20,
    )(me, lens, slot, tokens, cotangent, up_maps)
    recv = lax.all_to_all(send, "tp", split_axis=0, concat_axis=0, tiled=True)

    def product(first, size):
        block = 1024
        m = len(stages[0])
        each = rows // m
        return pl.pallas_call(
            product_kernel,
            grid=(size // block,),
            out_shape=[shape((each, size))] * m,
            in_specs=[
                pl.BlockSpec((rows, columns), lambda i: (0, 0)),
                pl.BlockSpec((columns, block), lambda i: (0, first // block + i)),
            ],
            out_specs=[pl.BlockSpec((each, block), lambda i: (0, i))] * m,
            cost_estimate=pl.CostEstimate(
                flops=2 * rows * columns * size,
                bytes_accessed=2 * columns * size + 2 * rows * size,
                transcendentals=0,
            ),
            compiler_params=pltpu.CompilerParams(vmem_limit_bytes=32 << 20),
        )(cotp, weight)

    def pairs(m):
        return [(i, i ^ m) for i in range(tp)]

    def scatter(parts):
        for s, masks in enumerate(stages):
            got = [lax.ppermute(part, "tp", pairs(m)) for m, part in zip(masks[1:], parts[1:])]
            if s == len(stages) - 1:
                return [parts[0]] + got
            m = len(stages[s + 1])
            each = parts[0].shape[0] // m
            new = []
            for i in range(m):
                total = parts[0][i * each : (i + 1) * each].astype(F32)
                for g in got:
                    total = total + g[i * each : (i + 1) * each].astype(F32)
                new.append(total.astype(BF))
            parts = new

    sizes = [width // 2, width // 2]
    chunks = []
    first = 0
    for size in sizes:
        chunks.append(scatter(product(first, size)))
        first += size

    send2, left = call(
        functools.partial(middle_kernel, rank),
        (shape((tp, own, share + rows)), shape((count * rank, rows))),
        4,
        flops=4 * rows * share * count * rank,
        nbytes=3 << 20,
    )(lens, slot, recv, down_flat)
    recv2 = lax.all_to_all(send2, "tp", split_axis=0, concat_axis=0, tiled=True)
    down_grad = call(
        down_kernel, shape((count * rank, share), F32), 2, flops=2 * rows * share * count * rank, nbytes=3 << 20
    )(left, recv)
    up_grad = call(
        functools.partial(up_kernel, rank),
        shape((columns, count * rank), F32),
        4,
        flops=2 * rows * columns * count * rank,
        nbytes=3 << 20,
    )(lens, slot, recv2, cotangent)
    flat = [piece for chunk in chunks for piece in chunk]
    grad_tokens = call(
        functools.partial(final_kernel, [len(c) for c in chunks]), shape((own, width)), 2 + len(flat), nbytes=2 << 20
    )(recv2, tokens, *flat)
    return grad_tokens, down_grad.reshape(count, rank, share), up_grad


def solution(mesh):
    in_specs = (
        P(("rep", "tp"), None),
        P("tp", "rep"),
        P("tp", None),
        P(None, None, "tp"),
        P("tp", None),
        P("rep"),
        P(),
    )
    out_specs = (P(("rep", "tp"), None), P("rep", None, "tp"), P("tp", "rep"))
    return jax.shard_map(body, mesh=mesh, in_specs=in_specs, out_specs=out_specs, check_vma=False)
```

time: 825 us -> 87.8 us (0.11)
  local copies, waits for them, and re-layouts: 378 us -> 14.5 us
  loops' own time: 250 us -> 0 us
  blocking collectives: 61.9 us -> 0 us
  other arithmetic: 55.8 us -> 3.84 us
  matrix products: 49.9 us -> 0 us
  waiting for transfers between devices: 0.02 us -> 30 us
  starting transfers between devices: 7.43 us -> 22.8 us
  Pallas kernels: 0 us -> 15.3 us
  between operations: 14.2 us -> 0.74 us
    another operation x1 -> x0, loops' own time: 250 us -> none  [body(): lax.map(one_segment, jnp.arange(adapter_list, dtype=jnp.int32))]
    dynamic_update_slice x256 -> x0, local copies, waits for them, and re-layouts: 244 us -> none  [body(): lax.map(one_segment, jnp.arange(adapter_list, dtype=jnp.int32))]
    dynamic_slice x192 -> x0, local copies, waits for them, and re-layouts: 112 us -> none  [the longest x64 37.7 us: one_segment(): keep = offsets < adapter_token_lengths[which]]
    psum x1 -> x0, blocking collectives: 61.9 us -> none  [body(): low_sum, back_sum = lax.psum((low_part, back_part), 'tp')]
    dot_general x133 -> x0, matrix products: 49.9 us -> none  [the longest x64 15.8 us: one_segment(): up_grad = jnp.dot(cot_seg, low_seg, preferred_element_type=jnp.float32)]
    lt x64 -> x0, other arithmetic: 41.6 us -> none  [one_segment(): keep = offsets < adapter_token_lengths[which]]
    ppermute x0 -> x10, waiting for transfers between devices: none -> 25.7 us  [scatter(): lax.ppermute(part, 'tp', pairs(m))]
    pallas_call x0 -> x7, Pallas kernels: none -> 15.3 us  [the longest x2 6.87 us: product(): pl.pallas_call(product_kernel, grid=(size // block,), out_shape=[shape((e...]
  transfers between devices with their start and end apart: 2 -> 12, of which waited for: 0 -> 4; matrix products, arithmetic and copies ran while one was open for 57% -> 4% of each run, Pallas kernels for 0% -> 10%
where the time goes in v1:
time: 87.8 us; the launch traced here: 87.2 us
  waiting for transfers between devices  30 us (34%)
  starting transfers between devices  22.8 us (26%)
  Pallas kernels  15.3 us (17%)
  local copies, waits for them, and re-layouts  14.5 us (17%)
  other arithmetic  3.84 us (4%)
    ppermute x10, waiting for transfers between devices, scatter(): lax.ppermute(part, 'tp', pairs(m))  25.7 us
    unnamed x26, local copies, waits for them, and re-layouts  14.5 us
    ppermute x10, starting transfers between devices, scatter(): lax.ppermute(part, 'tp', pairs(m))  12.2 us
    all_to_all x1, starting transfers between devices, body(): recv = lax.all_to_all(send, 'tp', split_axis=0, concat_axis=0, tiled=True)  7.04 us
    pallas_call x2, Pallas kernels, product(): pl.pallas_call(product_kernel, grid=(size // block,), out_shape=[shape((e...  6.87 us
    all_to_all x1, waiting for transfers between devices, body(): recv = lax.all_to_all(send, 'tp', split_axis=0, concat_axis=0, tiled=True)  4.37 us
    convert_element_type x4, other arithmetic, scatter(): new.append(total.astype(BF))  3.84 us
    all_to_all x1, starting transfers between devices, body(): recv2 = lax.all_to_all(send2, 'tp', split_axis=0, concat_axis=0, tiled=True)  3.55 us
  transfers between devices with their start and end apart: 12, of which 4 were waited for; matrix products, arithmetic and copies ran while one was open for 4% of the time, Pallas kernels for 10%

profile of v1, /device:TPU:0, one launch (start us, length us, event | category | flops | bytes accessed | tf_op | source)
XLA Modules:
  0.0 87.2 jit_solution(5387746219493706935)
XLA Ops:
  0.6 0.0 copy-start.2
  0.6 1.3 %copy-done.2 = bf16[640,1024]{1,0:T(8,128)(2,1)S(1)} copy-done((bf16[640,1024]{1,0:T(8,128)(2,1)S(1)}, bf16[640,1024]{1,0:T(8,128)(2,1)}, u32[]{:S(2)}) %copy-start.2) | copy-done | bytes 1310744
  2.0 0.0 copy-start.3
  2.0 1.0 %copy-done.3 = bf16[640,256]{1,0:T(8,128)(2,1)S(1)} copy-done((bf16[640,256]{1,0:T(8,128)(2,1)S(1)}, bf16[640,256]{1,0:T(8,128)(2,1)}, u32[]{:S(2)}) %copy-start.3) | copy-done | bytes 327704
  2.9 0.0 copy-start.5
  2.9 0.9 %copy-done.5 = bf16[16,8192]{1,0:T(8,128)(2,1)S(1)} copy-done((bf16[16,8192]{1,0:T(8,128)(2,1)S(1)}, bf16[16,8192]{1,0:T(8,128)(2,1)}, u32[]{:S(2)}) %copy-start.5) | copy-done | bytes 262168
  3.9 0.0 copy-start.8
  3.9 0.7 copy-done.8
  4.5 0.0 copy-start.10
  4.5 0.7 copy-done.10
  5.2 1.8 %shard_map.94 = (bf16[16,16,768]{2,1,0:T(8,128)(2,1)}, bf16[256,640]{1,0:T(8,128)(2,1)S(1)}) custom-call(s32[1]{0:T(128)} %bitcast.2.me_ref, s32[1,64]{1,0:T(1,128)S(1)} %bitcast.5, s32[1,64]{1,0:T(1,128)S(1)} %bitcast.8, bf16[16,8192]{1,0:T(8,128)(2,1)S(1)} %copy-done.5, bf16[640,256]{1,0:T(8,128)(2,1)S(1)} %copy-done.3, bf16[640,1024]{1,0:T(8,128)(2,1)S(1)} %copy-done.2), custom_call_target="tpu_custom_call" | custom-call | flops 335544320 | bytes 3145728 | tf_op jit(solution)/shard_map/pallas_call | solution.py:193
  7.0 0.0 copy-start
  7.0 4.0 %copy-done = bf16[640,8192]{1,0:T(8,128)(2,1)S(1)} copy-done((bf16[640,8192]{1,0:T(8,128)(2,1)S(1)}, bf16[640,8192]{1,0:T(8,128)(2,1)}, u32[]{:S(2)}) %copy-start) | copy-done | bytes 10485784
  11.0 3.4 %shard_map.97 = (bf16[128,4096]{1,0:T(8,128)(2,1)S(1)}, bf16[128,4096]{1,0:T(8,128)(2,1)}) custom-call(bf16[256,640]{1,0:T(8,128)(2,1)S(1)} %get-tuple-element.13.cotp_ref, bf16[640,8192]{1,0:T(8,128)(2,1)S(1)} %copy-done), custom_call_target="tpu_custom_call" | custom-call | flops 1342177280 | bytes 7340032 | tf_op jit(solution)/shard_map/pallas_call | solution.py:208
  14.4 0.5 collective-permute-start.5
  14.9 7.0 %all-to-all-start = ((bf16[16,16,768]{2,1,0:T(8,128)(2,1)}), bf16[16,16,768]{2,1,0:T(8,128)(2,1)S(1)}, u32[]{:S(2)}, u32[]{:S(2)}) async-start(bf16[16,16,768]{2,1,0:T(8,128)(2,1)} %get-tuple-element.11), calls=%async_computation | async-start | bytes 786432 | tf_op jit(solution)/shard_map/all_to_all | solution.py:202
  21.9 0.0 copy-start.1
  21.9 4.0 %copy-done.1 = bf16[640,8192]{1,0:T(8,128)(2,1)S(1)} copy-done((bf16[640,8192]{1,0:T(8,128)(2,1)S(1)}, bf16[640,8192]{1,0:T(8,128)(2,1)}, u32[]{:S(2)}) %copy-start.1) | copy-done | bytes 10485784
  25.9 0.0 copy-start.9
  25.9 0.0 copy-start.11
  25.9 3.4 %shard_map.96 = (bf16[128,4096]{1,0:T(8,128)(2,1)S(1)}, bf16[128,4096]{1,0:T(8,128)(2,1)}) custom-call(bf16[256,640]{1,0:T(8,128)(2,1)S(1)} %get-tuple-element.13.cotp_ref, bf16[640,8192]{1,0:T(8,128)(2,1)S(1)} %copy-done.1), custom_call_target="tpu_custom_call" | custom-call | flops 1342177280 | bytes 7340032 | tf_op jit(solution)/shard_map/pallas_call | solution.py:208
  29.3 0.4 collective-permute-start
  29.7 4.4 %all-to-all-done.recv_ref = bf16[16,16,768]{2,1,0:T(8,128)(2,1)S(1)} async-done(((bf16[16,16,768]{2,1,0:T(8,128)(2,1)}), bf16[16,16,768]{2,1,0:T(8,128)(2,1)S(1)}, u32[]{:S(2)}, u32[]{:S(2)}) %all-to-all-start) | async-done | bytes 393248 | tf_op jit(solution)/shard_map/all_to_all | solution.py:202
  34.1 0.0 copy-done.9
  34.1 0.0 copy-done.11
  34.1 0.0 copy-start.12
  34.1 1.2 %copy-done.12 = bf16[64,16,512]{2,1,0:T(8,128)(2,1)S(1)} copy-done((bf16[64,16,512]{2,1,0:T(8,128)(2,1)S(1)}, bf16[64,16,512]{2,1,0:T(8,128)(2,1)}, u32[]{:S(2)}) %copy-start.12) | copy-done | bytes 1048600
  35.3 1.2 %shard_map.95 = (bf16[16,16,768]{2,1,0:T(8,128)(2,1)S(1)}, bf16[1024,256]{1,0:T(8,128)(2,1)S(1)}) custom-call(s32[1,64]{1,0:T(1,128)S(1)} %bitcast.6, s32[1,64]{1,0:T(1,128)S(1)} %bitcast.9, bf16[16,16,768]{2,1,0:T(8,128)(2,1)S(1)} %all-to-all-done.recv_ref, bf16[1024,512]{1,0:T(8,128)(2,1)S(1)} %bitcast.11), custom_call_target="tpu_custom_call" | custom-call | flops 536870912 | bytes 3145728 | tf_op jit(solution)/shard_map/pallas_call | solution.py:250
  36.6 0.0 copy-start.7
  36.6 0.7 copy-done.7
  37.3 3.6 %all-to-all-start.1 = ((bf16[16,16,768]{2,1,0:T(8,128)(2,1)}), bf16[16,16,768]{2,1,0:T(8,128)(2,1)S(1)}, u32[]{:S(2)}, u32[]{:S(2)}) async-start(bf16[16,16,768]{2,1,0:T(8,128)(2,1)} %copy-done.7), calls=%async_computation.1 | async-start | bytes 786432 | tf_op jit(solution)/shard_map/all_to_all | solution.py:257
  40.9 0.0 collective-permute-done.5
  40.9 1.4 %add_convert_fusion.1 = (bf16[64,4096]{1,0:T(8,128)(2,1)S(1)}, bf16[64,4096]{1,0:T(8,128)(2,1)S(1)}) fusion(bf16[128,4096]{1,0:T(8,128)(2,1)} %collective-permute-done.5, bf16[128,4096]{1,0:T(8,128)(2,1)S(1)} %get-tuple-element.16), kind=kLoop, calls=%fused_computation.1 | loop fusion | flops 2097152 | bytes 3145728 | tf_op jit(solution)/shard_map/convert_element_type | solution.py:240
  42.3 2.0 %collective-permute-start.6 = (bf16[64,4096]{1,0:T(8,128)(2,1)S(1)}, bf16[64,4096]{1,0:T(8,128)(2,1)S(1)}, u32[]{:S(2)}, u32[]{:S(2)}) collective-permute-start(bf16[64,4096]{1,0:T(8,128)(2,1)S(1)} %get-tuple-element.20), channel_id=1, source_target_pairs={{0,2},{1,3},{2,0},{3,1},{4,6},{5,7},{6,4},{7,5},{8,10},{9,11},{10,... | collective-permute-start | bytes 1572872 | tf_op jit(solution)/shard_map/ppermute | solution.py:230
  44.3 0.0 collective-permute-done
  44.3 1.4 %add_convert_fusion.3 = (bf16[64,4096]{1,0:T(8,128)(2,1)S(1)}, bf16[64,4096]{1,0:T(8,128)(2,1)S(1)}) fusion(bf16[128,4096]{1,0:T(8,128)(2,1)} %collective-permute-done, bf16[128,4096]{1,0:T(8,128)(2,1)S(1)} %get-tuple-element.14), kind=kLoop, calls=%fused_computation.3 | loop fusion | flops 2097152 | bytes 3145728 | tf_op jit(solution)/shard_map/convert_element_type | solution.py:240
  45.7 0.2 collective-permute-start.1
  46.0 13.6 %collective-permute-done.6 = bf16[64,4096]{1,0:T(8,128)(2,1)S(1)} collective-permute-done((bf16[64,4096]{1,0:T(8,128)(2,1)S(1)}, bf16[64,4096]{1,0:T(8,128)(2,1)S(1)}, u32[]{:S(2)}, u32[]{:S(2)}) %collective-permute-start.6) | collective-permute-done | bytes 524320 | tf_op jit(solution)/shard_map/ppermute | solution.py:230
  59.6 0.1 add_convert_fusion.4
  59.7 0.0 copy-start.4
  59.7 2.3 %collective-permute-start.7 = (bf16[16,4096]{1,0:T(8,128)(2,1)S(1)}, bf16[16,4096]{1,0:T(8,128)(2,1)S(1)}, u32[]{:S(2)}, u32[]{:S(2)}) collective-permute-start(bf16[16,4096]{1,0:T(8,128)(2,1)S(1)} %get-tuple-element.25), channel_id=1, source_target_pairs={{0,4},{1,5},{2,6},{3,7},{4,0},{5,1},{6,2},{7,3},{8,12},{9,13},{10,... | collective-permute-start | bytes 393224 | tf_op jit(solution)/shard_map/ppermute | solution.py:230
  62.0 1.7 %collective-permute-start.8 = (bf16[16,4096]{1,0:T(8,128)(2,1)S(1)}, bf16[16,4096]{1,0:T(8,128)(2,1)S(1)}, u32[]{:S(2)}, u32[]{:S(2)}) collective-permute-start(bf16[16,4096]{1,0:T(8,128)(2,1)S(1)} %get-tuple-element.24), channel_id=1, source_target_pairs={{0,8},{1,9},{2,10},{3,11},{4,12},{5,13},{6,14},{7,15},{8,0},{9,1},... | collective-permute-start | bytes 393224 | tf_op jit(solution)/shard_map/ppermute | solution.py:230
  63.7 0.8 collective-permute-start.9
  64.5 6.2 %collective-permute-done.1 = bf16[64,4096]{1,0:T(8,128)(2,1)S(1)} collective-permute-done((bf16[64,4096]{1,0:T(8,128)(2,1)S(1)}, bf16[64,4096]{1,0:T(8,128)(2,1)S(1)}, u32[]{:S(2)}, u32[]{:S(2)}) %collective-permute-start.1) | collective-permute-done | bytes 524320 | tf_op jit(solution)/shard_map/ppermute | solution.py:230
  70.7 0.8 add_convert_fusion.8
  71.6 1.9 %collective-permute-start.2 = (bf16[16,4096]{1,0:T(8,128)(2,1)}, bf16[16,4096]{1,0:T(8,128)(2,1)S(1)}, u32[]{:S(2)}, u32[]{:S(2)}) collective-permute-start(bf16[16,4096]{1,0:T(8,128)(2,1)} %get-tuple-element.29), channel_id=1, source_target_pairs={{0,4},{1,5},{2,6},{3,7},{4,0},{5,1},{6,2},{7,3},{8,12},{9,13},{10,... | collective-permute-start | bytes 393224 | tf_op jit(solution)/shard_map/ppermute | solution.py:230
  73.4 1.9 %collective-permute-start.3 = (bf16[16,4096]{1,0:T(8,128)(2,1)}, bf16[16,4096]{1,0:T(8,128)(2,1)S(1)}, u32[]{:S(2)}, u32[]{:S(2)}) collective-permute-start(bf16[16,4096]{1,0:T(8,128)(2,1)} %get-tuple-element.28), channel_id=1, source_target_pairs={{0,8},{1,9},{2,10},{3,11},{4,12},{5,13},{6,14},{7,15},{8,0},{9,1},... | collective-permute-start | bytes 393224 | tf_op jit(solution)/shard_map/ppermute | solution.py:230
  75.3 0.0 collective-permute-done.7.refs_5_
  75.3 0.6 collective-permute-start.4
  76.0 0.0 copy-start.6
  76.0 1.8 %shard_map.99 = f32[1024,512]{1,0:T(8,128)} custom-call(bf16[1024,256]{1,0:T(8,128)(2,1)S(1)} %get-tuple-element.18.left_ref, bf16[16,16,768]{2,1,0:T(8,128)(2,1)S(1)} %all-to-all-done.recv_ref), custom_call_target="tpu_custom_call" | custom-call | flops 268435456 | bytes 3145728 | tf_op jit(solution)/shard_map/pallas_call | solution.py:258
  77.7 0.0 all-to-all-done.1.recv_ref
  77.7 0.0 copy-done.4
  77.7 2.5 %shard_map.100 = f32[640,1024]{1,0:T(8,128)} custom-call(s32[1,64]{1,0:T(1,128)S(1)} %bitcast.7, s32[1,64]{1,0:T(1,128)S(1)} %bitcast.10, bf16[16,16,768]{2,1,0:T(8,128)(2,1)S(1)} %all-to-all-done.1.recv_ref, bf16[640,256]{1,0:T(8,128)(2,1)S(1)} %copy-done.4), custom_call_target="tpu_custom_call" | custom-call | flops 335544320 | bytes 3145728 | tf_op jit(solution)/shard_map/pallas_call | solution.py:261
  80.2 0.0 collective-permute-done.8.refs_6_
  80.2 0.0 collective-permute-done.9.refs_7_
  80.2 0.0 collective-permute-done.2.refs_1_
  80.3 5.8 %collective-permute-done.3.refs_2_ = bf16[16,4096]{1,0:T(8,128)(2,1)S(1)} collective-permute-done((bf16[16,4096]{1,0:T(8,128)(2,1)}, bf16[16,4096]{1,0:T(8,128)(2,1)S(1)}, u32[]{:S(2)}, u32[]{:S(2)}) %collective-permute-start.3) | collective-permute-done | bytes 131104 | tf_op jit(solution)/shard_map/ppermute | solution.py:230
  86.0 0.0 collective-permute-done.4.refs_3_
  86.0 0.0 copy-done.6
  86.0 1.2 %shard_map.98 = bf16[16,8192]{1,0:T(8,128)(2,1)} custom-call(bf16[16,16,768]{2,1,0:T(8,128)(2,1)S(1)} %all-to-all-done.1.recv_ref, bf16[16,8192]{1,0:T(8,128)(2,1)S(1)} %copy-done.6, bf16[16,4096]{1,0:T(8,128)(2,1)S(1)} %get-tuple-element.30.refs_0_, bf16[16,4096]{1,0:T(8,128)(2,1)S(1)} %collective-permute-done.2.refs_1_, ...), custom_call_target="tpu_custom_call" | custom-call | bytes 2097152 | tf_op jit(solution)/shard_map/pallas_call | solution.py:269
Async XLA Ops:
  0.6 1.3 %copy-start.2 = (bf16[640,1024]{1,0:T(8,128)(2,1)S(1)}, bf16[640,1024]{1,0:T(8,128)(2,1)}, u32[]{:S(2)}) copy-start(bf16[640,1024]{1,0:T(8,128)(2,1)} %up_ref.1) | copy-start | bytes 3932164
  2.0 1.0 %copy-start.3 = (bf16[640,256]{1,0:T(8,128)(2,1)S(1)}, bf16[640,256]{1,0:T(8,128)(2,1)}, u32[]{:S(2)}) copy-start(bf16[640,256]{1,0:T(8,128)(2,1)} %cot_ref.3) | copy-start | bytes 983044
  2.9 0.9 %copy-start.5 = (bf16[16,8192]{1,0:T(8,128)(2,1)S(1)}, bf16[16,8192]{1,0:T(8,128)(2,1)}, u32[]{:S(2)}) copy-start(bf16[16,8192]{1,0:T(8,128)(2,1)} %tok_ref.3) | copy-start | bytes 786436
  3.9 0.7 copy-start.8
  4.5 0.7 copy-start.10
  7.0 4.0 %copy-start = (bf16[640,8192]{1,0:T(8,128)(2,1)S(1)}, bf16[640,8192]{1,0:T(8,128)(2,1)}, u32[]{:S(2)}) copy-start(bf16[640,8192]{1,0:T(8,128)(2,1)} %weight_ref.3) | copy-start | bytes 31457284
  14.4 26.5 %collective-permute-start.5 = (bf16[128,4096]{1,0:T(8,128)(2,1)}, bf16[128,4096]{1,0:T(8,128)(2,1)}, u32[]{:S(2)}, u32[]{:S(2)}) collective-permute-start(bf16[128,4096]{1,0:T(8,128)(2,1)} %get-tuple-element.17), channel_id=1, source_target_pairs={{0,1},{1,0},{2,3},{3,2},{4,5},{5,4},{6,7},{7,6},{8,9},{9,8},{10,11... | collective-permute-start | bytes 3145736 | tf_op jit(solution)/shard_map/ppermute | solution.py:230
  14.9 19.2 %all-to-all-start = ((bf16[16,16,768]{2,1,0:T(8,128)(2,1)}), bf16[16,16,768]{2,1,0:T(8,128)(2,1)S(1)}, u32[]{:S(2)}, u32[]{:S(2)}) async-start(bf16[16,16,768]{2,1,0:T(8,128)(2,1)} %get-tuple-element.11), calls=%async_computation | async-start | bytes 786432 | tf_op jit(solution)/shard_map/all_to_all | solution.py:202
  21.9 4.0 %copy-start.1 = (bf16[640,8192]{1,0:T(8,128)(2,1)S(1)}, bf16[640,8192]{1,0:T(8,128)(2,1)}, u32[]{:S(2)}) copy-start(bf16[640,8192]{1,0:T(8,128)(2,1)} %weight_ref.3) | copy-start | bytes 31457284
  25.9 8.2 %copy-start.9 = (s32[64]{0:T(128)S(1)}, s32[64]{0:T(128)}, u32[]{:S(2)}) copy-start(s32[64]{0:T(128)} %param.12) | copy-start | bytes 772
  25.9 8.2 %copy-start.11 = (s32[64]{0:T(128)S(1)}, s32[64]{0:T(128)}, u32[]{:S(2)}) copy-start(s32[64]{0:T(128)} %param.13) | copy-start | bytes 772
  29.3 15.0 %collective-permute-start = (bf16[128,4096]{1,0:T(8,128)(2,1)}, bf16[128,4096]{1,0:T(8,128)(2,1)}, u32[]{:S(2)}, u32[]{:S(2)}) collective-permute-start(bf16[128,4096]{1,0:T(8,128)(2,1)} %get-tuple-element.15), channel_id=1, source_target_pairs={{0,1},{1,0},{2,3},{3,2},{4,5},{5,4},{6,7},{7,6},{8,9},{9,8},{10,11... | collective-permute-start | bytes 3145736 | tf_op jit(solution)/shard_map/ppermute | solution.py:230
  34.1 1.2 %copy-start.12 = (bf16[64,16,512]{2,1,0:T(8,128)(2,1)S(1)}, bf16[64,16,512]{2,1,0:T(8,128)(2,1)}, u32[]{:S(2)}) copy-start(bf16[64,16,512]{2,1,0:T(8,128)(2,1)} %param.10) | copy-start | bytes 3145732
  36.6 0.8 copy-start.7
  37.3 40.4 %all-to-all-start.1 = ((bf16[16,16,768]{2,1,0:T(8,128)(2,1)}), bf16[16,16,768]{2,1,0:T(8,128)(2,1)S(1)}, u32[]{:S(2)}, u32[]{:S(2)}) async-start(bf16[16,16,768]{2,1,0:T(8,128)(2,1)} %copy-done.7), calls=%async_computation.1 | async-start | bytes 786432 | tf_op jit(solution)/shard_map/all_to_all | solution.py:257
  42.3 17.2 %collective-permute-start.6 = (bf16[64,4096]{1,0:T(8,128)(2,1)S(1)}, bf16[64,4096]{1,0:T(8,128)(2,1)S(1)}, u32[]{:S(2)}, u32[]{:S(2)}) collective-permute-start(bf16[64,4096]{1,0:T(8,128)(2,1)S(1)} %get-tuple-element.20), channel_id=1, source_target_pairs={{0,2},{1,3},{2,0},{3,1},{4,6},{5,7},{6,4},{7,5},{8,10},{9,11},{10,... | collective-permute-start | bytes 1572872 | tf_op jit(solution)/shard_map/ppermute | solution.py:230
  45.7 25.0 %collective-permute-start.1 = (bf16[64,4096]{1,0:T(8,128)(2,1)S(1)}, bf16[64,4096]{1,0:T(8,128)(2,1)S(1)}, u32[]{:S(2)}, u32[]{:S(2)}) collective-permute-start(bf16[64,4096]{1,0:T(8,128)(2,1)S(1)} %get-tuple-element.22), channel_id=1, source_target_pairs={{0,2},{1,3},{2,0},{3,1},{4,6},{5,7},{6,4},{7,5},{8,10},{9,11},{10,... | collective-permute-start | bytes 1572872 | tf_op jit(solution)/shard_map/ppermute | solution.py:230
  59.7 18.0 %copy-start.4 = (bf16[640,256]{1,0:T(8,128)(2,1)S(1)}, bf16[640,256]{1,0:T(8,128)(2,1)}, u32[]{:S(2)}) copy-start(bf16[640,256]{1,0:T(8,128)(2,1)} %cot_ref.3) | copy-start | bytes 983044
  59.7 15.6 %collective-permute-start.7 = (bf16[16,4096]{1,0:T(8,128)(2,1)S(1)}, bf16[16,4096]{1,0:T(8,128)(2,1)S(1)}, u32[]{:S(2)}, u32[]{:S(2)}) collective-permute-start(bf16[16,4096]{1,0:T(8,128)(2,1)S(1)} %get-tuple-element.25), channel_id=1, source_target_pairs={{0,4},{1,5},{2,6},{3,7},{4,0},{5,1},{6,2},{7,3},{8,12},{9,13},{10,... | collective-permute-start | bytes 393224 | tf_op jit(solution)/shard_map/ppermute | solution.py:230
  62.0 18.2 %collective-permute-start.8 = (bf16[16,4096]{1,0:T(8,128)(2,1)S(1)}, bf16[16,4096]{1,0:T(8,128)(2,1)S(1)}, u32[]{:S(2)}, u32[]{:S(2)}) collective-permute-start(bf16[16,4096]{1,0:T(8,128)(2,1)S(1)} %get-tuple-element.24), channel_id=1, source_target_pairs={{0,8},{1,9},{2,10},{3,11},{4,12},{5,13},{6,14},{7,15},{8,0},{9,1},... | collective-permute-start | bytes 393224 | tf_op jit(solution)/shard_map/ppermute | solution.py:230
  63.7 16.5 %collective-permute-start.9 = (bf16[16,4096]{1,0:T(8,128)(2,1)S(1)}, bf16[16,4096]{1,0:T(8,128)(2,1)S(1)}, u32[]{:S(2)}, u32[]{:S(2)}) collective-permute-start(bf16[16,4096]{1,0:T(8,128)(2,1)S(1)} %get-tuple-element.23), channel_id=1, source_target_pairs={{0,12},{1,13},{2,14},{3,15},{4,8},{5,9},{6,10},{7,11},{8,4},{9,5},... | collective-permute-start | bytes 393224 | tf_op jit(solution)/shard_map/ppermute | solution.py:230
  71.6 8.7 %collective-permute-start.2 = (bf16[16,4096]{1,0:T(8,128)(2,1)}, bf16[16,4096]{1,0:T(8,128)(2,1)S(1)}, u32[]{:S(2)}, u32[]{:S(2)}) collective-permute-start(bf16[16,4096]{1,0:T(8,128)(2,1)} %get-tuple-element.29), channel_id=1, source_target_pairs={{0,4},{1,5},{2,6},{3,7},{4,0},{5,1},{6,2},{7,3},{8,12},{9,13},{10,... | collective-permute-start | bytes 393224 | tf_op jit(solution)/shard_map/ppermute | solution.py:230
  73.4 12.6 %collective-permute-start.3 = (bf16[16,4096]{1,0:T(8,128)(2,1)}, bf16[16,4096]{1,0:T(8,128)(2,1)S(1)}, u32[]{:S(2)}, u32[]{:S(2)}) collective-permute-start(bf16[16,4096]{1,0:T(8,128)(2,1)} %get-tuple-element.28), channel_id=1, source_target_pairs={{0,8},{1,9},{2,10},{3,11},{4,12},{5,13},{6,14},{7,15},{8,0},{9,1},... | collective-permute-start | bytes 393224 | tf_op jit(solution)/shard_map/ppermute | solution.py:230
  75.3 10.7 %collective-permute-start.4 = (bf16[16,4096]{1,0:T(8,128)(2,1)S(1)}, bf16[16,4096]{1,0:T(8,128)(2,1)S(1)}, u32[]{:S(2)}, u32[]{:S(2)}) collective-permute-start(bf16[16,4096]{1,0:T(8,128)(2,1)S(1)} %get-tuple-element.27), channel_id=1, source_target_pairs={{0,12},{1,13},{2,14},{3,15},{4,8},{5,9},{6,10},{7,11},{8,4},{9,5},... | collective-permute-start | bytes 393224 | tf_op jit(solution)/shard_map/ppermute | solution.py:230
  76.0 10.1 %copy-start.6 = (bf16[16,8192]{1,0:T(8,128)(2,1)S(1)}, bf16[16,8192]{1,0:T(8,128)(2,1)}, u32[]{:S(2)}) copy-start(bf16[16,8192]{1,0:T(8,128)(2,1)} %tok_ref.3) | copy-start | bytes 786436

commit v2 on v1

--- a/solution.py
+++ b/solution.py
@@ -63,21 +63,78 @@
     return jnp.dot(wide, chosen, preferred_element_type=F32)
 
 
-def prep_kernel(order, rank, me_ref, lens_ref, slots_ref, tok_ref, cot_ref, up_ref, send_ref, cotp_ref, cott):
+def cast_parts(out, parts):
+    each = parts[0].shape[0]
+    for i, part in enumerate(parts):
+        part[...] = out[i * each : (i + 1) * each].astype(BF)
+
+
+def fetch_weight(weight_hbm, wbuf, sems, first, block):
+    copies = []
+    for i in range(wbuf.shape[1] // block):
+        copies.append(
+            pltpu.make_async_copy(
+                weight_hbm.at[:, pl.ds(first + i * block, block)], wbuf.at[:, pl.ds(i * block, block)], sems.at[i]
+            )
+        )
+    return copies
+
+
+def multiply(cotp, wbuf, copies, block, parts):
+    each = parts[0].shape[0]
+    for i, copy in enumerate(copies):
+        copy.wait()
+        columns = pl.ds(i * block, block)
+        out = jnp.dot(cotp, wbuf[:, columns], preferred_element_type=F32)
+        for k, part in enumerate(parts):
+            part[:, columns] = out[k * each : (k + 1) * each].astype(BF)
+
+
+def first_kernel(order, own, block, me_ref, cot_hbm, weight_hbm, cotp_ref, *refs):
+    *parts, cot, cott, wbuf, sem, sems = refs
+    cot_copy = pltpu.make_async_copy(cot_hbm, cot, sem)
+    cot_copy.start()
+    copies = fetch_weight(weight_hbm, wbuf, sems, 0, block)
+    for copy in copies:
+        copy.start()
+    cot_copy.wait()
+    cott[...] = cot[...].astype(F32).T.astype(BF)
+    me = me_ref[0]
+    for i, mask_bits in enumerate(order):
+        source = pl.multiple_of((me ^ mask_bits) * own, own)
+        cotp_ref[pl.ds(i * own, own), :] = cott[pl.ds(source, own), :]
+    multiply(cotp_ref[...], wbuf, copies, block, parts)
+
+
+def second_kernel(order, rank, first, block, me_ref, lens_ref, slots_ref, cotp_ref, tok_hbm, up_hbm, weight_hbm, send_ref, *refs):
+    *parts, tokv, up, wbuf, back_rows, sem, sems = refs
     tp, own, _ = send_ref.shape
-    width = tok_ref.shape[1]
+    width = tokv.shape[1]
     share = width // tp
-    rows, _ = cott.shape
-    cott[...] = cot_ref[...].astype(F32).T.astype(BF)
-    tok = tok_ref[...].astype(F32)
-    inv = lax.rsqrt(jnp.mean(tok * tok, axis=1, keepdims=True) + EPS)
-    normed = (tok * inv).astype(BF)
+    rows = cotp_ref.shape[0]
+    tok_copy = pltpu.make_async_copy(tok_hbm, tokv, sem.at[0])
+    tok_copy.start()
+    up_copy = pltpu.make_async_copy(up_hbm, up, sem.at[1])
+    up_copy.start()
+    copies = fetch_weight(weight_hbm, wbuf, sems, first, block)
+    for copy in copies:
+        copy.start()
     member, match = membership(lens_ref, slots_ref, rows)
     chosen = lax.dot_general(member, match, NT, preferred_element_type=F32).astype(BF)
     slots = match.shape[0]
     wide = (iota((slots, slots * rank), 1) // rank == iota((slots, slots * rank), 0)).astype(F32).astype(BF)
     mask = jnp.dot(chosen, wide, preferred_element_type=F32)
-    every = jnp.dot(cott[...], up_ref[...], preferred_element_type=F32) * mask
+    me = me_ref[0]
+    tok_copy.wait()
+    tok = tokv[...].astype(F32)
+    inv = lax.rsqrt(jnp.mean(tok * tok, axis=1, keepdims=True) + EPS)
+    normed = (tok * inv).astype(BF)
+    up_copy.wait()
+    every = jnp.dot(cotp_ref[...], up[...], preferred_element_type=F32)
+    for i, mask_bits in enumerate(order):
+        target = pl.multiple_of((me ^ mask_bits) * own, own)
+        back_rows[pl.ds(target, own), :] = every[i * own : (i + 1) * own]
+    every = back_rows[...] * mask
     lanes = every[:, :128]
     for i in range(1, slots * rank // 128):
         lanes = lanes + every[:, i * 128 : (i + 1) * 128]
@@ -89,17 +146,25 @@
     for q in range(tp):
         send_ref[q, :, :share] = normed[:, q * share : (q + 1) * share]
         send_ref[q, :, share:] = back
-    me = me_ref[0]
-    for i, mask_bits in enumerate(order):
-        source = pl.multiple_of((me ^ mask_bits) * own, own)
-        cotp_ref[pl.ds(i * own, own), :] = cott[pl.ds(source, own), :]
-
-
-def product_kernel(cotp_ref, weight_ref, *parts):
-    out = jnp.dot(cotp_ref[...], weight_ref[...], preferred_element_type=F32)
-    each = parts[0].shape[0]
-    for i, part in enumerate(parts):
-        part[...] = out[i * each : (i + 1) * each].astype(BF)
+    multiply(cotp_ref[...], wbuf, copies, block, parts)
+
+
+def total_of(refs, i, each):
+    total = refs[0][i * each : (i + 1) * each].astype(F32)
+    for r in refs[1:]:
+        total = total + r[i * each : (i + 1) * each].astype(F32)
+    return total.astype(BF)
+
+
+def sum_kernel(groups, passed, *refs):
+    n_in = sum(t for t, _ in groups)
+    terms, outs = refs[: n_in], refs[n_in + passed :]
+    at, to = 0, 0
+    for n, m in groups:
+        each = terms[at].shape[0] // m
+        for i in range(m):
+            outs[to + i][...] = total_of(terms[at : at + n], i, each)
+        at, to = at + n, to + m
 
 
 def middle_kernel(rank, lens_ref, slots_ref, recv_ref, down_ref, send_ref, left_ref):
@@ -161,13 +226,17 @@
     out_ref[...] = (inv * (grad - normed * mean)).astype(BF)
 
 
-def call(kernel, out, n_in, smem=(), scratch=(), flops=0, nbytes=0, vmem=48):
+HBM = pl.BlockSpec(memory_space=pltpu.HBM)
+
+
+def call(kernel, out, specs, scratch=(), flops=0, nbytes=0, vmem=48, out_specs=None, alias=None):
     return pl.pallas_call(
         kernel,
         out_shape=out,
-        in_specs=[SMEM if i in smem else VMEM for i in range(n_in)],
-        out_specs=jax.tree.map(lambda _: VMEM, out),
+        in_specs=specs,
+        out_specs=jax.tree.map(lambda _: VMEM, out) if out_specs is None else out_specs,
         scratch_shapes=list(scratch),
+        input_output_aliases=alias or {},
         cost_estimate=pl.CostEstimate(flops=int(flops), bytes_accessed=int(nbytes), transcendentals=0),
         compiler_params=pltpu.CompilerParams(vmem_limit_bytes=vmem << 20),
     )
@@ -190,84 +259,112 @@
     slot = slots.reshape(1, count)
     down_flat = down_maps.reshape(count * rank, share)
 
-    send, cotp = call(
-        functools.partial(prep_kernel, order, rank),
-        (shape((tp, own, share + rows)), shape((rows, columns))),
-        6,
-        smem=(0,),
-        scratch=[pltpu.VMEM((rows, columns), BF)],
-        flops=2 * rows * columns * count * rank,
-        nbytes=3 << 20,
-    )(me, lens, slot, tokens, cotangent, up_maps)
-    recv = lax.all_to_all(send, "tp", split_axis=0, concat_axis=0, tiled=True)
-
-    def product(first, size):
-        block = 1024
-        m = len(stages[0])
-        each = rows // m
-        return pl.pallas_call(
-            product_kernel,
-            grid=(size // block,),
-            out_shape=[shape((each, size))] * m,
-            in_specs=[
-                pl.BlockSpec((rows, columns), lambda i: (0, 0)),
-                pl.BlockSpec((columns, block), lambda i: (0, first // block + i)),
-            ],
-            out_specs=[pl.BlockSpec((each, block), lambda i: (0, i))] * m,
-            cost_estimate=pl.CostEstimate(
-                flops=2 * rows * columns * size,
-                bytes_accessed=2 * columns * size + 2 * rows * size,
-                transcendentals=0,
-            ),
-            compiler_params=pltpu.CompilerParams(vmem_limit_bytes=32 << 20),
-        )(cotp, weight)
+    half = width // 2
+    block = half // 4
+    m = len(stages[0])
+    each = rows // m
+    dma = pltpu.SemaphoreType.DMA
+    cotp, *parts_a = call(
+        functools.partial(first_kernel, order, own, block),
+        [shape((rows, columns))] + [shape((each, half))] * m,
+        [SMEM, HBM, HBM],
+        scratch=[
+            pltpu.VMEM((columns, rows), BF),
+            pltpu.VMEM((rows, columns), BF),
+            pltpu.VMEM((columns, half), BF),
+            dma,
+            dma((half // block,)),
+        ],
+        flops=2 * rows * columns * half,
+        nbytes=2 * columns * half,
+    )(me, cotangent, weight)
 
     def pairs(m):
         return [(i, i ^ m) for i in range(tp)]
 
-    def scatter(parts):
-        for s, masks in enumerate(stages):
-            got = [lax.ppermute(part, "tp", pairs(m)) for m, part in zip(masks[1:], parts[1:])]
-            if s == len(stages) - 1:
-                return [parts[0]] + got
-            m = len(stages[s + 1])
-            each = parts[0].shape[0] // m
-            new = []
-            for i in range(m):
-                total = parts[0][i * each : (i + 1) * each].astype(F32)
-                for g in got:
-                    total = total + g[i * each : (i + 1) * each].astype(F32)
-                new.append(total.astype(BF))
-            parts = new
-
-    sizes = [width // 2, width // 2]
-    chunks = []
-    first = 0
-    for size in sizes:
-        chunks.append(scatter(product(first, size)))
-        first += size
+    def exchange(stage, parts):
+        return [parts[0]] + [lax.ppermute(part, "tp", pairs(m)) for m, part in zip(stages[stage][1:], parts[1:])]
+
+    def summed(groups, stage_of, passed=()):
+        flat = [t for g in groups for t in g]
+        cuts = [len(stages[s]) for s in stage_of]
+        out = []
+        for g, c in zip(groups, cuts):
+            out += [shape((g[0].shape[0] // c, g[0].shape[1]))] * c
+        n = len(flat)
+        res = call(
+            functools.partial(sum_kernel, [(len(g), c) for g, c in zip(groups, cuts)], len(passed)),
+            out + [shape(x.shape, x.dtype) for x in passed],
+            [VMEM] * n + [HBM] * len(passed),
+            out_specs=[VMEM] * len(out) + [HBM] * len(passed),
+            alias={n + i: len(out) + i for i in range(len(passed))},
+            nbytes=4 * sum(x.size for x in flat),
+        )(*flat, *passed)
+        cut, at = [], 0
+        for c in cuts:
+            cut.append(list(res[at : at + c]))
+            at += c
+        return cut, list(res[at:])
+
+    send, *parts_b = call(
+        functools.partial(second_kernel, order, rank, half, block),
+        [shape((tp, own, share + rows))] + [shape((each, half))] * m,
+        [SMEM, VMEM, VMEM, VMEM, HBM, HBM, HBM],
+        scratch=[
+            pltpu.VMEM((own, width), BF),
+            pltpu.VMEM((columns, count * rank), BF),
+            pltpu.VMEM((columns, half), BF),
+            pltpu.VMEM((rows, count * rank), F32),
+            dma((2,)),
+            dma((half // block,)),
+        ],
+        out_specs=[VMEM] * (1 + m),
+        flops=2 * rows * columns * (half + count * rank),
+        nbytes=2 * columns * (half + count * rank),
+    )(me, lens, slot, cotp, tokens, up_maps, weight)
+
+    last = len(stages) - 1
+    held_a = exchange(0, parts_a)
+    held_b = exchange(0, parts_b)
+    (cut_a,), (send,) = summed([held_a], [1], [send])
+    recv = lax.all_to_all(send, "tp", split_axis=0, concat_axis=0, tiled=True)
+    for stage in range(1, last + 1):
+        held_a = exchange(stage, cut_a)
+        if stage < last:
+            (cut_a, cut_b), _ = summed([held_a, held_b], [stage + 1, stage])
+        else:
+            (cut_b,), _ = summed([held_b], [stage])
+        held_b = exchange(stage, cut_b)
+    chunks = [held_a, held_b]
 
     send2, left = call(
         functools.partial(middle_kernel, rank),
         (shape((tp, own, share + rows)), shape((count * rank, rows))),
-        4,
+        [VMEM] * 4,
         flops=4 * rows * share * count * rank,
         nbytes=3 << 20,
     )(lens, slot, recv, down_flat)
     recv2 = lax.all_to_all(send2, "tp", split_axis=0, concat_axis=0, tiled=True)
     down_grad = call(
-        down_kernel, shape((count * rank, share), F32), 2, flops=2 * rows * share * count * rank, nbytes=3 << 20
+        down_kernel,
+        shape((count * rank, share), F32),
+        [VMEM] * 2,
+        flops=2 * rows * share * count * rank,
+        nbytes=3 << 20,
     )(left, recv)
     up_grad = call(
         functools.partial(up_kernel, rank),
         shape((columns, count * rank), F32),
-        4,
+        [VMEM] * 4,
         flops=2 * rows * columns * count * rank,
         nbytes=3 << 20,
     )(lens, slot, recv2, cotangent)
     flat = [piece for chunk in chunks for piece in chunk]
     grad_tokens = call(
-        functools.partial(final_kernel, [len(c) for c in chunks]), shape((own, width)), 2 + len(flat), nbytes=2 << 20
+        functools.partial(final_kernel, [len(c) for c in chunks]),
+        shape((own, width)),
+        [VMEM] * (2 + len(flat)),
+        nbytes=2 << 20,
     )(recv2, tokens, *flat)
     return grad_tokens, down_grad.reshape(count, rank, share), up_grad
 

time: 87.8 us -> 75.7 us (0.86)
  local copies, waits for them, and re-layouts: 14.5 us -> 5.72 us
  other arithmetic: 3.84 us -> 0 us
  waiting for transfers between devices: 30 us -> 26.3 us
  Pallas kernels: 15.3 us -> 18.1 us
  starting transfers between devices: 22.8 us -> 24.4 us
    ppermute x10, waiting for transfers between devices: 25.7 us -> 16 us  [exchange(): lax.ppermute(part, 'tp', pairs(m))]
    unnamed x26 -> x24, local copies, waits for them, and re-layouts: 14.5 us -> 5.72 us
    all_to_all x1, waiting for transfers between devices: 4.37 us -> 10.3 us  [body(): recv = lax.all_to_all(send, 'tp', split_axis=0, concat_axis=0, tiled=True)]
    convert_element_type x4 -> x0, other arithmetic: 3.84 us -> none  [scatter(): new.append(total.astype(BF))]
    pallas_call x4 -> x6, Pallas kernels: 10.4 us -> 12.4 us  [the longest x1 4.95 us: body(): call(functools.partial(second_kernel, order, rank, half, block), [shape((...]
    ppermute x10, starting transfers between devices: 12.2 us -> 13.5 us  [exchange(): lax.ppermute(part, 'tp', pairs(m))]
  transfers between devices with their start and end apart: 12 -> 12, of which waited for: 4 -> 3; matrix products, arithmetic and copies ran while one was open for 4% -> 0% of each run, Pallas kernels for 10% -> 17%
where the time goes in v2:
time: 75.7 us; the launch traced here: 75.2 us
  waiting for transfers between devices  26.3 us (35%)
  starting transfers between devices  24.4 us (32%)
  Pallas kernels  18.1 us (24%)
  local copies, waits for them, and re-layouts  5.72 us (8%)
  between operations  0.76 us (1%)
    ppermute x10, waiting for transfers between devices, exchange(): lax.ppermute(part, 'tp', pairs(m))  16 us
    ppermute x10, starting transfers between devices, exchange(): lax.ppermute(part, 'tp', pairs(m))  13.5 us
    all_to_all x1, waiting for transfers between devices, body(): recv = lax.all_to_all(send, 'tp', split_axis=0, concat_axis=0, tiled=True)  10.3 us
    all_to_all x1, starting transfers between devices, body(): recv = lax.all_to_all(send, 'tp', split_axis=0, concat_axis=0, tiled=True)  7.37 us
    unnamed x24, local copies, waits for them, and re-layouts  5.72 us
    pallas_call x1, Pallas kernels, body(): call(functools.partial(second_kernel, order, rank, half, block), [shape((...  4.95 us
    pallas_call x1, Pallas kernels, body(): call(functools.partial(first_kernel, order, own, block), [shape((rows, co...  3.88 us
    all_to_all x1, starting transfers between devices, body(): recv2 = lax.all_to_all(send2, 'tp', split_axis=0, concat_axis=0, tiled=True)  3.55 us
  transfers between devices with their start and end apart: 12, of which 3 were waited for; matrix products, arithmetic and copies ran while one was open for 0% of the time, Pallas kernels for 17%

profile of v2, /device:TPU:0, one launch (start us, length us, event | category | flops | bytes accessed | tf_op | source)
XLA Modules:
  0.0 75.2 jit_solution(4129876593768172598)
XLA Ops:
  0.6 0.0 copy-start
  0.6 1.0 %copy-done = bf16[640,256]{1,0:T(8,128)(2,1)S(1)} copy-done((bf16[640,256]{1,0:T(8,128)(2,1)S(1)}, bf16[640,256]{1,0:T(8,128)(2,1)}, u32[]{:S(2)}) %copy-start) | copy-done | bytes 327704
  1.6 0.0 copy-start.2
  1.6 0.0 copy-start.3
  1.6 0.0 copy-start.8
  1.6 0.0 copy-start.9
  1.6 3.9 %shard_map.94 = (bf16[256,640]{1,0:T(8,128)(2,1)S(1)}, bf16[128,4096]{1,0:T(8,128)(2,1)S(1)}, bf16[128,4096]{1,0:T(8,128)(2,1)S(1)}) custom-call(s32[1]{0:T(128)} %bitcast.2.me_ref, bf16[640,256]{1,0:T(8,128)(2,1)S(1)} %copy-done, bf16[640,8192]{1,0:T(8,128)(2,1)} %weight_hbm.3), custom_call_target="tpu_custom_call" | custom-call | flops 1342177280 | bytes 5242880 | tf_op jit(solution)/shard_map/pallas_call | solution.py:267
  5.5 0.5 collective-permute-start
  6.0 0.0 copy-done.2
  6.0 0.0 copy-done.3
  6.0 0.0 copy-done.8
  6.0 0.0 copy-done.9
  6.0 5.0 %shard_map.95 = (bf16[16,16,768]{2,1,0:T(8,128)(2,1)}, bf16[128,4096]{1,0:T(8,128)(2,1)S(1)}, bf16[128,4096]{1,0:T(8,128)(2,1)}) custom-call(s32[1]{0:T(128)} %bitcast.2.me_ref, s32[1,64]{1,0:T(1,128)S(1)} %bitcast.5, s32[1,64]{1,0:T(1,128)S(1)} %bitcast.8, bf16[256,640]{1,0:T(8,128)(2,1)S(1)} %get-tuple-element.26.cotp_ref, bf16[16,8192]{1,0:T(8,128)(2,1)S(1)} %copy-done.3, ...), custom_call_target="tpu_custom_call" | custom-call | flops 1677721600 | bytes 6553600 | tf_op jit(solution)/shard_map/pallas_call | solution.py:309
  11.0 0.1 collective-permute-start.2
  11.1 0.0 collective-permute-done.refs_1_
  11.1 0.2 shard_map.96
  11.4 0.0 copy-start.6
  11.4 0.8 %copy-done.6 = bf16[64,4096]{1,0:T(8,128)(2,1)} copy-done((bf16[64,4096]{1,0:T(8,128)(2,1)}, bf16[64,4096]{1,0:T(8,128)(2,1)S(1)}, u32[]{:S(2)}) %copy-start.6) | copy-done | bytes 524312
  12.2 0.0 copy-start.11
  12.2 0.8 %copy-done.11 = bf16[64,4096]{1,0:T(8,128)(2,1)} copy-done((bf16[64,4096]{1,0:T(8,128)(2,1)}, bf16[64,4096]{1,0:T(8,128)(2,1)S(1)}, u32[]{:S(2)}) %copy-start.11) | copy-done | bytes 524312
  13.0 7.4 %all-to-all-start = ((bf16[16,16,768]{2,1,0:T(8,128)(2,1)}), bf16[16,16,768]{2,1,0:T(8,128)(2,1)S(1)}, u32[]{:S(2)}, u32[]{:S(2)}) async-start(bf16[16,16,768]{2,1,0:T(8,128)(2,1)} %get-tuple-element.28), calls=%async_computation | async-start | bytes 786432 | tf_op jit(solution)/shard_map/all_to_all | solution.py:330
  20.4 1.9 %collective-permute-start.1 = (bf16[64,4096]{1,0:T(8,128)(2,1)}, bf16[64,4096]{1,0:T(8,128)(2,1)}, u32[]{:S(2)}, u32[]{:S(2)}) collective-permute-start(bf16[64,4096]{1,0:T(8,128)(2,1)} %copy-done.11), channel_id=1, source_target_pairs={{0,2},{1,3},{2,0},{3,1},{4,6},{5,7},{6,4},{7,5},{8,10},{9,11},{10,... | collective-permute-start | bytes 1572872 | tf_op jit(solution)/shard_map/ppermute | solution.py:286
  22.3 10.3 %all-to-all-done.recv_ref = bf16[16,16,768]{2,1,0:T(8,128)(2,1)S(1)} async-done(((bf16[16,16,768]{2,1,0:T(8,128)(2,1)}), bf16[16,16,768]{2,1,0:T(8,128)(2,1)S(1)}, u32[]{:S(2)}, u32[]{:S(2)}) %all-to-all-start) | async-done | bytes 393248 | tf_op jit(solution)/shard_map/all_to_all | solution.py:330
  32.6 0.0 copy-start.10
  32.6 1.2 %copy-done.10 = bf16[64,16,512]{2,1,0:T(8,128)(2,1)S(1)} copy-done((bf16[64,16,512]{2,1,0:T(8,128)(2,1)S(1)}, bf16[64,16,512]{2,1,0:T(8,128)(2,1)}, u32[]{:S(2)}) %copy-start.10) | copy-done | bytes 1048600
  33.8 2.0 %shard_map.97 = (bf16[16,16,768]{2,1,0:T(8,128)(2,1)}, bf16[1024,256]{1,0:T(8,128)(2,1)S(1)}) custom-call(s32[1,64]{1,0:T(1,128)S(1)} %bitcast.6, s32[1,64]{1,0:T(1,128)S(1)} %bitcast.9, bf16[16,16,768]{2,1,0:T(8,128)(2,1)S(1)} %all-to-all-done.recv_ref, bf16[1024,512]{1,0:T(8,128)(2,1)S(1)} %bitcast.11), custom_call_target="tpu_custom_call" | custom-call | flops 536870912 | bytes 3145728 | tf_op jit(solution)/shard_map/pallas_call | solution.py:340
  35.8 0.0 copy-start.4
  35.8 0.8 %copy-done.4 = bf16[1024,256]{1,0:T(8,128)(2,1)} copy-done((bf16[1024,256]{1,0:T(8,128)(2,1)}, bf16[1024,256]{1,0:T(8,128)(2,1)S(1)}, u32[]{:S(2)}) %copy-start.4) | copy-done | bytes 524312
  36.6 3.6 %all-to-all-start.1 = ((bf16[16,16,768]{2,1,0:T(8,128)(2,1)}), bf16[16,16,768]{2,1,0:T(8,128)(2,1)S(1)}, u32[]{:S(2)}, u32[]{:S(2)}) async-start(bf16[16,16,768]{2,1,0:T(8,128)(2,1)} %get-tuple-element.29), calls=%async_computation.1 | async-start | bytes 786432 | tf_op jit(solution)/shard_map/all_to_all | solution.py:347
  40.2 0.0 copy-start.5
  40.2 0.0 collective-permute-done.2.refs_3_
  40.2 0.0 collective-permute-done.1.refs_1_
  40.2 0.0 copy-start.7
  40.2 1.1 %copy-done.7 = bf16[64,4096]{1,0:T(8,128)(2,1)S(1)} copy-done((bf16[64,4096]{1,0:T(8,128)(2,1)S(1)}, bf16[64,4096]{1,0:T(8,128)(2,1)}, u32[]{:S(2)}) %copy-start.7) | copy-done | bytes 524312
  41.3 1.4 %shard_map.98 = (bf16[16,4096]{1,0:T(8,128)(2,1)S(1)}, bf16[16,4096]{1,0:T(8,128)(2,1)S(1)}, bf16[16,4096]{1,0:T(8,128)(2,1)S(1)}, bf16[16,4096]{1,0:T(8,128)(2,...) custom-call(bf16[64,4096]{1,0:T(8,128)(2,1)S(1)} %copy-done.7, ...), custom_call_target="tpu_custom_call" | custom-call | bytes 6291456 | tf_op jit(solution)/shard_map/pallas_call | solution.py:295
  42.7 0.0 copy-start.1
  42.8 2.0 %collective-permute-start.6 = (bf16[64,4096]{1,0:T(8,128)(2,1)S(1)}, bf16[64,4096]{1,0:T(8,128)(2,1)S(1)}, u32[]{:S(2)}, u32[]{:S(2)}) collective-permute-start(bf16[64,4096]{1,0:T(8,128)(2,1)S(1)} %get-tuple-element.39), channel_id=1, source_target_pairs={{0,2},{1,3},{2,0},{3,1},{4,6},{5,7},{6,4},{7,5},{8,10},{9,11},{10,... | collective-permute-start | bytes 1572872 | tf_op jit(solution)/shard_map/ppermute | solution.py:286
  44.7 1.5 %collective-permute-start.3 = (bf16[16,4096]{1,0:T(8,128)(2,1)S(1)}, bf16[16,4096]{1,0:T(8,128)(2,1)S(1)}, u32[]{:S(2)}, u32[]{:S(2)}) collective-permute-start(bf16[16,4096]{1,0:T(8,128)(2,1)S(1)} %get-tuple-element.35), channel_id=1, source_target_pairs={{0,4},{1,5},{2,6},{3,7},{4,0},{5,1},{6,2},{7,3},{8,12},{9,13},{10,... | collective-permute-start | bytes 393224 | tf_op jit(solution)/shard_map/ppermute | solution.py:286
  46.2 2.4 %collective-permute-start.4 = (bf16[16,4096]{1,0:T(8,128)(2,1)S(1)}, bf16[16,4096]{1,0:T(8,128)(2,1)S(1)}, u32[]{:S(2)}, u32[]{:S(2)}) collective-permute-start(bf16[16,4096]{1,0:T(8,128)(2,1)S(1)} %get-tuple-element.36), channel_id=1, source_target_pairs={{0,8},{1,9},{2,10},{3,11},{4,12},{5,13},{6,14},{7,15},{8,0},{9,1},... | collective-permute-start | bytes 393224 | tf_op jit(solution)/shard_map/ppermute | solution.py:286
  48.6 0.6 collective-permute-start.5
  49.1 10.0 %collective-permute-done.6.refs_1_ = bf16[64,4096]{1,0:T(8,128)(2,1)S(1)} collective-permute-done((bf16[64,4096]{1,0:T(8,128)(2,1)S(1)}, bf16[64,4096]{1,0:T(8,128)(2,1)S(1)}, u32[]{:S(2)}, u32[]{:S(2)}) %collective-permute-start.6) | collective-permute-done | bytes 524320 | tf_op jit(solution)/shard_map/ppermute | solution.py:286
  59.1 0.1 shard_map.99
  59.2 2.1 %collective-permute-start.7 = (bf16[16,4096]{1,0:T(8,128)(2,1)S(1)}, bf16[16,4096]{1,0:T(8,128)(2,1)S(1)}, u32[]{:S(2)}, u32[]{:S(2)}) collective-permute-start(bf16[16,4096]{1,0:T(8,128)(2,1)S(1)} %get-tuple-element.41), channel_id=1, source_target_pairs={{0,4},{1,5},{2,6},{3,7},{4,0},{5,1},{6,2},{7,3},{8,12},{9,13},{10,... | collective-permute-start | bytes 393224 | tf_op jit(solution)/shard_map/ppermute | solution.py:286
  61.3 1.6 %collective-permute-start.8 = (bf16[16,4096]{1,0:T(8,128)(2,1)S(1)}, bf16[16,4096]{1,0:T(8,128)(2,1)S(1)}, u32[]{:S(2)}, u32[]{:S(2)}) collective-permute-start(bf16[16,4096]{1,0:T(8,128)(2,1)S(1)} %get-tuple-element.42), channel_id=1, source_target_pairs={{0,8},{1,9},{2,10},{3,11},{4,12},{5,13},{6,14},{7,15},{8,0},{9,1},... | collective-permute-start | bytes 393224 | tf_op jit(solution)/shard_map/ppermute | solution.py:286
  62.9 0.0 collective-permute-done.3.refs_1_
  62.9 0.8 %collective-permute-start.9 = (bf16[16,4096]{1,0:T(8,128)(2,1)S(1)}, bf16[16,4096]{1,0:T(8,128)(2,1)S(1)}, u32[]{:S(2)}, u32[]{:S(2)}) collective-permute-start(bf16[16,4096]{1,0:T(8,128)(2,1)S(1)} %get-tuple-element.43), channel_id=1, source_target_pairs={{0,12},{1,13},{2,14},{3,15},{4,8},{5,9},{6,10},{7,11},{8,4},{9,5},... | collective-permute-start | bytes 393224 | tf_op jit(solution)/shard_map/ppermute | solution.py:286
  63.8 0.0 copy-done.5
  63.8 1.8 %shard_map.101 = f32[1024,512]{1,0:T(8,128)} custom-call(bf16[1024,256]{1,0:T(8,128)(2,1)S(1)} %copy-done.5, bf16[16,16,768]{2,1,0:T(8,128)(2,1)S(1)} %all-to-all-done.recv_ref), custom_call_target="tpu_custom_call" | custom-call | flops 268435456 | bytes 3145728 | tf_op jit(solution)/shard_map/pallas_call | solution.py:348
  65.5 0.0 all-to-all-done.1.recv_ref
  65.5 0.0 copy-done.1
  65.5 2.5 %shard_map.102 = f32[640,1024]{1,0:T(8,128)} custom-call(s32[1,64]{1,0:T(1,128)S(1)} %bitcast.7, s32[1,64]{1,0:T(1,128)S(1)} %bitcast.10, bf16[16,16,768]{2,1,0:T(8,128)(2,1)S(1)} %all-to-all-done.1.recv_ref, bf16[640,256]{1,0:T(8,128)(2,1)S(1)} %copy-done.1), custom_call_target="tpu_custom_call" | custom-call | flops 335544320 | bytes 3145728 | tf_op jit(solution)/shard_map/pallas_call | solution.py:355
  68.0 0.0 collective-permute-done.4.refs_2_
  68.0 0.0 collective-permute-done.5.refs_3_
  68.0 0.0 collective-permute-done.7.refs_5_
  68.1 6.0 %collective-permute-done.8.refs_6_ = bf16[16,4096]{1,0:T(8,128)(2,1)S(1)} collective-permute-done((bf16[16,4096]{1,0:T(8,128)(2,1)S(1)}, bf16[16,4096]{1,0:T(8,128)(2,1)S(1)}, u32[]{:S(2)}, u32[]{:S(2)}) %collective-permute-start.8) | collective-permute-done | bytes 131104 | tf_op jit(solution)/shard_map/ppermute | solution.py:286
  74.0 0.0 collective-permute-done.9.refs_7_
  74.0 1.2 %shard_map.100 = bf16[16,8192]{1,0:T(8,128)(2,1)} custom-call(bf16[16,16,768]{2,1,0:T(8,128)(2,1)S(1)} %all-to-all-done.1.recv_ref, bf16[16,8192]{1,0:T(8,128)(2,1)S(1)} %copy-done.3, bf16[16,4096]{1,0:T(8,128)(2,1)S(1)} %get-tuple-element.34.refs_0_, bf16[16,4096]{1,0:T(8,128)(2,1)S(1)} %collective-permute-done.3.refs_1_, ...), custom_call_target="tpu_custom_call" | custom-call | bytes 2097152 | tf_op jit(solution)/shard_map/pallas_call | solution.py:363
Async XLA Ops:
  0.6 1.0 %copy-start = (bf16[640,256]{1,0:T(8,128)(2,1)S(1)}, bf16[640,256]{1,0:T(8,128)(2,1)}, u32[]{:S(2)}) copy-start(bf16[640,256]{1,0:T(8,128)(2,1)} %cot_ref.1) | copy-start | bytes 983044
  1.6 4.4 %copy-start.2 = (bf16[640,1024]{1,0:T(8,128)(2,1)S(1)}, bf16[640,1024]{1,0:T(8,128)(2,1)}, u32[]{:S(2)}) copy-start(bf16[640,1024]{1,0:T(8,128)(2,1)} %up_hbm.1) | copy-start | bytes 3932164
  1.6 4.4 %copy-start.3 = (bf16[16,8192]{1,0:T(8,128)(2,1)S(1)}, bf16[16,8192]{1,0:T(8,128)(2,1)}, u32[]{:S(2)}) copy-start(bf16[16,8192]{1,0:T(8,128)(2,1)} %tok_ref.1) | copy-start | bytes 786436
  1.6 4.4 %copy-start.8 = (s32[64]{0:T(128)S(1)}, s32[64]{0:T(128)}, u32[]{:S(2)}) copy-start(s32[64]{0:T(128)} %param.12) | copy-start | bytes 772
  1.6 4.4 %copy-start.9 = (s32[64]{0:T(128)S(1)}, s32[64]{0:T(128)}, u32[]{:S(2)}) copy-start(s32[64]{0:T(128)} %param.13) | copy-start | bytes 772
  5.5 5.6 %collective-permute-start = (bf16[128,4096]{1,0:T(8,128)(2,1)S(1)}, bf16[128,4096]{1,0:T(8,128)(2,1)S(1)}, u32[]{:S(2)}, u32[]{:S(2)}) collective-permute-start(bf16[128,4096]{1,0:T(8,128)(2,1)S(1)} %get-tuple-element.25), channel_id=1, source_target_pairs={{0,1},{1,0},{2,3},{3,2},{4,5},{5,4},{6,7},{7,6},{8,9},{9,8},{10,11... | collective-permute-start | bytes 3145736 | tf_op jit(solution)/shard_map/ppermute | solution.py:286
  11.0 29.2 %collective-permute-start.2 = (bf16[128,4096]{1,0:T(8,128)(2,1)}, bf16[128,4096]{1,0:T(8,128)(2,1)S(1)}, u32[]{:S(2)}, u32[]{:S(2)}) collective-permute-start(bf16[128,4096]{1,0:T(8,128)(2,1)} %get-tuple-element.33), channel_id=1, source_target_pairs={{0,1},{1,0},{2,3},{3,2},{4,5},{5,4},{6,7},{7,6},{8,9},{9,8},{10,11... | collective-permute-start | bytes 3145736 | tf_op jit(solution)/shard_map/ppermute | solution.py:286
  11.4 0.8 %copy-start.6 = (bf16[64,4096]{1,0:T(8,128)(2,1)}, bf16[64,4096]{1,0:T(8,128)(2,1)S(1)}, u32[]{:S(2)}) copy-start(bf16[64,4096]{1,0:T(8,128)(2,1)S(1)} %get-tuple-element.30.refs_0_) | copy-start | bytes 1572868
  12.2 0.8 %copy-start.11 = (bf16[64,4096]{1,0:T(8,128)(2,1)}, bf16[64,4096]{1,0:T(8,128)(2,1)S(1)}, u32[]{:S(2)}) copy-start(bf16[64,4096]{1,0:T(8,128)(2,1)S(1)} %get-tuple-element.31) | copy-start | bytes 1572868
  13.0 19.6 %all-to-all-start = ((bf16[16,16,768]{2,1,0:T(8,128)(2,1)}), bf16[16,16,768]{2,1,0:T(8,128)(2,1)S(1)}, u32[]{:S(2)}, u32[]{:S(2)}) async-start(bf16[16,16,768]{2,1,0:T(8,128)(2,1)} %get-tuple-element.28), calls=%async_computation | async-start | bytes 786432 | tf_op jit(solution)/shard_map/all_to_all | solution.py:330
  20.4 19.8 %collective-permute-start.1 = (bf16[64,4096]{1,0:T(8,128)(2,1)}, bf16[64,4096]{1,0:T(8,128)(2,1)}, u32[]{:S(2)}, u32[]{:S(2)}) collective-permute-start(bf16[64,4096]{1,0:T(8,128)(2,1)} %copy-done.11), channel_id=1, source_target_pairs={{0,2},{1,3},{2,0},{3,1},{4,6},{5,7},{6,4},{7,5},{8,10},{9,11},{10,... | collective-permute-start | bytes 1572872 | tf_op jit(solution)/shard_map/ppermute | solution.py:286
  32.6 1.2 %copy-start.10 = (bf16[64,16,512]{2,1,0:T(8,128)(2,1)S(1)}, bf16[64,16,512]{2,1,0:T(8,128)(2,1)}, u32[]{:S(2)}) copy-start(bf16[64,16,512]{2,1,0:T(8,128)(2,1)} %param.10) | copy-start | bytes 3145732
  35.8 0.8 %copy-start.4 = (bf16[1024,256]{1,0:T(8,128)(2,1)}, bf16[1024,256]{1,0:T(8,128)(2,1)S(1)}, u32[]{:S(2)}) copy-start(bf16[1024,256]{1,0:T(8,128)(2,1)S(1)} %get-tuple-element.44.left_ref) | copy-start | bytes 1572868
  36.6 28.9 %all-to-all-start.1 = ((bf16[16,16,768]{2,1,0:T(8,128)(2,1)}), bf16[16,16,768]{2,1,0:T(8,128)(2,1)S(1)}, u32[]{:S(2)}, u32[]{:S(2)}) async-start(bf16[16,16,768]{2,1,0:T(8,128)(2,1)} %get-tuple-element.29), calls=%async_computation.1 | async-start | bytes 786432 | tf_op jit(solution)/shard_map/all_to_all | solution.py:347
  40.2 23.6 %copy-start.5 = (bf16[1024,256]{1,0:T(8,128)(2,1)S(1)}, bf16[1024,256]{1,0:T(8,128)(2,1)}, u32[]{:S(2)}) copy-start(bf16[1024,256]{1,0:T(8,128)(2,1)} %copy-done.4) | copy-start | bytes 1572868
  40.2 1.1 %copy-start.7 = (bf16[64,4096]{1,0:T(8,128)(2,1)S(1)}, bf16[64,4096]{1,0:T(8,128)(2,1)}, u32[]{:S(2)}) copy-start(bf16[64,4096]{1,0:T(8,128)(2,1)} %copy-done.6) | copy-start | bytes 1572868
  42.7 22.8 %copy-start.1 = (bf16[640,256]{1,0:T(8,128)(2,1)S(1)}, bf16[640,256]{1,0:T(8,128)(2,1)}, u32[]{:S(2)}) copy-start(bf16[640,256]{1,0:T(8,128)(2,1)} %cot_ref.1) | copy-start | bytes 983044
  42.8 16.3 %collective-permute-start.6 = (bf16[64,4096]{1,0:T(8,128)(2,1)S(1)}, bf16[64,4096]{1,0:T(8,128)(2,1)S(1)}, u32[]{:S(2)}, u32[]{:S(2)}) collective-permute-start(bf16[64,4096]{1,0:T(8,128)(2,1)S(1)} %get-tuple-element.39), channel_id=1, source_target_pairs={{0,2},{1,3},{2,0},{3,1},{4,6},{5,7},{6,4},{7,5},{8,10},{9,11},{10,... | collective-permute-start | bytes 1572872 | tf_op jit(solution)/shard_map/ppermute | solution.py:286
  44.7 18.2 %collective-permute-start.3 = (bf16[16,4096]{1,0:T(8,128)(2,1)S(1)}, bf16[16,4096]{1,0:T(8,128)(2,1)S(1)}, u32[]{:S(2)}, u32[]{:S(2)}) collective-permute-start(bf16[16,4096]{1,0:T(8,128)(2,1)S(1)} %get-tuple-element.35), channel_id=1, source_target_pairs={{0,4},{1,5},{2,6},{3,7},{4,0},{5,1},{6,2},{7,3},{8,12},{9,13},{10,... | collective-permute-start | bytes 393224 | tf_op jit(solution)/shard_map/ppermute | solution.py:286
  46.2 21.9 %collective-permute-start.4 = (bf16[16,4096]{1,0:T(8,128)(2,1)S(1)}, bf16[16,4096]{1,0:T(8,128)(2,1)S(1)}, u32[]{:S(2)}, u32[]{:S(2)}) collective-permute-start(bf16[16,4096]{1,0:T(8,128)(2,1)S(1)} %get-tuple-element.36), channel_id=1, source_target_pairs={{0,8},{1,9},{2,10},{3,11},{4,12},{5,13},{6,14},{7,15},{8,0},{9,1},... | collective-permute-start | bytes 393224 | tf_op jit(solution)/shard_map/ppermute | solution.py:286
  48.6 19.5 %collective-permute-start.5 = (bf16[16,4096]{1,0:T(8,128)(2,1)S(1)}, bf16[16,4096]{1,0:T(8,128)(2,1)S(1)}, u32[]{:S(2)}, u32[]{:S(2)}) collective-permute-start(bf16[16,4096]{1,0:T(8,128)(2,1)S(1)} %get-tuple-element.37), channel_id=1, source_target_pairs={{0,12},{1,13},{2,14},{3,15},{4,8},{5,9},{6,10},{7,11},{8,4},{9,5},... | collective-permute-start | bytes 393224 | tf_op jit(solution)/shard_map/ppermute | solution.py:286
  59.2 8.8 %collective-permute-start.7 = (bf16[16,4096]{1,0:T(8,128)(2,1)S(1)}, bf16[16,4096]{1,0:T(8,128)(2,1)S(1)}, u32[]{:S(2)}, u32[]{:S(2)}) collective-permute-start(bf16[16,4096]{1,0:T(8,128)(2,1)S(1)} %get-tuple-element.41), channel_id=1, source_target_pairs={{0,4},{1,5},{2,6},{3,7},{4,0},{5,1},{6,2},{7,3},{8,12},{9,13},{10,... | collective-permute-start | bytes 393224 | tf_op jit(solution)/shard_map/ppermute | solution.py:286
  61.3 12.7 %collective-permute-start.8 = (bf16[16,4096]{1,0:T(8,128)(2,1)S(1)}, bf16[16,4096]{1,0:T(8,128)(2,1)S(1)}, u32[]{:S(2)}, u32[]{:S(2)}) collective-permute-start(bf16[16,4096]{1,0:T(8,128)(2,1)S(1)} %get-tuple-element.42), channel_id=1, source_target_pairs={{0,8},{1,9},{2,10},{3,11},{4,12},{5,13},{6,14},{7,15},{8,0},{9,1},... | collective-permute-start | bytes 393224 | tf_op jit(solution)/shard_map/ppermute | solution.py:286
  62.9 11.1 %collective-permute-start.9 = (bf16[16,4096]{1,0:T(8,128)(2,1)S(1)}, bf16[16,4096]{1,0:T(8,128)(2,1)S(1)}, u32[]{:S(2)}, u32[]{:S(2)}) collective-permute-start(bf16[16,4096]{1,0:T(8,128)(2,1)S(1)} %get-tuple-element.43), channel_id=1, source_target_pairs={{0,12},{1,13},{2,14},{3,15},{4,8},{5,9},{6,10},{7,11},{8,4},{9,5},... | collective-permute-start | bytes 393224 | tf_op jit(solution)/shard_map/ppermute | solution.py:286

commit v3 on v2

--- a/solution.py
+++ b/solution.py
@@ -106,8 +106,8 @@
     multiply(cotp_ref[...], wbuf, copies, block, parts)
 
 
-def second_kernel(order, rank, first, block, me_ref, lens_ref, slots_ref, cotp_ref, tok_hbm, up_hbm, weight_hbm, send_ref, *refs):
-    *parts, tokv, up, wbuf, back_rows, sem, sems = refs
+def second_kernel(order, rank, first, block, me_ref, lens_ref, slots_ref, cotp_ref, tok_hbm, up_hbm, weight_hbm, send_hbm, *refs):
+    *parts, send_ref, tokv, up, wbuf, back_rows, sem, sems = refs
     tp, own, _ = send_ref.shape
     width = tokv.shape[1]
     share = width // tp
@@ -146,7 +146,10 @@
     for q in range(tp):
         send_ref[q, :, :share] = normed[:, q * share : (q + 1) * share]
         send_ref[q, :, share:] = back
+    send_copy = pltpu.make_async_copy(send_ref, send_hbm, sem.at[2])
+    send_copy.start()
     multiply(cotp_ref[...], wbuf, copies, block, parts)
+    send_copy.wait()
 
 
 def total_of(refs, i, each):
@@ -167,11 +170,15 @@
         at, to = at + n, to + m
 
 
-def middle_kernel(rank, lens_ref, slots_ref, recv_ref, down_ref, send_ref, left_ref):
+def mask_kernel(rank, lens_ref, slots_ref, after_hbm, send_hbm, mask_ref, send_out):
+    mask_ref[...] = mask_by_column(lens_ref, slots_ref, mask_ref.shape[1], rank).astype(BF)
+
+
+def middle_kernel(rank, mask_ref, recv_ref, down_ref, after_hbm, send_hbm, left_ref, send_ref, sem):
     tp, own, wide = recv_ref.shape
     rows = tp * own
     share = wide - rows
-    mask = mask_by_column(lens_ref, slots_ref, rows, rank)
+    mask = mask_ref[...].astype(F32)
     normed = recv_ref[:, :, :share].reshape(rows, share)
     every = lax.dot_general(down_ref[...], normed, NT, preferred_element_type=F32) * mask
     slots = every.shape[0] // rank
@@ -183,6 +190,9 @@
     send_ref[:, :, :share] = term.astype(BF).reshape(tp, own, share)
     for q in range(tp):
         send_ref[q, :, share:] = low
+    copy = pltpu.make_async_copy(send_ref, send_hbm, sem)
+    copy.start()
+    copy.wait()
 
 
 def down_kernel(left_ref, recv_ref, out_ref):
@@ -193,11 +203,11 @@
     out_ref[...] = SCALE * jnp.dot(left_ref[...], normed, preferred_element_type=F32)
 
 
-def up_kernel(rank, lens_ref, slots_ref, recv_ref, cot_ref, out_ref):
+def up_kernel(rank, mask_ref, recv_ref, cot_ref, out_ref):
     tp, own, wide = recv_ref.shape
     rows = tp * own
     share = wide - rows
-    mask = mask_by_column(lens_ref, slots_ref, rows, rank)
+    mask = mask_ref[...].astype(F32)
     slots = mask.shape[0] // rank
     low = jnp.sum(recv_ref[:, :, share:].astype(F32), axis=0).astype(BF).astype(F32)
     left = (mask.reshape(slots, rank, rows) * low[None]).reshape(slots * rank, rows).astype(BF)
@@ -311,14 +321,15 @@
         [shape((tp, own, share + rows))] + [shape((each, half))] * m,
         [SMEM, VMEM, VMEM, VMEM, HBM, HBM, HBM],
         scratch=[
+            pltpu.VMEM((tp, own, share + rows), BF),
             pltpu.VMEM((own, width), BF),
             pltpu.VMEM((columns, count * rank), BF),
             pltpu.VMEM((columns, half), BF),
             pltpu.VMEM((rows, count * rank), F32),
-            dma((2,)),
+            dma((3,)),
             dma((half // block,)),
         ],
-        out_specs=[VMEM] * (1 + m),
+        out_specs=[HBM] + [VMEM] * m,
         flops=2 * rows * columns * (half + count * rank),
         nbytes=2 * columns * (half + count * rank),
     )(me, lens, slot, cotp, tokens, up_maps, weight)
@@ -326,7 +337,15 @@
     last = len(stages) - 1
     held_a = exchange(0, parts_a)
     held_b = exchange(0, parts_b)
-    (cut_a,), (send,) = summed([held_a], [1], [send])
+    (cut_a,), _ = summed([held_a], [1])
+    mask, send = call(
+        functools.partial(mask_kernel, rank),
+        [shape((count * rank, rows)), shape(send.shape)],
+        [VMEM, VMEM, HBM, HBM],
+        out_specs=[VMEM, HBM],
+        alias={3: 1},
+        flops=2 * rows * count * count * rank,
+    )(lens, slot, cut_a[0], send)
     recv = lax.all_to_all(send, "tp", split_axis=0, concat_axis=0, tiled=True)
     for stage in range(1, last + 1):
         held_a = exchange(stage, cut_a)
@@ -334,16 +353,20 @@
             (cut_a, cut_b), _ = summed([held_a, held_b], [stage + 1, stage])
         else:
             (cut_b,), _ = summed([held_b], [stage])
+        if stage == 1:
+            after = cut_b[0]
         held_b = exchange(stage, cut_b)
     chunks = [held_a, held_b]
 
     send2, left = call(
         functools.partial(middle_kernel, rank),
         (shape((tp, own, share + rows)), shape((count * rank, rows))),
-        [VMEM] * 4,
+        [VMEM] * 3 + [HBM],
+        scratch=[pltpu.VMEM((tp, own, share + rows), BF), dma],
+        out_specs=[HBM, VMEM],
         flops=4 * rows * share * count * rank,
         nbytes=3 << 20,
-    )(lens, slot, recv, down_flat)
+    )(mask, recv, down_flat, after)
     recv2 = lax.all_to_all(send2, "tp", split_axis=0, concat_axis=0, tiled=True)
     down_grad = call(
         down_kernel,
@@ -355,10 +378,10 @@
     up_grad = call(
         functools.partial(up_kernel, rank),
         shape((columns, count * rank), F32),
-        [VMEM] * 4,
+        [VMEM] * 3,
         flops=2 * rows * columns * count * rank,
         nbytes=3 << 20,
-    )(lens, slot, recv2, cotangent)
+    )(mask, recv2, cotangent)
     flat = [piece for chunk in chunks for piece in chunk]
     grad_tokens = call(
         functools.partial(final_kernel, [len(c) for c in chunks]),

time: 75.7 us -> 83.1 us (1.098)
  waiting for transfers between devices: 26.3 us -> 35.1 us
  local copies, waits for them, and re-layouts: 5.72 us -> 2.22 us
  starting transfers between devices: 24.4 us -> 25.5 us
  Pallas kernels: 18.1 us -> 19.2 us
    ppermute x10, waiting for transfers between devices: 16 us -> 35.1 us  [exchange(): lax.ppermute(part, 'tp', pairs(m))]
    all_to_all x1, waiting for transfers between devices: 10.3 us -> 0.01 us  [body(): recv = lax.all_to_all(send, 'tp', split_axis=0, concat_axis=0, tiled=True)]
    unnamed x24 -> x16, local copies, waits for them, and re-layouts: 5.72 us -> 2.22 us
    pallas_call x3, Pallas kernels: 1.81 us -> 3.29 us  [summed(): call(functools.partial(sum_kernel, [(len(g), c) for g, c in zip(groups, c...]
    all_to_all x1, starting transfers between devices: 3.55 us -> 4.79 us  [body(): recv2 = lax.all_to_all(send2, 'tp', split_axis=0, concat_axis=0, tiled=True)]
  transfers between devices with their start and end apart: 12 -> 12, of which waited for: 3 -> 3; matrix products, arithmetic and copies ran while one was open for 0% -> 0% of each run, Pallas kernels for 17% -> 15%
where the time goes in v3:
time: 83.1 us; the launch traced here: 82.7 us
  waiting for transfers between devices  35.1 us (42%)
  starting transfers between devices  25.5 us (31%)
  Pallas kernels  19.2 us (23%)
  local copies, waits for them, and re-layouts  2.22 us (3%)
    ppermute x10, waiting for transfers between devices, exchange(): lax.ppermute(part, 'tp', pairs(m))  35.1 us
    ppermute x10, starting transfers between devices, exchange(): lax.ppermute(part, 'tp', pairs(m))  13.3 us
    all_to_all x1, starting transfers between devices, body(): recv = lax.all_to_all(send, 'tp', split_axis=0, concat_axis=0, tiled=True)  7.4 us
    pallas_call x1, Pallas kernels, body(): call(functools.partial(second_kernel, order, rank, half, block), [shape((...  4.95 us
    all_to_all x1, starting transfers between devices, body(): recv2 = lax.all_to_all(send2, 'tp', split_axis=0, concat_axis=0, tiled=True)  4.79 us
    pallas_call x1, Pallas kernels, body(): call(functools.partial(first_kernel, order, own, block), [shape((rows, co...  3.88 us
    pallas_call x3, Pallas kernels, summed(): call(functools.partial(sum_kernel, [(len(g), c) for g, c in zip(groups, c...  3.29 us
    unnamed x16, local copies, waits for them, and re-layouts  2.22 us
  transfers between devices with their start and end apart: 12, of which 3 were waited for; matrix products, arithmetic and copies ran while one was open for 0% of the time, Pallas kernels for 15%

profile of v3, /device:TPU:0, one launch (start us, length us, event | category | flops | bytes accessed | tf_op | source)
XLA Modules:
  0.0 82.7 jit_solution(7330496145407572035)
XLA Ops:
  0.6 0.0 copy-start.1
  0.6 1.0 %copy-done.1 = bf16[640,256]{1,0:T(8,128)(2,1)S(1)} copy-done((bf16[640,256]{1,0:T(8,128)(2,1)S(1)}, bf16[640,256]{1,0:T(8,128)(2,1)}, u32[]{:S(2)}) %copy-start.1) | copy-done | bytes 327704
  1.6 0.0 copy-start
  1.6 0.0 copy-start.3
  1.6 0.0 copy-start.6
  1.6 0.0 copy-start.7
  1.6 3.9 %shard_map.94 = (bf16[256,640]{1,0:T(8,128)(2,1)S(1)}, bf16[128,4096]{1,0:T(8,128)(2,1)S(1)}, bf16[128,4096]{1,0:T(8,128)(2,1)S(1)}) custom-call(s32[1]{0:T(128)} %bitcast.2.me_ref, bf16[640,256]{1,0:T(8,128)(2,1)S(1)} %copy-done.1, bf16[640,8192]{1,0:T(8,128)(2,1)} %weight_hbm.3), custom_call_target="tpu_custom_call" | custom-call | flops 1342177280 | bytes 5242880 | tf_op jit(solution)/shard_map/pallas_call | solution.py:277
  5.5 0.5 collective-permute-start
  6.0 0.0 copy-done
  6.0 0.0 copy-done.3
  6.0 0.0 copy-done.6
  6.0 0.0 copy-done.7
  6.0 4.9 %shard_map.96 = (bf16[16,16,768]{2,1,0:T(8,128)(2,1)}, bf16[128,4096]{1,0:T(8,128)(2,1)S(1)}, bf16[128,4096]{1,0:T(8,128)(2,1)}) custom-call(s32[1]{0:T(128)} %bitcast.2.me_ref, s32[1,64]{1,0:T(1,128)S(1)} %bitcast.6, s32[1,64]{1,0:T(1,128)S(1)} %bitcast.8, bf16[256,640]{1,0:T(8,128)(2,1)S(1)} %get-tuple-element.28.cotp_ref, bf16[16,8192]{1,0:T(8,128)(2,1)S(1)} %copy-done.3, ...), custom_call_target="tpu_custom_call" | custom-call | flops 1677721600 | bytes 6553600 | tf_op jit(solution)/shard_map/pallas_call | solution.py:319
  11.0 0.1 collective-permute-start.2
  11.1 0.0 collective-permute-done.refs_1_
  11.1 0.2 shard_map.95
  11.4 0.6 shard_map.97
  11.9 7.4 %all-to-all-start = ((bf16[16,16,768]{2,1,0:T(8,128)(2,1)}), bf16[16,16,768]{2,1,0:T(8,128)(2,1)S(1)}, u32[]{:S(2)}, u32[]{:S(2)}) async-start(bf16[16,16,768]{2,1,0:T(8,128)(2,1)} %get-tuple-element.31), calls=%async_computation | async-start | bytes 786432 | tf_op jit(solution)/shard_map/all_to_all | solution.py:349
  19.4 1.9 %collective-permute-start.1 = (bf16[64,4096]{1,0:T(8,128)(2,1)S(1)}, bf16[64,4096]{1,0:T(8,128)(2,1)S(1)}, u32[]{:S(2)}, u32[]{:S(2)}) collective-permute-start(bf16[64,4096]{1,0:T(8,128)(2,1)S(1)} %get-tuple-element.32), channel_id=1, source_target_pairs={{0,2},{1,3},{2,0},{3,1},{4,6},{5,7},{6,4},{7,5},{8,10},{9,11},{10,... | collective-permute-start | bytes 1572872 | tf_op jit(solution)/shard_map/ppermute | solution.py:296
  21.3 0.0 collective-permute-done.2.refs_3_
  21.3 16.6 %collective-permute-done.1.refs_1_ = bf16[64,4096]{1,0:T(8,128)(2,1)S(1)} collective-permute-done((bf16[64,4096]{1,0:T(8,128)(2,1)S(1)}, bf16[64,4096]{1,0:T(8,128)(2,1)S(1)}, u32[]{:S(2)}, u32[]{:S(2)}) %collective-permute-start.1) | collective-permute-done | bytes 524320 | tf_op jit(solution)/shard_map/ppermute | solution.py:296
  37.9 2.2 %shard_map.98 = (bf16[16,4096]{1,0:T(8,128)(2,1)S(1)}, bf16[16,4096]{1,0:T(8,128)(2,1)}, bf16[16,4096]{1,0:T(8,128)(2,1)}, bf16[16,4096]{1,0:T(8,128)(2,1)}, bf1...) custom-call(bf16[64,4096]{1,0:T(8,128)(2,1)S(1)} %get-tuple-element.27.after_hbm.refs_0_, ...), custom_call_target="tpu_custom_call" | custom-call | bytes 6291456 | tf_op jit(solution)/shard_map/pallas_call | solution.py:305
  40.2 0.0 all-to-all-done.recv_ref
  40.2 0.0 copy-start.5
  40.2 1.2 %copy-done.5 = bf16[64,16,512]{2,1,0:T(8,128)(2,1)S(1)} copy-done((bf16[64,16,512]{2,1,0:T(8,128)(2,1)S(1)}, bf16[64,16,512]{2,1,0:T(8,128)(2,1)}, u32[]{:S(2)}) %copy-start.5) | copy-done | bytes 1048600
  41.4 1.5 %shard_map.99 = (bf16[16,16,768]{2,1,0:T(8,128)(2,1)}, bf16[1024,256]{1,0:T(8,128)(2,1)S(1)}) custom-call(bf16[1024,256]{1,0:T(8,128)(2,1)S(1)} %get-tuple-element.30.mask_ref, bf16[16,16,768]{2,1,0:T(8,128)(2,1)S(1)} %all-to-all-done.recv_ref, bf16[1024,512]{1,0:T(8,128)(2,1)S(1)} %bitcast.5, bf16[64,4096]{1,0:T(8,128)(2,1)S(1)} %get-tuple-element.35.after_hbm.refs_0_), custom_call_target="tpu_custom_call" | custom-call | flops 536870912 | bytes 3145728 | tf_op jit(solution)/shard_map/pallas_call | solution.py:361
  42.9 0.0 copy-start.2
  42.9 4.8 %all-to-all-start.1 = ((bf16[16,16,768]{2,1,0:T(8,128)(2,1)}), bf16[16,16,768]{2,1,0:T(8,128)(2,1)S(1)}, u32[]{:S(2)}, u32[]{:S(2)}) async-start(bf16[16,16,768]{2,1,0:T(8,128)(2,1)} %get-tuple-element.36), calls=%async_computation.1 | async-start | bytes 786432 | tf_op jit(solution)/shard_map/all_to_all | solution.py:370
  47.7 1.9 %collective-permute-start.6 = (bf16[64,4096]{1,0:T(8,128)(2,1)}, bf16[64,4096]{1,0:T(8,128)(2,1)S(1)}, u32[]{:S(2)}, u32[]{:S(2)}) collective-permute-start(bf16[64,4096]{1,0:T(8,128)(2,1)} %get-tuple-element.41), channel_id=1, source_target_pairs={{0,2},{1,3},{2,0},{3,1},{4,6},{5,7},{6,4},{7,5},{8,10},{9,11},{10,... | collective-permute-start | bytes 1572872 | tf_op jit(solution)/shard_map/ppermute | solution.py:296
  49.7 1.5 %collective-permute-start.3 = (bf16[16,4096]{1,0:T(8,128)(2,1)}, bf16[16,4096]{1,0:T(8,128)(2,1)S(1)}, u32[]{:S(2)}, u32[]{:S(2)}) collective-permute-start(bf16[16,4096]{1,0:T(8,128)(2,1)} %get-tuple-element.38), channel_id=1, source_target_pairs={{0,4},{1,5},{2,6},{3,7},{4,0},{5,1},{6,2},{7,3},{8,12},{9,13},{10,... | collective-permute-start | bytes 393224 | tf_op jit(solution)/shard_map/ppermute | solution.py:296
  51.1 2.4 %collective-permute-start.4 = (bf16[16,4096]{1,0:T(8,128)(2,1)}, bf16[16,4096]{1,0:T(8,128)(2,1)S(1)}, u32[]{:S(2)}, u32[]{:S(2)}) collective-permute-start(bf16[16,4096]{1,0:T(8,128)(2,1)} %get-tuple-element.39), channel_id=1, source_target_pairs={{0,8},{1,9},{2,10},{3,11},{4,12},{5,13},{6,14},{7,15},{8,0},{9,1},... | collective-permute-start | bytes 393224 | tf_op jit(solution)/shard_map/ppermute | solution.py:296
  53.5 0.6 collective-permute-start.5
  54.1 12.3 %collective-permute-done.6.refs_1_ = bf16[64,4096]{1,0:T(8,128)(2,1)S(1)} collective-permute-done((bf16[64,4096]{1,0:T(8,128)(2,1)}, bf16[64,4096]{1,0:T(8,128)(2,1)S(1)}, u32[]{:S(2)}, u32[]{:S(2)}) %collective-permute-start.6) | collective-permute-done | bytes 524320 | tf_op jit(solution)/shard_map/ppermute | solution.py:296
  66.3 0.8 shard_map.100
  67.1 1.5 %collective-permute-start.7 = (bf16[16,4096]{1,0:T(8,128)(2,1)}, bf16[16,4096]{1,0:T(8,128)(2,1)S(1)}, u32[]{:S(2)}, u32[]{:S(2)}) collective-permute-start(bf16[16,4096]{1,0:T(8,128)(2,1)} %get-tuple-element.43), channel_id=1, source_target_pairs={{0,4},{1,5},{2,6},{3,7},{4,0},{5,1},{6,2},{7,3},{8,12},{9,13},{10,... | collective-permute-start | bytes 393224 | tf_op jit(solution)/shard_map/ppermute | solution.py:296
  68.6 2.4 %collective-permute-start.8 = (bf16[16,4096]{1,0:T(8,128)(2,1)}, bf16[16,4096]{1,0:T(8,128)(2,1)S(1)}, u32[]{:S(2)}, u32[]{:S(2)}) collective-permute-start(bf16[16,4096]{1,0:T(8,128)(2,1)} %get-tuple-element.44), channel_id=1, source_target_pairs={{0,8},{1,9},{2,10},{3,11},{4,12},{5,13},{6,14},{7,15},{8,0},{9,1},... | collective-permute-start | bytes 393224 | tf_op jit(solution)/shard_map/ppermute | solution.py:296
  71.0 0.0 collective-permute-done.3.refs_1_
  71.0 0.6 collective-permute-start.9
  71.5 1.8 %shard_map.102 = f32[1024,512]{1,0:T(8,128)} custom-call(bf16[1024,256]{1,0:T(8,128)(2,1)S(1)} %get-tuple-element.46.left_ref, bf16[16,16,768]{2,1,0:T(8,128)(2,1)S(1)} %all-to-all-done.recv_ref), custom_call_target="tpu_custom_call" | custom-call | flops 268435456 | bytes 3145728 | tf_op jit(solution)/shard_map/pallas_call | solution.py:371
  73.3 0.0 copy-start.4
  73.3 0.0 all-to-all-done.1.recv_ref
  73.3 0.0 copy-done.2
  73.3 2.1 %shard_map.103 = f32[640,1024]{1,0:T(8,128)} custom-call(bf16[1024,256]{1,0:T(8,128)(2,1)S(1)} %get-tuple-element.30.mask_ref, bf16[16,16,768]{2,1,0:T(8,128)(2,1)S(1)} %all-to-all-done.1.recv_ref, bf16[640,256]{1,0:T(8,128)(2,1)S(1)} %copy-done.2), custom_call_target="tpu_custom_call" | custom-call | flops 335544320 | bytes 3145728 | tf_op jit(solution)/shard_map/pallas_call | solution.py:378
  75.3 0.0 collective-permute-done.4.refs_2_
  75.3 0.0 collective-permute-done.5.refs_3_
  75.4 0.0 collective-permute-done.7.refs_5_
  75.4 6.2 %collective-permute-done.8.refs_6_ = bf16[16,4096]{1,0:T(8,128)(2,1)S(1)} collective-permute-done((bf16[16,4096]{1,0:T(8,128)(2,1)}, bf16[16,4096]{1,0:T(8,128)(2,1)S(1)}, u32[]{:S(2)}, u32[]{:S(2)}) %collective-permute-start.8) | collective-permute-done | bytes 131104 | tf_op jit(solution)/shard_map/ppermute | solution.py:296
  81.5 0.0 collective-permute-done.9.refs_7_
  81.5 0.0 copy-done.4
  81.5 1.2 %shard_map.101 = bf16[16,8192]{1,0:T(8,128)(2,1)} custom-call(bf16[16,16,768]{2,1,0:T(8,128)(2,1)S(1)} %all-to-all-done.1.recv_ref, bf16[16,8192]{1,0:T(8,128)(2,1)S(1)} %copy-done.4, bf16[16,4096]{1,0:T(8,128)(2,1)S(1)} %get-tuple-element.37.refs_0_, bf16[16,4096]{1,0:T(8,128)(2,1)S(1)} %collective-permute-done.3.refs_1_, ...), custom_call_target="tpu_custom_call" | custom-call | bytes 2097152 | tf_op jit(solution)/shard_map/pallas_call | solution.py:386
Async XLA Ops:
  0.6 1.0 %copy-start.1 = (bf16[640,256]{1,0:T(8,128)(2,1)S(1)}, bf16[640,256]{1,0:T(8,128)(2,1)}, u32[]{:S(2)}) copy-start(bf16[640,256]{1,0:T(8,128)(2,1)} %cot_ref.1) | copy-start | bytes 983044
  1.6 4.4 %copy-start = (bf16[640,1024]{1,0:T(8,128)(2,1)S(1)}, bf16[640,1024]{1,0:T(8,128)(2,1)}, u32[]{:S(2)}) copy-start(bf16[640,1024]{1,0:T(8,128)(2,1)} %up_hbm.1) | copy-start | bytes 3932164
  1.6 4.4 %copy-start.3 = (bf16[16,8192]{1,0:T(8,128)(2,1)S(1)}, bf16[16,8192]{1,0:T(8,128)(2,1)}, u32[]{:S(2)}) copy-start(bf16[16,8192]{1,0:T(8,128)(2,1)} %tok_ref.1) | copy-start | bytes 786436
  1.6 4.4 %copy-start.6 = (s32[64]{0:T(128)S(1)}, s32[64]{0:T(128)}, u32[]{:S(2)}) copy-start(s32[64]{0:T(128)} %param.12) | copy-start | bytes 772
  1.6 4.4 %copy-start.7 = (s32[64]{0:T(128)S(1)}, s32[64]{0:T(128)}, u32[]{:S(2)}) copy-start(s32[64]{0:T(128)} %param.13) | copy-start | bytes 772
  5.5 5.6 %collective-permute-start = (bf16[128,4096]{1,0:T(8,128)(2,1)S(1)}, bf16[128,4096]{1,0:T(8,128)(2,1)S(1)}, u32[]{:S(2)}, u32[]{:S(2)}) collective-permute-start(bf16[128,4096]{1,0:T(8,128)(2,1)S(1)} %get-tuple-element.26), channel_id=1, source_target_pairs={{0,1},{1,0},{2,3},{3,2},{4,5},{5,4},{6,7},{7,6},{8,9},{9,8},{10,11... | collective-permute-start | bytes 3145736 | tf_op jit(solution)/shard_map/ppermute | solution.py:296
  11.0 10.3 %collective-permute-start.2 = (bf16[128,4096]{1,0:T(8,128)(2,1)}, bf16[128,4096]{1,0:T(8,128)(2,1)}, u32[]{:S(2)}, u32[]{:S(2)}) collective-permute-start(bf16[128,4096]{1,0:T(8,128)(2,1)} %get-tuple-element.34), channel_id=1, source_target_pairs={{0,1},{1,0},{2,3},{3,2},{4,5},{5,4},{6,7},{7,6},{8,9},{9,8},{10,11... | collective-permute-start | bytes 3145736 | tf_op jit(solution)/shard_map/ppermute | solution.py:296
  11.9 28.2 %all-to-all-start = ((bf16[16,16,768]{2,1,0:T(8,128)(2,1)}), bf16[16,16,768]{2,1,0:T(8,128)(2,1)S(1)}, u32[]{:S(2)}, u32[]{:S(2)}) async-start(bf16[16,16,768]{2,1,0:T(8,128)(2,1)} %get-tuple-element.31), calls=%async_computation | async-start | bytes 786432 | tf_op jit(solution)/shard_map/all_to_all | solution.py:349
  19.4 18.6 %collective-permute-start.1 = (bf16[64,4096]{1,0:T(8,128)(2,1)S(1)}, bf16[64,4096]{1,0:T(8,128)(2,1)S(1)}, u32[]{:S(2)}, u32[]{:S(2)}) collective-permute-start(bf16[64,4096]{1,0:T(8,128)(2,1)S(1)} %get-tuple-element.32), channel_id=1, source_target_pairs={{0,2},{1,3},{2,0},{3,1},{4,6},{5,7},{6,4},{7,5},{8,10},{9,11},{10,... | collective-permute-start | bytes 1572872 | tf_op jit(solution)/shard_map/ppermute | solution.py:296
  40.2 1.2 %copy-start.5 = (bf16[64,16,512]{2,1,0:T(8,128)(2,1)S(1)}, bf16[64,16,512]{2,1,0:T(8,128)(2,1)}, u32[]{:S(2)}) copy-start(bf16[64,16,512]{2,1,0:T(8,128)(2,1)} %param.10) | copy-start | bytes 3145732
  42.9 30.3 %copy-start.2 = (bf16[640,256]{1,0:T(8,128)(2,1)S(1)}, bf16[640,256]{1,0:T(8,128)(2,1)}, u32[]{:S(2)}) copy-start(bf16[640,256]{1,0:T(8,128)(2,1)} %cot_ref.1) | copy-start | bytes 983044
  42.9 30.3 %all-to-all-start.1 = ((bf16[16,16,768]{2,1,0:T(8,128)(2,1)}), bf16[16,16,768]{2,1,0:T(8,128)(2,1)S(1)}, u32[]{:S(2)}, u32[]{:S(2)}) async-start(bf16[16,16,768]{2,1,0:T(8,128)(2,1)} %get-tuple-element.36), calls=%async_computation.1 | async-start | bytes 786432 | tf_op jit(solution)/shard_map/all_to_all | solution.py:370
  47.7 18.6 %collective-permute-start.6 = (bf16[64,4096]{1,0:T(8,128)(2,1)}, bf16[64,4096]{1,0:T(8,128)(2,1)S(1)}, u32[]{:S(2)}, u32[]{:S(2)}) collective-permute-start(bf16[64,4096]{1,0:T(8,128)(2,1)} %get-tuple-element.41), channel_id=1, source_target_pairs={{0,2},{1,3},{2,0},{3,1},{4,6},{5,7},{6,4},{7,5},{8,10},{9,11},{10,... | collective-permute-start | bytes 1572872 | tf_op jit(solution)/shard_map/ppermute | solution.py:296
  49.7 21.3 %collective-permute-start.3 = (bf16[16,4096]{1,0:T(8,128)(2,1)}, bf16[16,4096]{1,0:T(8,128)(2,1)S(1)}, u32[]{:S(2)}, u32[]{:S(2)}) collective-permute-start(bf16[16,4096]{1,0:T(8,128)(2,1)} %get-tuple-element.38), channel_id=1, source_target_pairs={{0,4},{1,5},{2,6},{3,7},{4,0},{5,1},{6,2},{7,3},{8,12},{9,13},{10,... | collective-permute-start | bytes 393224 | tf_op jit(solution)/shard_map/ppermute | solution.py:296
  51.1 24.2 %collective-permute-start.4 = (bf16[16,4096]{1,0:T(8,128)(2,1)}, bf16[16,4096]{1,0:T(8,128)(2,1)S(1)}, u32[]{:S(2)}, u32[]{:S(2)}) collective-permute-start(bf16[16,4096]{1,0:T(8,128)(2,1)} %get-tuple-element.39), channel_id=1, source_target_pairs={{0,8},{1,9},{2,10},{3,11},{4,12},{5,13},{6,14},{7,15},{8,0},{9,1},... | collective-permute-start | bytes 393224 | tf_op jit(solution)/shard_map/ppermute | solution.py:296
  53.5 21.8 %collective-permute-start.5 = (bf16[16,4096]{1,0:T(8,128)(2,1)}, bf16[16,4096]{1,0:T(8,128)(2,1)S(1)}, u32[]{:S(2)}, u32[]{:S(2)}) collective-permute-start(bf16[16,4096]{1,0:T(8,128)(2,1)} %get-tuple-element.40), channel_id=1, source_target_pairs={{0,12},{1,13},{2,14},{3,15},{4,8},{5,9},{6,10},{7,11},{8,4},{9,5},... | collective-permute-start | bytes 393224 | tf_op jit(solution)/shard_map/ppermute | solution.py:296
  67.1 8.2 %collective-permute-start.7 = (bf16[16,4096]{1,0:T(8,128)(2,1)}, bf16[16,4096]{1,0:T(8,128)(2,1)S(1)}, u32[]{:S(2)}, u32[]{:S(2)}) collective-permute-start(bf16[16,4096]{1,0:T(8,128)(2,1)} %get-tuple-element.43), channel_id=1, source_target_pairs={{0,4},{1,5},{2,6},{3,7},{4,0},{5,1},{6,2},{7,3},{8,12},{9,13},{10,... | collective-permute-start | bytes 393224 | tf_op jit(solution)/shard_map/ppermute | solution.py:296
  68.6 12.9 %collective-permute-start.8 = (bf16[16,4096]{1,0:T(8,128)(2,1)}, bf16[16,4096]{1,0:T(8,128)(2,1)S(1)}, u32[]{:S(2)}, u32[]{:S(2)}) collective-permute-start(bf16[16,4096]{1,0:T(8,128)(2,1)} %get-tuple-element.44), channel_id=1, source_target_pairs={{0,8},{1,9},{2,10},{3,11},{4,12},{5,13},{6,14},{7,15},{8,0},{9,1},... | collective-permute-start | bytes 393224 | tf_op jit(solution)/shard_map/ppermute | solution.py:296
  71.0 10.6 %collective-permute-start.9 = (bf16[16,4096]{1,0:T(8,128)(2,1)}, bf16[16,4096]{1,0:T(8,128)(2,1)S(1)}, u32[]{:S(2)}, u32[]{:S(2)}) collective-permute-start(bf16[16,4096]{1,0:T(8,128)(2,1)} %get-tuple-element.45), channel_id=1, source_target_pairs={{0,12},{1,13},{2,14},{3,15},{4,8},{5,9},{6,10},{7,11},{8,4},{9,5},... | collective-permute-start | bytes 393224 | tf_op jit(solution)/shard_map/ppermute | solution.py:296
  73.3 8.3 %copy-start.4 = (bf16[16,8192]{1,0:T(8,128)(2,1)S(1)}, bf16[16,8192]{1,0:T(8,128)(2,1)}, u32[]{:S(2)}) copy-start(bf16[16,8192]{1,0:T(8,128)(2,1)} %tok_ref.1) | copy-start | bytes 786436

commit v4 on v2

--- a/solution.py
+++ b/solution.py
@@ -37,6 +37,13 @@
     for masks in stages:
         order = [o | m for o in order for m in masks]
     return order
+
+
+def came_from(order):
+    came = [0]
+    for masks in stages_of(len(order)):
+        came = [m | c for m in masks for c in came]
+    return came
 
 
 def iota(shape, dim):
@@ -106,31 +113,50 @@
     multiply(cotp_ref[...], wbuf, copies, block, parts)
 
 
-def second_kernel(order, rank, first, block, me_ref, lens_ref, slots_ref, cotp_ref, tok_hbm, up_hbm, weight_hbm, send_ref, *refs):
-    *parts, tokv, up, wbuf, back_rows, sem, sems = refs
-    tp, own, _ = send_ref.shape
-    width = tokv.shape[1]
+def split_rows(x, share):
+    high = x.astype(BF)
+    low = (x - high.astype(F32)).astype(BF)
+    lanes = jnp.concatenate([high, low], axis=1)
+    return [lanes[:, i : i + share] for i in range(0, lanes.shape[1], share)]
+
+
+def join_rows(ref, first, rank, tokens):
+    share = ref.shape[1]
+    pieces = [ref[first + i * rank : first + (i + 1) * rank].astype(F32) for i in range(2 * tokens // share)]
+    lanes = jnp.concatenate(pieces, axis=1) if len(pieces) > 1 else pieces[0]
+    return lanes[:, :tokens] + lanes[:, tokens:]
+
+
+def put_rows(ref, first, x):
+    for i, piece in enumerate(split_rows(x, ref.shape[1])):
+        ref[first + i * piece.shape[0] : first + (i + 1) * piece.shape[0]] = piece
+
+
+def adapter_kernel(order, rank, me_ref, lens_ref, slots_ref, cotp_ref, tok_ref, up_ref, mask_ref, sum_ref, keep_ref, send_ref, normed_ref, back_rows):
+    own, width = tok_ref.shape
+    tp = len(order)
     share = width // tp
     rows = cotp_ref.shape[0]
-    tok_copy = pltpu.make_async_copy(tok_hbm, tokv, sem.at[0])
-    tok_copy.start()
-    up_copy = pltpu.make_async_copy(up_hbm, up, sem.at[1])
-    up_copy.start()
-    copies = fetch_weight(weight_hbm, wbuf, sems, first, block)
-    for copy in copies:
-        copy.start()
+    me = me_ref[0]
+    tok = tok_ref[...].astype(F32)
+    inv = lax.rsqrt(jnp.mean(tok * tok, axis=1, keepdims=True) + EPS)
+    normed_ref[...] = (tok * inv).astype(BF)
+    half = len(order) // 2
+    for i, mask_bits in enumerate(order):
+        block = normed_ref[:, pl.ds(pl.multiple_of((me ^ mask_bits) * share, share), share)]
+        if i < half:
+            keep_ref[i * own : (i + 1) * own] = block
+        else:
+            send_ref[(i - half) * own : (i - half + 1) * own] = block
     member, match = membership(lens_ref, slots_ref, rows)
+    slots = match.shape[0]
+    chosen = lax.dot_general(match, member, NT, preferred_element_type=F32).astype(BF)
+    tall = (iota((slots * rank, slots), 0) // rank == iota((slots * rank, slots), 1)).astype(F32).astype(BF)
+    mask_ref[...] = jnp.dot(tall, chosen, preferred_element_type=F32).astype(BF)
     chosen = lax.dot_general(member, match, NT, preferred_element_type=F32).astype(BF)
-    slots = match.shape[0]
     wide = (iota((slots, slots * rank), 1) // rank == iota((slots, slots * rank), 0)).astype(F32).astype(BF)
     mask = jnp.dot(chosen, wide, preferred_element_type=F32)
-    me = me_ref[0]
-    tok_copy.wait()
-    tok = tokv[...].astype(F32)
-    inv = lax.rsqrt(jnp.mean(tok * tok, axis=1, keepdims=True) + EPS)
-    normed = (tok * inv).astype(BF)
-    up_copy.wait()
-    every = jnp.dot(cotp_ref[...], up[...], preferred_element_type=F32)
+    every = jnp.dot(cotp_ref[...], up_ref[...], preferred_element_type=F32)
     for i, mask_bits in enumerate(order):
         target = pl.multiple_of((me ^ mask_bits) * own, own)
         back_rows[pl.ds(target, own), :] = every[i * own : (i + 1) * own]
@@ -142,11 +168,37 @@
     back = turned[:rank]
     for i in range(1, 128 // rank):
         back = back + turned[i * rank : (i + 1) * rank]
-    back = back.astype(BF)
-    for q in range(tp):
-        send_ref[q, :, :share] = normed[:, q * share : (q + 1) * share]
-        send_ref[q, :, share:] = back
+    sum_ref[...] = back
+    put_rows(send_ref, half * own, back)
+
+
+def second_kernel(first, block, cotp_ref, weight_hbm, *refs):
+    *parts, wbuf, sems = refs
+    copies = fetch_weight(weight_hbm, wbuf, sems, first, block)
+    for copy in copies:
+        copy.start()
     multiply(cotp_ref[...], wbuf, copies, block, parts)
+
+
+def turn_kernel(sources, cuts, sum_in, keep_in, *refs):
+    n_in = len(refs) - 1 - cuts
+    got, sum_out, outs = refs[:n_in], refs[n_in], refs[n_in + 1 :]
+    rank, tokens = sum_in.shape
+    rows = keep_in.shape[0]
+    total = sum_in[...]
+    for g in got:
+        total = total + join_rows(g, rows, rank, tokens)
+    sum_out[...] = total
+    per = rows // sources
+    each = per // cuts
+    for c in range(cuts):
+        at = 0
+        for piece in (keep_in,) + tuple(got):
+            for k in range(sources):
+                outs[c][at : at + each] = piece[k * per + c * each : k * per + (c + 1) * each]
+                at += each
+        if c:
+            put_rows(outs[c], at, total)
 
 
 def total_of(refs, i, each):
@@ -167,48 +219,73 @@
         at, to = at + n, to + m
 
 
-def middle_kernel(rank, lens_ref, slots_ref, recv_ref, down_ref, send_ref, left_ref):
-    tp, own, wide = recv_ref.shape
-    rows = tp * own
-    share = wide - rows
-    mask = mask_by_column(lens_ref, slots_ref, rows, rank)
-    normed = recv_ref[:, :, :share].reshape(rows, share)
-    every = lax.dot_general(down_ref[...], normed, NT, preferred_element_type=F32) * mask
-    slots = every.shape[0] // rank
-    low = jnp.sum(every.reshape(slots, rank, rows), axis=0).astype(BF)
-    back = jnp.sum(recv_ref[:, :, share:].astype(F32), axis=0).astype(BF).astype(F32)
+def middle_kernel(rank, order, me_ref, mask_ref, down_ref, sum_in, keep_in, *refs):
+    *got, left_ref, normed_ref, sum_ref, keep_ref, send_ref, term_ref = refs
+    rows, share = normed_ref.shape
+    tp = len(order)
+    own = rows // tp
+    me = me_ref[0]
+    per = keep_in.shape[0]
+    back = sum_in[...]
+    for g in got:
+        back = back + join_rows(g, per, rank, rows)
+    at = 0
+    came = came_from(order)
+    for piece in (keep_in,) + tuple(got):
+        for k in range(per // own):
+            target = pl.multiple_of((me ^ came[at]) * own, own)
+            normed_ref[pl.ds(target, own), :] = piece[k * own : (k + 1) * own]
+            at += 1
+    mask = mask_ref[...].astype(F32)
+    slots = mask.shape[0] // rank
+    back = back.astype(BF).astype(F32)
     left = (mask.reshape(slots, rank, rows) * back[None]).reshape(slots * rank, rows).astype(BF)
     left_ref[...] = left
-    term = SCALE * lax.dot_general(left, down_ref[...], TN, preferred_element_type=F32)
-    send_ref[:, :, :share] = term.astype(BF).reshape(tp, own, share)
-    for q in range(tp):
-        send_ref[q, :, share:] = low
-
-
-def down_kernel(left_ref, recv_ref, out_ref):
-    tp, own, wide = recv_ref.shape
-    rows = tp * own
-    share = wide - rows
-    normed = recv_ref[:, :, :share].reshape(rows, share)
-    out_ref[...] = SCALE * jnp.dot(left_ref[...], normed, preferred_element_type=F32)
-
-
-def up_kernel(rank, lens_ref, slots_ref, recv_ref, cot_ref, out_ref):
-    tp, own, wide = recv_ref.shape
-    rows = tp * own
-    share = wide - rows
-    mask = mask_by_column(lens_ref, slots_ref, rows, rank)
+    every = lax.dot_general(down_ref[...], normed_ref[...], NT, preferred_element_type=F32) * mask
+    low = jnp.sum(every.reshape(slots, rank, rows), axis=0)
+    sum_ref[...] = low
+    term_ref[...] = (SCALE * lax.dot_general(left, down_ref[...], TN, preferred_element_type=F32)).astype(BF)
+    half = tp // 2
+    for i, mask_bits in enumerate(order):
+        block = term_ref[pl.ds(pl.multiple_of((me ^ mask_bits) * own, own), own), :]
+        if i < half:
+            keep_ref[i * own : (i + 1) * own] = block
+        else:
+            send_ref[(i - half) * own : (i - half + 1) * own] = block
+    put_rows(send_ref, half * own, low)
+
+
+def down_kernel(left_ref, normed_ref, out_ref):
+    out_ref[...] = SCALE * jnp.dot(left_ref[...], normed_ref[...], preferred_element_type=F32)
+
+
+def up_kernel(rank, rows_of_piece, mask_ref, cot_ref, sum_in, *refs):
+    *got, out_ref = refs
+    low = sum_in[...]
+    for g in got:
+        low = low + join_rows(g, rows_of_piece, rank, low.shape[1])
+    low = low.astype(BF).astype(F32)
+    mask = mask_ref[...].astype(F32)
     slots = mask.shape[0] // rank
-    low = jnp.sum(recv_ref[:, :, share:].astype(F32), axis=0).astype(BF).astype(F32)
+    rows = mask.shape[1]
     left = (mask.reshape(slots, rank, rows) * low[None]).reshape(slots * rank, rows).astype(BF)
     out_ref[...] = SCALE * lax.dot_general(cot_ref[...], left, NT, preferred_element_type=F32)
 
 
-def final_kernel(pieces, recv_ref, tok_ref, *refs):
-    out_ref = refs[-1]
-    tp, own, _ = recv_ref.shape
-    width = tok_ref.shape[1]
-    share = width // tp
+def final_kernel(pieces, order, me_ref, tok_ref, keep_in, *refs):
+    *refs, out_ref, term_ref = refs
+    own, width = tok_ref.shape
+    share = width // len(order)
+    me = me_ref[0]
+    n_got = len(refs) - sum(pieces)
+    got, refs = refs[:n_got], refs[n_got:]
+    came = came_from(order)
+    at = 0
+    for piece in (keep_in,) + tuple(got):
+        for k in range(keep_in.shape[0] // own):
+            target = pl.multiple_of((me ^ came[at]) * share, share)
+            term_ref[:, pl.ds(target, share)] = piece[k * own : (k + 1) * own].astype(F32)
+            at += 1
     chunks = []
     at = 0
     for n in pieces:
@@ -217,8 +294,7 @@
             total = total + r[...].astype(F32)
         at += n
         chunks.append(total)
-    term = jnp.concatenate([recv_ref[q, :, :share].astype(F32) for q in range(tp)], axis=1)
-    grad = jnp.concatenate(chunks, axis=1) + term
+    grad = jnp.concatenate(chunks, axis=1) + term_ref[...]
     tok = tok_ref[...].astype(F32)
     inv = lax.rsqrt(jnp.mean(tok * tok, axis=1, keepdims=True) + EPS)
     normed = tok * inv
@@ -306,28 +382,52 @@
             at += c
         return cut, list(res[at:])
 
-    send, *parts_b = call(
-        functools.partial(second_kernel, order, rank, half, block),
-        [shape((tp, own, share + rows))] + [shape((each, half))] * m,
-        [SMEM, VMEM, VMEM, VMEM, HBM, HBM, HBM],
-        scratch=[
-            pltpu.VMEM((own, width), BF),
-            pltpu.VMEM((columns, count * rank), BF),
-            pltpu.VMEM((columns, half), BF),
-            pltpu.VMEM((rows, count * rank), F32),
-            dma((2,)),
-            dma((half // block,)),
+    extra = 2 * rows * rank // share
+    mask, partial, keep, gift = call(
+        functools.partial(adapter_kernel, order, rank),
+        [
+            shape((count * rank, rows)),
+            shape((rank, rows), F32),
+            shape((rows // 2, share)),
+            shape((rows // 2 + extra, share)),
         ],
-        out_specs=[VMEM] * (1 + m),
-        flops=2 * rows * columns * (half + count * rank),
-        nbytes=2 * columns * (half + count * rank),
-    )(me, lens, slot, cotp, tokens, up_maps, weight)
+        [SMEM, VMEM, VMEM, VMEM, VMEM, VMEM],
+        scratch=[pltpu.VMEM((own, width), BF), pltpu.VMEM((rows, count * rank), F32)],
+        flops=2 * rows * columns * count * rank,
+        nbytes=2 * columns * count * rank,
+    )(me, lens, slot, cotp, tokens, up_maps)
+    *parts_b, = call(
+        functools.partial(second_kernel, half, block),
+        [shape((each, half))] * m,
+        [VMEM, HBM],
+        scratch=[pltpu.VMEM((columns, half), BF), dma((half // block,))],
+        flops=2 * rows * columns * half,
+        nbytes=2 * columns * half,
+    )(cotp, weight)
+
+    def shuffled(partial, keep, gift):
+        parts = [gift]
+        for stage in range(len(stages)):
+            got = [lax.ppermute(g, "tp", pairs(k)) for k, g in zip(stages[stage][1:], parts)]
+            if stage == len(stages) - 1:
+                return partial, keep, got
+            sources = 1
+            for masks in stages[:stage]:
+                sources *= len(masks)
+            cuts = len(stages[stage + 1])
+            size = keep.shape[0] * len(stages[stage]) // cuts
+            partial, keep, *parts = call(
+                functools.partial(turn_kernel, sources, cuts),
+                [shape((rank, rows), F32), shape((size, share))] + [shape((size + extra, share))] * (cuts - 1),
+                [VMEM] * (2 + len(got)),
+                nbytes=4 * keep.size * 4,
+            )(partial, keep, *got)
 
     last = len(stages) - 1
     held_a = exchange(0, parts_a)
+    partial, keep, got = shuffled(partial, keep, gift)
     held_b = exchange(0, parts_b)
-    (cut_a,), (send,) = summed([held_a], [1], [send])
-    recv = lax.all_to_all(send, "tp", split_axis=0, concat_axis=0, tiled=True)
+    (cut_a,), _ = summed([held_a], [1])
     for stage in range(1, last + 1):
         held_a = exchange(stage, cut_a)
         if stage < last:
@@ -337,35 +437,43 @@
         held_b = exchange(stage, cut_b)
     chunks = [held_a, held_b]
 
-    send2, left = call(
-        functools.partial(middle_kernel, rank),
-        (shape((tp, own, share + rows)), shape((count * rank, rows))),
-        [VMEM] * 4,
+    left, normed, partial, keep, gift = call(
+        functools.partial(middle_kernel, rank, order),
+        [
+            shape((count * rank, rows)),
+            shape((rows, share)),
+            shape((rank, rows), F32),
+            shape((rows // 2, share)),
+            shape((rows // 2 + extra, share)),
+        ],
+        [SMEM] + [VMEM] * (4 + len(got)),
+        scratch=[pltpu.VMEM((rows, share), BF)],
         flops=4 * rows * share * count * rank,
         nbytes=3 << 20,
-    )(lens, slot, recv, down_flat)
-    recv2 = lax.all_to_all(send2, "tp", split_axis=0, concat_axis=0, tiled=True)
+    )(me, mask, down_flat, partial, keep, *got)
     down_grad = call(
         down_kernel,
         shape((count * rank, share), F32),
         [VMEM] * 2,
         flops=2 * rows * share * count * rank,
         nbytes=3 << 20,
-    )(left, recv)
+    )(left, normed)
+    partial, keep, got = shuffled(partial, keep, gift)
     up_grad = call(
-        functools.partial(up_kernel, rank),
+        functools.partial(up_kernel, rank, keep.shape[0]),
         shape((columns, count * rank), F32),
-        [VMEM] * 4,
+        [VMEM] * (3 + len(got)),
         flops=2 * rows * columns * count * rank,
         nbytes=3 << 20,
-    )(lens, slot, recv2, cotangent)
+    )(mask, cotangent, partial, *got)
     flat = [piece for chunk in chunks for piece in chunk]
     grad_tokens = call(
-        functools.partial(final_kernel, [len(c) for c in chunks]),
+        functools.partial(final_kernel, [len(c) for c in chunks], order),
         shape((own, width)),
-        [VMEM] * (2 + len(flat)),
+        [SMEM] + [VMEM] * (2 + len(got) + len(flat)),
+        scratch=[pltpu.VMEM((own, width), F32)],
         nbytes=2 << 20,
-    )(recv2, tokens, *flat)
+    )(me, tokens, keep, *got, *flat)
     return grad_tokens, down_grad.reshape(count, rank, share), up_grad
 
 

time: 75.7 us -> 80.4 us (1.062)
  waiting for transfers between devices: 26.3 us -> 39 us
  local copies, waits for them, and re-layouts: 5.72 us -> 1 us
  Pallas kernels: 18.1 us -> 15.4 us
    ppermute x0 -> x10, waiting for transfers between devices: none -> 22.5 us  [shuffled(): lax.ppermute(g, 'tp', pairs(k))]
    ppermute x0 -> x10, starting transfers between devices: none -> 11.6 us  [shuffled(): lax.ppermute(g, 'tp', pairs(k))]
    all_to_all x2 -> x0, starting transfers between devices: 10.9 us -> none  [the longest x1 7.37 us: body(): recv = lax.all_to_all(send, 'tp', split_axis=0, concat_axis=0, tiled=True)]
    all_to_all x2 -> x0, waiting for transfers between devices: 10.3 us -> none  [the longest x1 10.3 us: body(): recv = lax.all_to_all(send, 'tp', split_axis=0, concat_axis=0, tiled=True)]
    unnamed x24 -> x14, local copies, waits for them, and re-layouts: 5.72 us -> 1 us
    pallas_call x4 -> x9, Pallas kernels: 10.7 us -> 9.21 us  [the longest x1 3.7 us: body(): call(functools.partial(second_kernel, half, block), [shape((each, half))]...]
    pallas_call x3, Pallas kernels: 1.81 us -> 0.72 us  [summed(): call(functools.partial(sum_kernel, [(len(g), c) for g, c in zip(groups, c...]
    ppermute x10, starting transfers between devices: 13.5 us -> 12.5 us  [exchange(): lax.ppermute(part, 'tp', pairs(m))]
  transfers between devices with their start and end apart: 12 -> 20, of which waited for: 3 -> 11; matrix products, arithmetic and copies ran while one was open for 0% -> 0% of each run, Pallas kernels for 17% -> 13%
where the time goes in v4:
time: 80.4 us; the launch traced here: 80.3 us
  waiting for transfers between devices  39 us (49%)
  starting transfers between devices  24 us (30%)
  Pallas kernels  15.4 us (19%)
  local copies, waits for them, and re-layouts  1 us (1%)
    ppermute x10, waiting for transfers between devices, shuffled(): lax.ppermute(g, 'tp', pairs(k))  22.5 us
    ppermute x10, waiting for transfers between devices, exchange(): lax.ppermute(part, 'tp', pairs(m))  16.5 us
    ppermute x10, starting transfers between devices, exchange(): lax.ppermute(part, 'tp', pairs(m))  12.5 us
    ppermute x10, starting transfers between devices, shuffled(): lax.ppermute(g, 'tp', pairs(k))  11.6 us
    pallas_call x1, Pallas kernels, body(): call(functools.partial(first_kernel, order, own, block), [shape((rows, co...  3.77 us
    pallas_call x1, Pallas kernels, body(): call(functools.partial(second_kernel, half, block), [shape((each, half))]...  3.7 us
    pallas_call x1, Pallas kernels, body(): call(functools.partial(up_kernel, rank, keep.shape[0]), shape((columns, c...  2.05 us
    pallas_call x1, Pallas kernels, body(): call(down_kernel, shape((count * rank, share), F32), [VMEM] * 2, flops=2...  1.75 us
  transfers between devices with their start and end apart: 20, of which 11 were waited for; matrix products, arithmetic and copies ran while one was open for 0% of the time, Pallas kernels for 13%

profile of v4, /device:TPU:0, one launch (start us, length us, event | category | flops | bytes accessed | tf_op | source)
XLA Modules:
  0.0 80.3 jit_solution(14352372800185275446)
XLA Ops:
  0.6 0.0 copy-start
  0.6 1.0 %copy-done = bf16[640,256]{1,0:T(8,128)(2,1)S(1)} copy-done((bf16[640,256]{1,0:T(8,128)(2,1)S(1)}, bf16[640,256]{1,0:T(8,128)(2,1)}, u32[]{:S(2)}) %copy-start) | copy-done | bytes 327704
  1.6 3.8 %shard_map.94 = (bf16[256,640]{1,0:T(8,128)(2,1)S(1)}, bf16[128,4096]{1,0:T(8,128)(2,1)S(1)}, bf16[128,4096]{1,0:T(8,128)(2,1)S(1)}) custom-call(s32[1]{0:T(128)} %bitcast.me_ref, bf16[640,256]{1,0:T(8,128)(2,1)S(1)} %copy-done, bf16[640,8192]{1,0:T(8,128)(2,1)} %weight_hbm.3), custom_call_target="tpu_custom_call" | custom-call | flops 1342177280 | bytes 5242880 | tf_op jit(solution)/shard_map/pallas_call | solution.py:343
  5.4 0.5 collective-permute-start.10
  5.9 0.0 copy-start.3
  5.9 0.0 copy-start.4
  5.9 0.0 copy-start.5
  5.9 3.7 %shard_map.102 = (bf16[128,4096]{1,0:T(8,128)(2,1)S(1)}, bf16[128,4096]{1,0:T(8,128)(2,1)S(1)}) custom-call(bf16[256,640]{1,0:T(8,128)(2,1)S(1)} %get-tuple-element.45.cotp_ref, bf16[640,8192]{1,0:T(8,128)(2,1)} %weight_hbm.3), custom_call_target="tpu_custom_call" | custom-call | flops 1342177280 | bytes 5242880 | tf_op jit(solution)/shard_map/pallas_call | solution.py:399
  9.6 0.0 copy-start.2
  9.6 0.1 collective-permute-start.12
  9.8 0.0 collective-permute-done.10.refs_1_
  9.8 0.2 shard_map.101
  10.0 3.0 %collective-permute-start.11 = (bf16[64,4096]{1,0:T(8,128)(2,1)S(1)}, bf16[64,4096]{1,0:T(8,128)(2,1)S(1)}, u32[]{:S(2)}, u32[]{:S(2)}) collective-permute-start(bf16[64,4096]{1,0:T(8,128)(2,1)S(1)} %get-tuple-element.71), channel_id=1, source_target_pairs={{0,2},{1,3},{2,0},{3,1},{4,6},{5,7},{6,4},{7,5},{8,10},{9,11},{10,... | collective-permute-start | bytes 1572872 | tf_op jit(solution)/shard_map/ppermute | solution.py:362
  13.0 0.0 copy-done.3
  13.0 0.0 copy-done.4
  13.0 0.0 copy-done.5
  13.0 0.0 copy-done.2
  13.0 0.0 copy-start.6
  13.1 1.4 %shard_map.95 = (bf16[1024,256]{1,0:T(8,128)(2,1)S(1)}, f32[16,256]{1,0:T(8,128)S(1)}, bf16[128,512]{1,0:T(8,128)(2,1)S(1)}, bf16[144,512]{1,0:T(8,128)(2,1)S(1)}) custom-call(s32[1]{0:T(128)} %bitcast.me_ref, s32[1,64]{1,0:T(1,128)S(1)} %bitcast.5, s32[1,64]{1,0:T(1,128)S(1)} %bitcast.6, bf16[256,640]{1,0:T(8,128)(2,1)S(1)} %get-tuple-element.45.cotp_ref, ...), custom_call_target="tpu_custom_call" | custom-call | flops 335544320 | bytes 1310720 | tf_op jit(solution)/shard_map/pallas_call | solution.py:386
  14.5 0.1 collective-permute-start
  14.6 1.4 %collective-permute-done.refs_0_ = bf16[144,512]{1,0:T(8,128)(2,1)S(1)} collective-permute-done((bf16[144,512]{1,0:T(8,128)(2,1)S(1)}, bf16[144,512]{1,0:T(8,128)(2,1)S(1)}, u32[]{:S(2)}, u32[]{:S(2)}) %collective-permute-start) | collective-permute-done | bytes 147488 | tf_op jit(solution)/shard_map/ppermute | solution.py:411
  15.9 0.6 collective-permute-start.1
  16.6 0.0 collective-permute-done.12.refs_3_
  16.6 9.2 %collective-permute-done.11.refs_1_ = bf16[64,4096]{1,0:T(8,128)(2,1)S(1)} collective-permute-done((bf16[64,4096]{1,0:T(8,128)(2,1)S(1)}, bf16[64,4096]{1,0:T(8,128)(2,1)S(1)}, u32[]{:S(2)}, u32[]{:S(2)}) %collective-permute-start.11) | collective-permute-done | bytes 524320 | tf_op jit(solution)/shard_map/ppermute | solution.py:362
  25.8 0.4 shard_map.103
  26.1 2.1 %collective-permute-start.16 = (bf16[64,4096]{1,0:T(8,128)(2,1)S(1)}, bf16[64,4096]{1,0:T(8,128)(2,1)S(1)}, u32[]{:S(2)}, u32[]{:S(2)}) collective-permute-start(bf16[64,4096]{1,0:T(8,128)(2,1)S(1)} %get-tuple-element.79), channel_id=1, source_target_pairs={{0,2},{1,3},{2,0},{3,1},{4,6},{5,7},{6,4},{7,5},{8,10},{9,11},{10,... | collective-permute-start | bytes 1572872 | tf_op jit(solution)/shard_map/ppermute | solution.py:362
  28.2 0.7 collective-permute-done.1.refs_0_
  29.0 2.2 %collective-permute-start.2 = (bf16[80,512]{1,0:T(8,128)(2,1)S(1)}, bf16[80,512]{1,0:T(8,128)(2,1)S(1)}, u32[]{:S(2)}, u32[]{:S(2)}) collective-permute-start(bf16[80,512]{1,0:T(8,128)(2,1)S(1)} %get-tuple-element.55), channel_id=1, source_target_pairs={{0,4},{1,5},{2,6},{3,7},{4,0},{5,1},{6,2},{7,3},{8,12},{9,13},{10,... | collective-permute-start | bytes 245768 | tf_op jit(solution)/shard_map/ppermute | solution.py:411
  31.1 2.6 %collective-permute-start.3 = (bf16[80,512]{1,0:T(8,128)(2,1)S(1)}, bf16[80,512]{1,0:T(8,128)(2,1)S(1)}, u32[]{:S(2)}, u32[]{:S(2)}) collective-permute-start(bf16[80,512]{1,0:T(8,128)(2,1)S(1)} %get-tuple-element.56), channel_id=1, source_target_pairs={{0,8},{1,9},{2,10},{3,11},{4,12},{5,13},{6,14},{7,15},{8,0},{9,1},... | collective-permute-start | bytes 245768 | tf_op jit(solution)/shard_map/ppermute | solution.py:411
  33.7 0.0 collective-permute-start.4
  33.7 0.6 collective-permute-done.2.refs_0_
  34.3 3.9 %collective-permute-done.3.refs_1_ = bf16[80,512]{1,0:T(8,128)(2,1)S(1)} collective-permute-done((bf16[80,512]{1,0:T(8,128)(2,1)S(1)}, bf16[80,512]{1,0:T(8,128)(2,1)S(1)}, u32[]{:S(2)}, u32[]{:S(2)}) %collective-permute-start.3) | collective-permute-done | bytes 81952 | tf_op jit(solution)/shard_map/ppermute | solution.py:411
  38.2 1.8 %collective-permute-done.4.refs_2_ = bf16[80,512]{1,0:T(8,128)(2,1)S(1)} collective-permute-done((bf16[80,512]{1,0:T(8,128)(2,1)S(1)}, bf16[80,512]{1,0:T(8,128)(2,1)S(1)}, u32[]{:S(2)}, u32[]{:S(2)}) %collective-permute-start.4) | collective-permute-done | bytes 81952 | tf_op jit(solution)/shard_map/ppermute | solution.py:411
  40.0 0.0 copy-done.6
  40.0 0.8 shard_map.98
  40.8 0.0 copy-start.1
  40.8 0.1 collective-permute-start.5
  40.9 1.4 %collective-permute-done.5.refs_0_ = bf16[144,512]{1,0:T(8,128)(2,1)S(1)} collective-permute-done((bf16[144,512]{1,0:T(8,128)(2,1)S(1)}, bf16[144,512]{1,0:T(8,128)(2,1)S(1)}, u32[]{:S(2)}, u32[]{:S(2)}) %collective-permute-start.5) | collective-permute-done | bytes 147488 | tf_op jit(solution)/shard_map/ppermute | solution.py:411
  42.2 1.6 %collective-permute-start.6 = (bf16[144,512]{1,0:T(8,128)(2,1)S(1)}, bf16[144,512]{1,0:T(8,128)(2,1)S(1)}, u32[]{:S(2)}, u32[]{:S(2)}) collective-permute-start(bf16[144,512]{1,0:T(8,128)(2,1)S(1)} %get-tuple-element.63), channel_id=1, source_target_pairs={{0,2},{1,3},{2,0},{3,1},{4,6},{5,7},{6,4},{7,5},{8,10},{9,11},{10,... | collective-permute-start | bytes 442376 | tf_op jit(solution)/shard_map/ppermute | solution.py:411
  43.8 0.0 collective-permute-start.13
  43.8 4.4 %collective-permute-done.6.refs_0_ = bf16[144,512]{1,0:T(8,128)(2,1)S(1)} collective-permute-done((bf16[144,512]{1,0:T(8,128)(2,1)S(1)}, bf16[144,512]{1,0:T(8,128)(2,1)S(1)}, u32[]{:S(2)}, u32[]{:S(2)}) %collective-permute-start.6) | collective-permute-done | bytes 147488 | tf_op jit(solution)/shard_map/ppermute | solution.py:411
  48.2 0.1 collective-permute-start.7
  48.3 1.9 %collective-permute-start.8 = (bf16[80,512]{1,0:T(8,128)(2,1)S(1)}, bf16[80,512]{1,0:T(8,128)(2,1)S(1)}, u32[]{:S(2)}, u32[]{:S(2)}) collective-permute-start(bf16[80,512]{1,0:T(8,128)(2,1)S(1)} %get-tuple-element.66), channel_id=1, source_target_pairs={{0,8},{1,9},{2,10},{3,11},{4,12},{5,13},{6,14},{7,15},{8,0},{9,1},... | collective-permute-start | bytes 245768 | tf_op jit(solution)/shard_map/ppermute | solution.py:411
  50.2 2.5 %collective-permute-start.9 = (bf16[80,512]{1,0:T(8,128)(2,1)S(1)}, bf16[80,512]{1,0:T(8,128)(2,1)S(1)}, u32[]{:S(2)}, u32[]{:S(2)}) collective-permute-start(bf16[80,512]{1,0:T(8,128)(2,1)S(1)} %get-tuple-element.67), channel_id=1, source_target_pairs={{0,12},{1,13},{2,14},{3,15},{4,8},{5,9},{6,10},{7,11},{8,4},{9,5},... | collective-permute-start | bytes 245768 | tf_op jit(solution)/shard_map/ppermute | solution.py:411
  52.7 0.0 collective-permute-done.16.refs_1_
  52.7 0.4 collective-permute-start.14
  53.1 0.1 shard_map.104
  53.2 0.0 collective-permute-done.7.refs_0_
  53.3 1.3 %collective-permute-start.15 = (bf16[16,4096]{1,0:T(8,128)(2,1)S(1)}, bf16[16,4096]{1,0:T(8,128)(2,1)S(1)}, u32[]{:S(2)}, u32[]{:S(2)}) collective-permute-start(bf16[16,4096]{1,0:T(8,128)(2,1)S(1)} %get-tuple-element.77), channel_id=1, source_target_pairs={{0,12},{1,13},{2,14},{3,15},{4,8},{5,9},{6,10},{7,11},{8,4},{9,5},... | collective-permute-start | bytes 393224 | tf_op jit(solution)/shard_map/ppermute | solution.py:362
  54.6 8.5 %collective-permute-done.8.refs_1_ = bf16[80,512]{1,0:T(8,128)(2,1)S(1)} collective-permute-done((bf16[80,512]{1,0:T(8,128)(2,1)S(1)}, bf16[80,512]{1,0:T(8,128)(2,1)S(1)}, u32[]{:S(2)}, u32[]{:S(2)}) %collective-permute-start.8) | collective-permute-done | bytes 81952 | tf_op jit(solution)/shard_map/ppermute | solution.py:411
  63.0 0.0 collective-permute-start.17
  63.0 0.0 collective-permute-done.9.refs_2_
  63.1 3.4 %collective-permute-start.18 = (bf16[16,4096]{1,0:T(8,128)(2,1)S(1)}, bf16[16,4096]{1,0:T(8,128)(2,1)S(1)}, u32[]{:S(2)}, u32[]{:S(2)}) collective-permute-start(bf16[16,4096]{1,0:T(8,128)(2,1)S(1)} %get-tuple-element.82), channel_id=1, source_target_pairs={{0,8},{1,9},{2,10},{3,11},{4,12},{5,13},{6,14},{7,15},{8,0},{9,1},... | collective-permute-start | bytes 393224 | tf_op jit(solution)/shard_map/ppermute | solution.py:362
  66.5 0.0 collective-permute-done.13.refs_4_
  66.5 1.5 %collective-permute-start.19 = (bf16[16,4096]{1,0:T(8,128)(2,1)S(1)}, bf16[16,4096]{1,0:T(8,128)(2,1)S(1)}, u32[]{:S(2)}, u32[]{:S(2)}) collective-permute-start(bf16[16,4096]{1,0:T(8,128)(2,1)S(1)} %get-tuple-element.83), channel_id=1, source_target_pairs={{0,12},{1,13},{2,14},{3,15},{4,8},{5,9},{6,10},{7,11},{8,4},{9,5},... | collective-permute-start | bytes 393224 | tf_op jit(solution)/shard_map/ppermute | solution.py:362
  68.0 1.7 %shard_map.106 = f32[1024,512]{1,0:T(8,128)} custom-call(bf16[1024,256]{1,0:T(8,128)(2,1)S(1)} %get-tuple-element.84.left_ref, bf16[256,512]{1,0:T(8,128)(2,1)S(1)} %get-tuple-element.85.normed_ref), custom_call_target="tpu_custom_call" | custom-call | flops 268435456 | bytes 3145728 | tf_op jit(solution)/shard_map/pallas_call | solution.py:454
  69.7 0.0 copy-done.1
  69.7 2.1 %shard_map.107 = f32[640,1024]{1,0:T(8,128)} custom-call(bf16[1024,256]{1,0:T(8,128)(2,1)S(1)} %get-tuple-element.46.mask_ref, bf16[640,256]{1,0:T(8,128)(2,1)S(1)} %copy-done.1, f32[16,256]{1,0:T(8,128)S(1)} %get-tuple-element.86.sum_in, bf16[80,512]{1,0:T(8,128)(2,1)S(1)} %collective-permute-done.7.refs_0_, ...), custom_call_target="tpu_custom_call" | custom-call | flops 335544320 | bytes 3145728 | tf_op jit(solution)/shard_map/pallas_call | solution.py:462
  71.8 1.7 %collective-permute-done.14.refs_5_ = bf16[16,4096]{1,0:T(8,128)(2,1)S(1)} collective-permute-done((bf16[16,4096]{1,0:T(8,128)(2,1)S(1)}, bf16[16,4096]{1,0:T(8,128)(2,1)S(1)}, u32[]{:S(2)}, u32[]{:S(2)}) %collective-permute-start.14) | collective-permute-done | bytes 131104 | tf_op jit(solution)/shard_map/ppermute | solution.py:362
  73.5 0.0 collective-permute-done.15.refs_6_
  73.5 0.0 collective-permute-done.17.refs_8_
  73.5 5.6 %collective-permute-done.18.refs_9_ = bf16[16,4096]{1,0:T(8,128)(2,1)S(1)} collective-permute-done((bf16[16,4096]{1,0:T(8,128)(2,1)S(1)}, bf16[16,4096]{1,0:T(8,128)(2,1)S(1)}, u32[]{:S(2)}, u32[]{:S(2)}) %collective-permute-start.18) | collective-permute-done | bytes 131104 | tf_op jit(solution)/shard_map/ppermute | solution.py:362
  79.1 0.0 collective-permute-done.19.refs_10_
  79.1 1.2 %shard_map.105 = bf16[16,8192]{1,0:T(8,128)(2,1)} custom-call(s32[1]{0:T(128)} %bitcast.me_ref, bf16[16,8192]{1,0:T(8,128)(2,1)S(1)} %copy-done.3, bf16[64,512]{1,0:T(8,128)(2,1)S(1)} %get-tuple-element.64.keep_in, bf16[80,512]{1,0:T(8,128)(2,1)S(1)} %collective-permute-done.7.refs_0_, bf16[80,512]{1,0:T(8,128)(2,1)S(1)} %collective-permute-done.8.refs_1_, ...), custom_call_target="tpu_custom_call" | custom-call | bytes 2097152 | tf_op jit(solution)/shard_map/pallas_call | solution.py:470
  (4 shorter events, 0.1 us)
Async XLA Ops:
  0.6 1.0 %copy-start = (bf16[640,256]{1,0:T(8,128)(2,1)S(1)}, bf16[640,256]{1,0:T(8,128)(2,1)}, u32[]{:S(2)}) copy-start(bf16[640,256]{1,0:T(8,128)(2,1)} %cot_ref.1) | copy-start | bytes 983044
  5.4 4.4 %collective-permute-start.10 = (bf16[128,4096]{1,0:T(8,128)(2,1)S(1)}, bf16[128,4096]{1,0:T(8,128)(2,1)S(1)}, u32[]{:S(2)}, u32[]{:S(2)}) collective-permute-start(bf16[128,4096]{1,0:T(8,128)(2,1)S(1)} %get-tuple-element.69), channel_id=1, source_target_pairs={{0,1},{1,0},{2,3},{3,2},{4,5},{5,4},{6,7},{7,6},{8,9},{9,8},{10,11... | collective-permute-start | bytes 3145736 | tf_op jit(solution)/shard_map/ppermute | solution.py:362
  5.9 7.1 %copy-start.3 = (bf16[16,8192]{1,0:T(8,128)(2,1)S(1)}, bf16[16,8192]{1,0:T(8,128)(2,1)}, u32[]{:S(2)}) copy-start(bf16[16,8192]{1,0:T(8,128)(2,1)} %tok_ref.3) | copy-start | bytes 786436
  5.9 7.1 %copy-start.4 = (s32[64]{0:T(128)S(1)}, s32[64]{0:T(128)}, u32[]{:S(2)}) copy-start(s32[64]{0:T(128)} %param.12) | copy-start | bytes 772
  5.9 7.1 %copy-start.5 = (s32[64]{0:T(128)S(1)}, s32[64]{0:T(128)}, u32[]{:S(2)}) copy-start(s32[64]{0:T(128)} %param.13) | copy-start | bytes 772
  9.6 3.4 %copy-start.2 = (bf16[640,1024]{1,0:T(8,128)(2,1)S(1)}, bf16[640,1024]{1,0:T(8,128)(2,1)}, u32[]{:S(2)}) copy-start(bf16[640,1024]{1,0:T(8,128)(2,1)} %up_ref.1) | copy-start | bytes 3932164
  9.6 6.9 %collective-permute-start.12 = (bf16[128,4096]{1,0:T(8,128)(2,1)S(1)}, bf16[128,4096]{1,0:T(8,128)(2,1)S(1)}, u32[]{:S(2)}, u32[]{:S(2)}) collective-permute-start(bf16[128,4096]{1,0:T(8,128)(2,1)S(1)} %get-tuple-element.73), channel_id=1, source_target_pairs={{0,1},{1,0},{2,3},{3,2},{4,5},{5,4},{6,7},{7,6},{8,9},{9,8},{10,11... | collective-permute-start | bytes 3145736 | tf_op jit(solution)/shard_map/ppermute | solution.py:362
  10.0 15.8 %collective-permute-start.11 = (bf16[64,4096]{1,0:T(8,128)(2,1)S(1)}, bf16[64,4096]{1,0:T(8,128)(2,1)S(1)}, u32[]{:S(2)}, u32[]{:S(2)}) collective-permute-start(bf16[64,4096]{1,0:T(8,128)(2,1)S(1)} %get-tuple-element.71), channel_id=1, source_target_pairs={{0,2},{1,3},{2,0},{3,1},{4,6},{5,7},{6,4},{7,5},{8,10},{9,11},{10,... | collective-permute-start | bytes 1572872 | tf_op jit(solution)/shard_map/ppermute | solution.py:362
  13.0 26.9 %copy-start.6 = (bf16[64,16,512]{2,1,0:T(8,128)(2,1)S(1)}, bf16[64,16,512]{2,1,0:T(8,128)(2,1)}, u32[]{:S(2)}) copy-start(bf16[64,16,512]{2,1,0:T(8,128)(2,1)} %param.10) | copy-start | bytes 3145732
  14.5 1.4 %collective-permute-start = (bf16[144,512]{1,0:T(8,128)(2,1)S(1)}, bf16[144,512]{1,0:T(8,128)(2,1)S(1)}, u32[]{:S(2)}, u32[]{:S(2)}) collective-permute-start(bf16[144,512]{1,0:T(8,128)(2,1)S(1)} %get-tuple-element.49), channel_id=1, source_target_pairs={{0,1},{1,0},{2,3},{3,2},{4,5},{5,4},{6,7},{7,6},{8,9},{9,8},{10,11... | collective-permute-start | bytes 442376 | tf_op jit(solution)/shard_map/ppermute | solution.py:411
  15.9 13.0 %collective-permute-start.1 = (bf16[144,512]{1,0:T(8,128)(2,1)S(1)}, bf16[144,512]{1,0:T(8,128)(2,1)S(1)}, u32[]{:S(2)}, u32[]{:S(2)}) collective-permute-start(bf16[144,512]{1,0:T(8,128)(2,1)S(1)} %get-tuple-element.52), channel_id=1, source_target_pairs={{0,2},{1,3},{2,0},{3,1},{4,6},{5,7},{6,4},{7,5},{8,10},{9,11},{10,... | collective-permute-start | bytes 442376 | tf_op jit(solution)/shard_map/ppermute | solution.py:411
  26.1 26.6 %collective-permute-start.16 = (bf16[64,4096]{1,0:T(8,128)(2,1)S(1)}, bf16[64,4096]{1,0:T(8,128)(2,1)S(1)}, u32[]{:S(2)}, u32[]{:S(2)}) collective-permute-start(bf16[64,4096]{1,0:T(8,128)(2,1)S(1)} %get-tuple-element.79), channel_id=1, source_target_pairs={{0,2},{1,3},{2,0},{3,1},{4,6},{5,7},{6,4},{7,5},{8,10},{9,11},{10,... | collective-permute-start | bytes 1572872 | tf_op jit(solution)/shard_map/ppermute | solution.py:362
  29.0 5.4 %collective-permute-start.2 = (bf16[80,512]{1,0:T(8,128)(2,1)S(1)}, bf16[80,512]{1,0:T(8,128)(2,1)S(1)}, u32[]{:S(2)}, u32[]{:S(2)}) collective-permute-start(bf16[80,512]{1,0:T(8,128)(2,1)S(1)} %get-tuple-element.55), channel_id=1, source_target_pairs={{0,4},{1,5},{2,6},{3,7},{4,0},{5,1},{6,2},{7,3},{8,12},{9,13},{10,... | collective-permute-start | bytes 245768 | tf_op jit(solution)/shard_map/ppermute | solution.py:411
  31.1 7.1 %collective-permute-start.3 = (bf16[80,512]{1,0:T(8,128)(2,1)S(1)}, bf16[80,512]{1,0:T(8,128)(2,1)S(1)}, u32[]{:S(2)}, u32[]{:S(2)}) collective-permute-start(bf16[80,512]{1,0:T(8,128)(2,1)S(1)} %get-tuple-element.56), channel_id=1, source_target_pairs={{0,8},{1,9},{2,10},{3,11},{4,12},{5,13},{6,14},{7,15},{8,0},{9,1},... | collective-permute-start | bytes 245768 | tf_op jit(solution)/shard_map/ppermute | solution.py:411
  33.7 6.3 %collective-permute-start.4 = (bf16[80,512]{1,0:T(8,128)(2,1)S(1)}, bf16[80,512]{1,0:T(8,128)(2,1)S(1)}, u32[]{:S(2)}, u32[]{:S(2)}) collective-permute-start(bf16[80,512]{1,0:T(8,128)(2,1)S(1)} %get-tuple-element.57), channel_id=1, source_target_pairs={{0,12},{1,13},{2,14},{3,15},{4,8},{5,9},{6,10},{7,11},{8,4},{9,5},... | collective-permute-start | bytes 245768 | tf_op jit(solution)/shard_map/ppermute | solution.py:411
  40.8 28.9 %copy-start.1 = (bf16[640,256]{1,0:T(8,128)(2,1)S(1)}, bf16[640,256]{1,0:T(8,128)(2,1)}, u32[]{:S(2)}) copy-start(bf16[640,256]{1,0:T(8,128)(2,1)} %cot_ref.1) | copy-start | bytes 983044
  40.8 1.4 %collective-permute-start.5 = (bf16[144,512]{1,0:T(8,128)(2,1)S(1)}, bf16[144,512]{1,0:T(8,128)(2,1)S(1)}, u32[]{:S(2)}, u32[]{:S(2)}) collective-permute-start(bf16[144,512]{1,0:T(8,128)(2,1)S(1)} %get-tuple-element.60), channel_id=1, source_target_pairs={{0,1},{1,0},{2,3},{3,2},{4,5},{5,4},{6,7},{7,6},{8,9},{9,8},{10,11... | collective-permute-start | bytes 442376 | tf_op jit(solution)/shard_map/ppermute | solution.py:411
  42.2 6.0 %collective-permute-start.6 = (bf16[144,512]{1,0:T(8,128)(2,1)S(1)}, bf16[144,512]{1,0:T(8,128)(2,1)S(1)}, u32[]{:S(2)}, u32[]{:S(2)}) collective-permute-start(bf16[144,512]{1,0:T(8,128)(2,1)S(1)} %get-tuple-element.63), channel_id=1, source_target_pairs={{0,2},{1,3},{2,0},{3,1},{4,6},{5,7},{6,4},{7,5},{8,10},{9,11},{10,... | collective-permute-start | bytes 442376 | tf_op jit(solution)/shard_map/ppermute | solution.py:411
  43.8 22.7 %collective-permute-start.13 = (bf16[16,4096]{1,0:T(8,128)(2,1)S(1)}, bf16[16,4096]{1,0:T(8,128)(2,1)S(1)}, u32[]{:S(2)}, u32[]{:S(2)}) collective-permute-start(bf16[16,4096]{1,0:T(8,128)(2,1)S(1)} %get-tuple-element.75), channel_id=1, source_target_pairs={{0,4},{1,5},{2,6},{3,7},{4,0},{5,1},{6,2},{7,3},{8,12},{9,13},{10,... | collective-permute-start | bytes 393224 | tf_op jit(solution)/shard_map/ppermute | solution.py:362
  48.2 5.0 %collective-permute-start.7 = (bf16[80,512]{1,0:T(8,128)(2,1)S(1)}, bf16[80,512]{1,0:T(8,128)(2,1)S(1)}, u32[]{:S(2)}, u32[]{:S(2)}) collective-permute-start(bf16[80,512]{1,0:T(8,128)(2,1)S(1)} %get-tuple-element.65), channel_id=1, source_target_pairs={{0,4},{1,5},{2,6},{3,7},{4,0},{5,1},{6,2},{7,3},{8,12},{9,13},{10,... | collective-permute-start | bytes 245768 | tf_op jit(solution)/shard_map/ppermute | solution.py:411
  48.3 14.7 %collective-permute-start.8 = (bf16[80,512]{1,0:T(8,128)(2,1)S(1)}, bf16[80,512]{1,0:T(8,128)(2,1)S(1)}, u32[]{:S(2)}, u32[]{:S(2)}) collective-permute-start(bf16[80,512]{1,0:T(8,128)(2,1)S(1)} %get-tuple-element.66), channel_id=1, source_target_pairs={{0,8},{1,9},{2,10},{3,11},{4,12},{5,13},{6,14},{7,15},{8,0},{9,1},... | collective-permute-start | bytes 245768 | tf_op jit(solution)/shard_map/ppermute | solution.py:411
  50.2 12.8 %collective-permute-start.9 = (bf16[80,512]{1,0:T(8,128)(2,1)S(1)}, bf16[80,512]{1,0:T(8,128)(2,1)S(1)}, u32[]{:S(2)}, u32[]{:S(2)}) collective-permute-start(bf16[80,512]{1,0:T(8,128)(2,1)S(1)} %get-tuple-element.67), channel_id=1, source_target_pairs={{0,12},{1,13},{2,14},{3,15},{4,8},{5,9},{6,10},{7,11},{8,4},{9,5},... | collective-permute-start | bytes 245768 | tf_op jit(solution)/shard_map/ppermute | solution.py:411
  52.7 20.8 %collective-permute-start.14 = (bf16[16,4096]{1,0:T(8,128)(2,1)S(1)}, bf16[16,4096]{1,0:T(8,128)(2,1)S(1)}, u32[]{:S(2)}, u32[]{:S(2)}) collective-permute-start(bf16[16,4096]{1,0:T(8,128)(2,1)S(1)} %get-tuple-element.76), channel_id=1, source_target_pairs={{0,8},{1,9},{2,10},{3,11},{4,12},{5,13},{6,14},{7,15},{8,0},{9,1},... | collective-permute-start | bytes 393224 | tf_op jit(solution)/shard_map/ppermute | solution.py:362
  53.3 20.2 %collective-permute-start.15 = (bf16[16,4096]{1,0:T(8,128)(2,1)S(1)}, bf16[16,4096]{1,0:T(8,128)(2,1)S(1)}, u32[]{:S(2)}, u32[]{:S(2)}) collective-permute-start(bf16[16,4096]{1,0:T(8,128)(2,1)S(1)} %get-tuple-element.77), channel_id=1, source_target_pairs={{0,12},{1,13},{2,14},{3,15},{4,8},{5,9},{6,10},{7,11},{8,4},{9,5},... | collective-permute-start | bytes 393224 | tf_op jit(solution)/shard_map/ppermute | solution.py:362
  63.0 10.4 %collective-permute-start.17 = (bf16[16,4096]{1,0:T(8,128)(2,1)S(1)}, bf16[16,4096]{1,0:T(8,128)(2,1)S(1)}, u32[]{:S(2)}, u32[]{:S(2)}) collective-permute-start(bf16[16,4096]{1,0:T(8,128)(2,1)S(1)} %get-tuple-element.81), channel_id=1, source_target_pairs={{0,4},{1,5},{2,6},{3,7},{4,0},{5,1},{6,2},{7,3},{8,12},{9,13},{10,... | collective-permute-start | bytes 393224 | tf_op jit(solution)/shard_map/ppermute | solution.py:362
  63.1 16.0 %collective-permute-start.18 = (bf16[16,4096]{1,0:T(8,128)(2,1)S(1)}, bf16[16,4096]{1,0:T(8,128)(2,1)S(1)}, u32[]{:S(2)}, u32[]{:S(2)}) collective-permute-start(bf16[16,4096]{1,0:T(8,128)(2,1)S(1)} %get-tuple-element.82), channel_id=1, source_target_pairs={{0,8},{1,9},{2,10},{3,11},{4,12},{5,13},{6,14},{7,15},{8,0},{9,1},... | collective-permute-start | bytes 393224 | tf_op jit(solution)/shard_map/ppermute | solution.py:362
  66.5 12.6 %collective-permute-start.19 = (bf16[16,4096]{1,0:T(8,128)(2,1)S(1)}, bf16[16,4096]{1,0:T(8,128)(2,1)S(1)}, u32[]{:S(2)}, u32[]{:S(2)}) collective-permute-start(bf16[16,4096]{1,0:T(8,128)(2,1)S(1)} %get-tuple-element.83), channel_id=1, source_target_pairs={{0,12},{1,13},{2,14},{3,15},{4,8},{5,9},{6,10},{7,11},{8,4},{9,5},... | collective-permute-start | bytes 393224 | tf_op jit(solution)/shard_map/ppermute | solution.py:362

commit v5 on v3

--- a/solution.py
+++ b/solution.py
@@ -170,11 +170,11 @@
         at, to = at + n, to + m
 
 
-def mask_kernel(rank, lens_ref, slots_ref, after_hbm, send_hbm, mask_ref, send_out):
+def mask_kernel(rank, lens_ref, slots_ref, mask_ref):
     mask_ref[...] = mask_by_column(lens_ref, slots_ref, mask_ref.shape[1], rank).astype(BF)
 
 
-def middle_kernel(rank, mask_ref, recv_ref, down_ref, after_hbm, send_hbm, left_ref, send_ref, sem):
+def middle_kernel(rank, mask_ref, recv_ref, down_ref, send_hbm, left_ref, send_ref, sem):
     tp, own, wide = recv_ref.shape
     rows = tp * own
     share = wide - rows
@@ -239,7 +239,7 @@
 HBM = pl.BlockSpec(memory_space=pltpu.HBM)
 
 
-def call(kernel, out, specs, scratch=(), flops=0, nbytes=0, vmem=48, out_specs=None, alias=None):
+def call(kernel, out, specs, scratch=(), flops=0, nbytes=0, vmem=20, out_specs=None, alias=None):
     return pl.pallas_call(
         kernel,
         out_shape=out,
@@ -269,8 +269,8 @@
     slot = slots.reshape(1, count)
     down_flat = down_maps.reshape(count * rank, share)
 
-    half = width // 2
-    block = half // 4
+    half = width * 5 // 8
+    block = 1024
     m = len(stages[0])
     each = rows // m
     dma = pltpu.SemaphoreType.DMA
@@ -285,6 +285,7 @@
             dma,
             dma((half // block,)),
         ],
+        vmem=48,
         flops=2 * rows * columns * half,
         nbytes=2 * columns * half,
     )(me, cotangent, weight)
@@ -318,18 +319,19 @@
 
     send, *parts_b = call(
         functools.partial(second_kernel, order, rank, half, block),
-        [shape((tp, own, share + rows))] + [shape((each, half))] * m,
+        [shape((tp, own, share + rows))] + [shape((each, width - half))] * m,
         [SMEM, VMEM, VMEM, VMEM, HBM, HBM, HBM],
         scratch=[
             pltpu.VMEM((tp, own, share + rows), BF),
             pltpu.VMEM((own, width), BF),
             pltpu.VMEM((columns, count * rank), BF),
-            pltpu.VMEM((columns, half), BF),
+            pltpu.VMEM((columns, width - half), BF),
             pltpu.VMEM((rows, count * rank), F32),
             dma((3,)),
-            dma((half // block,)),
+            dma(((width - half) // block,)),
         ],
         out_specs=[HBM] + [VMEM] * m,
+        vmem=48,
         flops=2 * rows * columns * (half + count * rank),
         nbytes=2 * columns * (half + count * rank),
     )(me, lens, slot, cotp, tokens, up_maps, weight)
@@ -338,14 +340,7 @@
     held_a = exchange(0, parts_a)
     held_b = exchange(0, parts_b)
     (cut_a,), _ = summed([held_a], [1])
-    mask, send = call(
-        functools.partial(mask_kernel, rank),
-        [shape((count * rank, rows)), shape(send.shape)],
-        [VMEM, VMEM, HBM, HBM],
-        out_specs=[VMEM, HBM],
-        alias={3: 1},
-        flops=2 * rows * count * count * rank,
-    )(lens, slot, cut_a[0], send)
+    (mask,) = call(functools.partial(mask_kernel, rank), [shape((count * rank, rows))], [VMEM, VMEM])(lens, slot)
     recv = lax.all_to_all(send, "tp", split_axis=0, concat_axis=0, tiled=True)
     for stage in range(1, last + 1):
         held_a = exchange(stage, cut_a)
@@ -353,20 +348,18 @@
             (cut_a, cut_b), _ = summed([held_a, held_b], [stage + 1, stage])
         else:
             (cut_b,), _ = summed([held_b], [stage])
-        if stage == 1:
-            after = cut_b[0]
         held_b = exchange(stage, cut_b)
     chunks = [held_a, held_b]
 
     send2, left = call(
         functools.partial(middle_kernel, rank),
         (shape((tp, own, share + rows)), shape((count * rank, rows))),
-        [VMEM] * 3 + [HBM],
+        [VMEM] * 3,
         scratch=[pltpu.VMEM((tp, own, share + rows), BF), dma],
         out_specs=[HBM, VMEM],
         flops=4 * rows * share * count * rank,
         nbytes=3 << 20,
-    )(mask, recv, down_flat, after)
+    )(mask, recv, down_flat)
     recv2 = lax.all_to_all(send2, "tp", split_axis=0, concat_axis=0, tiled=True)
     down_grad = call(
         down_kernel,

time: 83.1 us -> 72.8 us (0.88)
  waiting for transfers between devices: 35.1 us -> 23.2 us
  local copies, waits for them, and re-layouts: 2.22 us -> 4.74 us
  starting transfers between devices: 25.5 us -> 24.3 us
    ppermute x10, waiting for transfers between devices: 35.1 us -> 16 us  [exchange(): lax.ppermute(part, 'tp', pairs(m))]
    all_to_all x1, waiting for transfers between devices: 0.01 us -> 7.24 us  [body(): recv = lax.all_to_all(send, 'tp', split_axis=0, concat_axis=0, tiled=True)]
    unnamed x16 -> x26, local copies, waits for them, and re-layouts: 2.22 us -> 4.74 us
    pallas_call x3, Pallas kernels: 3.29 us -> 5.08 us  [summed(): call(functools.partial(sum_kernel, [(len(g), c) for g, c in zip(groups, c...]
    pallas_call x1, Pallas kernels: 4.95 us -> 3.38 us  [body(): call(functools.partial(second_kernel, order, rank, half, block), [shape((...]
    all_to_all x1, starting transfers between devices: 4.79 us -> 3.55 us  [body(): recv2 = lax.all_to_all(send2, 'tp', split_axis=0, concat_axis=0, tiled=True)]
  transfers between devices with their start and end apart: 12 -> 12, of which waited for: 3 -> 4; matrix products, arithmetic and copies ran while one was open for 0% -> 0% of each run, Pallas kernels for 15% -> 19%
where the time goes in v5:
time: 72.8 us; the launch traced here: 72.4 us
  starting transfers between devices  24.3 us (33%)
  waiting for transfers between devices  23.2 us (32%)
  Pallas kernels  19.4 us (27%)
  local copies, waits for them, and re-layouts  4.74 us (7%)
  between operations  0.75 us (1%)
    ppermute x10, waiting for transfers between devices, exchange(): lax.ppermute(part, 'tp', pairs(m))  16 us
    ppermute x10, starting transfers between devices, exchange(): lax.ppermute(part, 'tp', pairs(m))  13.7 us
    all_to_all x1, waiting for transfers between devices, body(): recv = lax.all_to_all(send, 'tp', split_axis=0, concat_axis=0, tiled=True)  7.24 us
    all_to_all x1, starting transfers between devices, body(): recv = lax.all_to_all(send, 'tp', split_axis=0, concat_axis=0, tiled=True)  7.05 us
    pallas_call x3, Pallas kernels, summed(): call(functools.partial(sum_kernel, [(len(g), c) for g, c in zip(groups, c...  5.08 us
    unnamed x26, local copies, waits for them, and re-layouts  4.74 us
    pallas_call x1, Pallas kernels, body(): call(functools.partial(first_kernel, order, own, block), [shape((rows, co...  4.46 us
    all_to_all x1, starting transfers between devices, body(): recv2 = lax.all_to_all(send2, 'tp', split_axis=0, concat_axis=0, tiled=True)  3.55 us
  transfers between devices with their start and end apart: 12, of which 4 were waited for; matrix products, arithmetic and copies ran while one was open for 0% of the time, Pallas kernels for 19%

profile of v5, /device:TPU:0, one launch (start us, length us, event | category | flops | bytes accessed | tf_op | source)
XLA Modules:
  0.0 72.4 jit_solution(14725870095912748559)
XLA Ops:
  0.6 0.0 copy-start.1
  0.6 1.0 %copy-done.1 = bf16[640,256]{1,0:T(8,128)(2,1)S(1)} copy-done((bf16[640,256]{1,0:T(8,128)(2,1)S(1)}, bf16[640,256]{1,0:T(8,128)(2,1)}, u32[]{:S(2)}) %copy-start.1) | copy-done | bytes 327704
  1.6 0.0 copy-start
  1.6 0.0 copy-start.3
  1.6 0.0 copy-start.9
  1.6 0.0 copy-start.10
  1.6 4.5 %shard_map.95 = (bf16[256,640]{1,0:T(8,128)(2,1)S(1)}, bf16[128,5120]{1,0:T(8,128)(2,1)S(1)}, bf16[128,5120]{1,0:T(8,128)(2,1)S(1)}) custom-call(s32[1]{0:T(128)} %bitcast.2.me_ref, bf16[640,256]{1,0:T(8,128)(2,1)S(1)} %copy-done.1, bf16[640,8192]{1,0:T(8,128)(2,1)} %weight_hbm.3), custom_call_target="tpu_custom_call" | custom-call | flops 1677721600 | bytes 6553600 | tf_op jit(solution)/shard_map/pallas_call | solution.py:277
  6.1 0.5 collective-permute-start
  6.6 0.0 copy-done
  6.6 0.0 copy-done.3
  6.6 0.0 copy-done.9
  6.6 0.0 copy-done.10
  6.6 3.4 %shard_map.96 = (bf16[16,16,768]{2,1,0:T(8,128)(2,1)}, bf16[128,3072]{1,0:T(8,128)(2,1)S(1)}, bf16[128,3072]{1,0:T(8,128)(2,1)S(1)}) custom-call(s32[1]{0:T(128)} %bitcast.2.me_ref, s32[1,64]{1,0:T(1,128)S(1)} %bitcast.5, s32[1,64]{1,0:T(1,128)S(1)} %bitcast.7, bf16[256,640]{1,0:T(8,128)(2,1)S(1)} %get-tuple-element.23.cotp_ref, ...), custom_call_target="tpu_custom_call" | custom-call | flops 2013265920 | bytes 7864320 | tf_op jit(solution)/shard_map/pallas_call | solution.py:320
  10.0 0.0 copy-start.4
  10.0 0.9 %copy-done.4 = bf16[128,3072]{1,0:T(8,128)(2,1)} copy-done((bf16[128,3072]{1,0:T(8,128)(2,1)}, bf16[128,3072]{1,0:T(8,128)(2,1)S(1)}, u32[]{:S(2)}) %copy-start.4) | copy-done | bytes 786456
  10.9 0.0 copy-start.12
  10.9 0.9 %copy-done.12 = bf16[128,3072]{1,0:T(8,128)(2,1)} copy-done((bf16[128,3072]{1,0:T(8,128)(2,1)}, bf16[128,3072]{1,0:T(8,128)(2,1)S(1)}, u32[]{:S(2)}) %copy-start.12) | copy-done | bytes 786456
  11.8 7.0 %all-to-all-start = ((bf16[16,16,768]{2,1,0:T(8,128)(2,1)}), bf16[16,16,768]{2,1,0:T(8,128)(2,1)S(1)}, u32[]{:S(2)}, u32[]{:S(2)}) async-start(bf16[16,16,768]{2,1,0:T(8,128)(2,1)} %get-tuple-element.24), calls=%async_computation | async-start | bytes 786432 | tf_op jit(solution)/shard_map/all_to_all | solution.py:344
  18.8 0.4 collective-permute-start.2
  19.2 0.0 collective-permute-done.refs_1_
  19.2 2.3 %shard_map.98 = (bf16[64,5120]{1,0:T(8,128)(2,1)S(1)}, bf16[64,5120]{1,0:T(8,128)(2,1)}) custom-call(bf16[128,5120]{1,0:T(8,128)(2,1)S(1)} %get-tuple-element.26.refs_0_, bf16[128,5120]{1,0:T(8,128)(2,1)} %collective-permute-done.refs_1_), custom_call_target="tpu_custom_call" | custom-call | bytes 5242880 | tf_op jit(solution)/shard_map/pallas_call | solution.py:306
  21.6 1.7 %collective-permute-start.1 = (bf16[64,5120]{1,0:T(8,128)(2,1)}, bf16[64,5120]{1,0:T(8,128)(2,1)}, u32[]{:S(2)}, u32[]{:S(2)}) collective-permute-start(bf16[64,5120]{1,0:T(8,128)(2,1)} %get-tuple-element.29), channel_id=1, source_target_pairs={{0,2},{1,3},{2,0},{3,1},{4,6},{5,7},{6,4},{7,5},{8,10},{9,11},{10,... | collective-permute-start | bytes 1966088 | tf_op jit(solution)/shard_map/ppermute | solution.py:297
  23.2 0.6 shard_map.94.mask_ref
  23.8 7.2 %all-to-all-done.recv_ref = bf16[16,16,768]{2,1,0:T(8,128)(2,1)S(1)} async-done(((bf16[16,16,768]{2,1,0:T(8,128)(2,1)}), bf16[16,16,768]{2,1,0:T(8,128)(2,1)S(1)}, u32[]{:S(2)}, u32[]{:S(2)}) %all-to-all-start) | async-done | bytes 393248 | tf_op jit(solution)/shard_map/all_to_all | solution.py:344
  31.1 0.0 copy-start.11
  31.1 1.2 %copy-done.11 = bf16[64,16,512]{2,1,0:T(8,128)(2,1)S(1)} copy-done((bf16[64,16,512]{2,1,0:T(8,128)(2,1)S(1)}, bf16[64,16,512]{2,1,0:T(8,128)(2,1)}, u32[]{:S(2)}) %copy-start.11) | copy-done | bytes 1048600
  32.3 0.0 copy-start.5
  32.3 1.0 %shard_map.97 = (bf16[16,16,768]{2,1,0:T(8,128)(2,1)S(1)}, bf16[1024,256]{1,0:T(8,128)(2,1)S(1)}) custom-call(bf16[1024,256]{1,0:T(8,128)(2,1)S(1)} %shard_map.94.mask_ref, bf16[16,16,768]{2,1,0:T(8,128)(2,1)S(1)} %all-to-all-done.recv_ref, bf16[1024,512]{1,0:T(8,128)(2,1)S(1)} %bitcast.9), custom_call_target="tpu_custom_call" | custom-call | flops 536870912 | bytes 3145728 | tf_op jit(solution)/shard_map/pallas_call | solution.py:354
  33.3 0.0 copy-start.6
  33.3 0.8 %copy-done.6 = bf16[16,16,768]{2,1,0:T(8,128)(2,1)} copy-done((bf16[16,16,768]{2,1,0:T(8,128)(2,1)}, bf16[16,16,768]{2,1,0:T(8,128)(2,1)S(1)}, u32[]{:S(2)}) %copy-start.6) | copy-done | bytes 393240
  34.0 3.6 %all-to-all-start.1 = ((bf16[16,16,768]{2,1,0:T(8,128)(2,1)}), bf16[16,16,768]{2,1,0:T(8,128)(2,1)S(1)}, u32[]{:S(2)}, u32[]{:S(2)}) async-start(bf16[16,16,768]{2,1,0:T(8,128)(2,1)} %copy-done.6), calls=%async_computation.1 | async-start | bytes 786432 | tf_op jit(solution)/shard_map/all_to_all | solution.py:363
  37.6 0.0 collective-permute-done.2.refs_3_
  37.6 3.1 %collective-permute-done.1.refs_1_ = bf16[64,5120]{1,0:T(8,128)(2,1)} collective-permute-done((bf16[64,5120]{1,0:T(8,128)(2,1)}, bf16[64,5120]{1,0:T(8,128)(2,1)}, u32[]{:S(2)}, u32[]{:S(2)}) %collective-permute-start.1) | collective-permute-done | bytes 655392 | tf_op jit(solution)/shard_map/ppermute | solution.py:297
  40.7 0.0 copy-done.5
  40.7 2.1 %shard_map.99 = (bf16[16,5120]{1,0:T(8,128)(2,1)S(1)}, bf16[16,5120]{1,0:T(8,128)(2,1)S(1)}, bf16[16,5120]{1,0:T(8,128)(2,1)}, bf16[16,5120]{1,0:T(8,128)(2,1)},...) custom-call(bf16[64,5120]{1,0:T(8,128)(2,1)S(1)} %get-tuple-element.28.refs_0_, ...), custom_call_target="tpu_custom_call" | custom-call | bytes 5767168 | tf_op jit(solution)/shard_map/pallas_call | solution.py:306
  42.8 0.0 copy-start.7
  42.8 2.3 %collective-permute-start.6 = (bf16[64,3072]{1,0:T(8,128)(2,1)S(1)}, bf16[64,3072]{1,0:T(8,128)(2,1)S(1)}, u32[]{:S(2)}, u32[]{:S(2)}) collective-permute-start(bf16[64,3072]{1,0:T(8,128)(2,1)S(1)} %get-tuple-element.37), channel_id=1, source_target_pairs={{0,2},{1,3},{2,0},{3,1},{4,6},{5,7},{6,4},{7,5},{8,10},{9,11},{10,... | collective-permute-start | bytes 1179656 | tf_op jit(solution)/shard_map/ppermute | solution.py:297
  45.1 1.6 %collective-permute-start.3 = (bf16[16,5120]{1,0:T(8,128)(2,1)S(1)}, bf16[16,5120]{1,0:T(8,128)(2,1)S(1)}, u32[]{:S(2)}, u32[]{:S(2)}) collective-permute-start(bf16[16,5120]{1,0:T(8,128)(2,1)S(1)} %get-tuple-element.33), channel_id=1, source_target_pairs={{0,4},{1,5},{2,6},{3,7},{4,0},{5,1},{6,2},{7,3},{8,12},{9,13},{10,... | collective-permute-start | bytes 491528 | tf_op jit(solution)/shard_map/ppermute | solution.py:297
  46.7 1.8 %collective-permute-start.4 = (bf16[16,5120]{1,0:T(8,128)(2,1)}, bf16[16,5120]{1,0:T(8,128)(2,1)S(1)}, u32[]{:S(2)}, u32[]{:S(2)}) collective-permute-start(bf16[16,5120]{1,0:T(8,128)(2,1)} %get-tuple-element.34), channel_id=1, source_target_pairs={{0,8},{1,9},{2,10},{3,11},{4,12},{5,13},{6,14},{7,15},{8,0},{9,1},... | collective-permute-start | bytes 491528 | tf_op jit(solution)/shard_map/ppermute | solution.py:297
  48.5 1.0 %collective-permute-start.5 = (bf16[16,5120]{1,0:T(8,128)(2,1)}, bf16[16,5120]{1,0:T(8,128)(2,1)S(1)}, u32[]{:S(2)}, u32[]{:S(2)}) collective-permute-start(bf16[16,5120]{1,0:T(8,128)(2,1)} %get-tuple-element.35), channel_id=1, source_target_pairs={{0,12},{1,13},{2,14},{3,15},{4,8},{5,9},{6,10},{7,11},{8,4},{9,5},... | collective-permute-start | bytes 491528 | tf_op jit(solution)/shard_map/ppermute | solution.py:297
  49.5 6.0 %collective-permute-done.6.refs_1_ = bf16[64,3072]{1,0:T(8,128)(2,1)S(1)} collective-permute-done((bf16[64,3072]{1,0:T(8,128)(2,1)S(1)}, bf16[64,3072]{1,0:T(8,128)(2,1)S(1)}, u32[]{:S(2)}, u32[]{:S(2)}) %collective-permute-start.6) | collective-permute-done | bytes 393248 | tf_op jit(solution)/shard_map/ppermute | solution.py:297
  55.5 0.7 shard_map.100
  56.1 1.9 %collective-permute-start.7 = (bf16[16,3072]{1,0:T(8,128)(2,1)}, bf16[16,3072]{1,0:T(8,128)(2,1)S(1)}, u32[]{:S(2)}, u32[]{:S(2)}) collective-permute-start(bf16[16,3072]{1,0:T(8,128)(2,1)} %get-tuple-element.39), channel_id=1, source_target_pairs={{0,4},{1,5},{2,6},{3,7},{4,0},{5,1},{6,2},{7,3},{8,12},{9,13},{10,... | collective-permute-start | bytes 294920 | tf_op jit(solution)/shard_map/ppermute | solution.py:297
  58.0 1.0 %collective-permute-start.8 = (bf16[16,3072]{1,0:T(8,128)(2,1)S(1)}, bf16[16,3072]{1,0:T(8,128)(2,1)S(1)}, u32[]{:S(2)}, u32[]{:S(2)}) collective-permute-start(bf16[16,3072]{1,0:T(8,128)(2,1)S(1)} %get-tuple-element.40), channel_id=1, source_target_pairs={{0,8},{1,9},{2,10},{3,11},{4,12},{5,13},{6,14},{7,15},{8,0},{9,1},... | collective-permute-start | bytes 294920 | tf_op jit(solution)/shard_map/ppermute | solution.py:297
  59.0 0.0 collective-permute-done.3.refs_1_
  59.0 1.5 %collective-permute-start.9 = (bf16[16,3072]{1,0:T(8,128)(2,1)S(1)}, bf16[16,3072]{1,0:T(8,128)(2,1)S(1)}, u32[]{:S(2)}, u32[]{:S(2)}) collective-permute-start(bf16[16,3072]{1,0:T(8,128)(2,1)S(1)} %get-tuple-element.41), channel_id=1, source_target_pairs={{0,12},{1,13},{2,14},{3,15},{4,8},{5,9},{6,10},{7,11},{8,4},{9,5},... | collective-permute-start | bytes 294920 | tf_op jit(solution)/shard_map/ppermute | solution.py:297
  60.5 0.0 copy-done.7
  60.5 0.0 copy-start.2
  60.5 1.8 %shard_map.102 = f32[1024,512]{1,0:T(8,128)} custom-call(bf16[1024,256]{1,0:T(8,128)(2,1)S(1)} %get-tuple-element.42.left_ref, bf16[16,16,768]{2,1,0:T(8,128)(2,1)S(1)} %all-to-all-done.recv_ref), custom_call_target="tpu_custom_call" | custom-call | flops 268435456 | bytes 3145728 | tf_op jit(solution)/shard_map/pallas_call | solution.py:364
  62.3 0.0 copy-start.8
  62.3 0.0 all-to-all-done.1.recv_ref
  62.3 0.0 copy-done.2
  62.3 2.1 %shard_map.103 = f32[640,1024]{1,0:T(8,128)} custom-call(bf16[1024,256]{1,0:T(8,128)(2,1)S(1)} %shard_map.94.mask_ref, bf16[16,16,768]{2,1,0:T(8,128)(2,1)S(1)} %all-to-all-done.1.recv_ref, bf16[640,256]{1,0:T(8,128)(2,1)S(1)} %copy-done.2), custom_call_target="tpu_custom_call" | custom-call | flops 335544320 | bytes 3145728 | tf_op jit(solution)/shard_map/pallas_call | solution.py:371
  64.4 0.0 collective-permute-done.4.refs_2_
  64.4 0.0 collective-permute-done.5.refs_3_
  64.4 0.0 collective-permute-done.7.refs_5_
  64.4 6.8 %collective-permute-done.8.refs_6_ = bf16[16,3072]{1,0:T(8,128)(2,1)S(1)} collective-permute-done((bf16[16,3072]{1,0:T(8,128)(2,1)S(1)}, bf16[16,3072]{1,0:T(8,128)(2,1)S(1)}, u32[]{:S(2)}, u32[]{:S(2)}) %collective-permute-start.8) | collective-permute-done | bytes 98336 | tf_op jit(solution)/shard_map/ppermute | solution.py:297
  71.2 0.0 collective-permute-done.9.refs_7_
  71.2 0.0 copy-done.8
  71.2 1.2 %shard_map.101 = bf16[16,8192]{1,0:T(8,128)(2,1)} custom-call(bf16[16,16,768]{2,1,0:T(8,128)(2,1)S(1)} %all-to-all-done.1.recv_ref, bf16[16,8192]{1,0:T(8,128)(2,1)S(1)} %copy-done.3, bf16[16,5120]{1,0:T(8,128)(2,1)S(1)} %copy-done.8, bf16[16,5120]{1,0:T(8,128)(2,1)S(1)} %collective-permute-done.3.refs_1_, ...), custom_call_target="tpu_custom_call" | custom-call | bytes 2097152 | tf_op jit(solution)/shard_map/pallas_call | solution.py:379
Async XLA Ops:
  0.6 1.0 %copy-start.1 = (bf16[640,256]{1,0:T(8,128)(2,1)S(1)}, bf16[640,256]{1,0:T(8,128)(2,1)}, u32[]{:S(2)}) copy-start(bf16[640,256]{1,0:T(8,128)(2,1)} %cot_ref.1) | copy-start | bytes 983044
  1.6 5.0 %copy-start = (bf16[640,1024]{1,0:T(8,128)(2,1)S(1)}, bf16[640,1024]{1,0:T(8,128)(2,1)}, u32[]{:S(2)}) copy-start(bf16[640,1024]{1,0:T(8,128)(2,1)} %up_hbm.1) | copy-start | bytes 3932164
  1.6 5.0 %copy-start.3 = (bf16[16,8192]{1,0:T(8,128)(2,1)S(1)}, bf16[16,8192]{1,0:T(8,128)(2,1)}, u32[]{:S(2)}) copy-start(bf16[16,8192]{1,0:T(8,128)(2,1)} %tok_ref.1) | copy-start | bytes 786436
  1.6 5.0 %copy-start.9 = (s32[64]{0:T(128)S(1)}, s32[64]{0:T(128)}, u32[]{:S(2)}) copy-start(s32[64]{0:T(128)} %param.12) | copy-start | bytes 772
  1.6 5.0 %copy-start.10 = (s32[64]{0:T(128)S(1)}, s32[64]{0:T(128)}, u32[]{:S(2)}) copy-start(s32[64]{0:T(128)} %param.13) | copy-start | bytes 772
  6.1 13.2 %collective-permute-start = (bf16[128,5120]{1,0:T(8,128)(2,1)S(1)}, bf16[128,5120]{1,0:T(8,128)(2,1)}, u32[]{:S(2)}, u32[]{:S(2)}) collective-permute-start(bf16[128,5120]{1,0:T(8,128)(2,1)S(1)} %get-tuple-element.27), channel_id=1, source_target_pairs={{0,1},{1,0},{2,3},{3,2},{4,5},{5,4},{6,7},{7,6},{8,9},{9,8},{10,11... | collective-permute-start | bytes 3932168 | tf_op jit(solution)/shard_map/ppermute | solution.py:297
  10.0 0.9 %copy-start.4 = (bf16[128,3072]{1,0:T(8,128)(2,1)}, bf16[128,3072]{1,0:T(8,128)(2,1)S(1)}, u32[]{:S(2)}) copy-start(bf16[128,3072]{1,0:T(8,128)(2,1)S(1)} %get-tuple-element.30.refs_2_) | copy-start | bytes 2359300
  10.9 0.9 %copy-start.12 = (bf16[128,3072]{1,0:T(8,128)(2,1)}, bf16[128,3072]{1,0:T(8,128)(2,1)S(1)}, u32[]{:S(2)}) copy-start(bf16[128,3072]{1,0:T(8,128)(2,1)S(1)} %get-tuple-element.31) | copy-start | bytes 2359300
  11.8 19.3 %all-to-all-start = ((bf16[16,16,768]{2,1,0:T(8,128)(2,1)}), bf16[16,16,768]{2,1,0:T(8,128)(2,1)S(1)}, u32[]{:S(2)}, u32[]{:S(2)}) async-start(bf16[16,16,768]{2,1,0:T(8,128)(2,1)} %get-tuple-element.24), calls=%async_computation | async-start | bytes 786432 | tf_op jit(solution)/shard_map/all_to_all | solution.py:344
  18.8 18.8 %collective-permute-start.2 = (bf16[128,3072]{1,0:T(8,128)(2,1)}, bf16[128,3072]{1,0:T(8,128)(2,1)}, u32[]{:S(2)}, u32[]{:S(2)}) collective-permute-start(bf16[128,3072]{1,0:T(8,128)(2,1)} %copy-done.12), channel_id=1, source_target_pairs={{0,1},{1,0},{2,3},{3,2},{4,5},{5,4},{6,7},{7,6},{8,9},{9,8},{10,11... | collective-permute-start | bytes 2359304 | tf_op jit(solution)/shard_map/ppermute | solution.py:297
  21.6 19.2 %collective-permute-start.1 = (bf16[64,5120]{1,0:T(8,128)(2,1)}, bf16[64,5120]{1,0:T(8,128)(2,1)}, u32[]{:S(2)}, u32[]{:S(2)}) collective-permute-start(bf16[64,5120]{1,0:T(8,128)(2,1)} %get-tuple-element.29), channel_id=1, source_target_pairs={{0,2},{1,3},{2,0},{3,1},{4,6},{5,7},{6,4},{7,5},{8,10},{9,11},{10,... | collective-permute-start | bytes 1966088 | tf_op jit(solution)/shard_map/ppermute | solution.py:297
  31.1 1.2 %copy-start.11 = (bf16[64,16,512]{2,1,0:T(8,128)(2,1)S(1)}, bf16[64,16,512]{2,1,0:T(8,128)(2,1)}, u32[]{:S(2)}) copy-start(bf16[64,16,512]{2,1,0:T(8,128)(2,1)} %param.10) | copy-start | bytes 3145732
  32.3 8.4 %copy-start.5 = (bf16[128,3072]{1,0:T(8,128)(2,1)S(1)}, bf16[128,3072]{1,0:T(8,128)(2,1)}, u32[]{:S(2)}) copy-start(bf16[128,3072]{1,0:T(8,128)(2,1)} %copy-done.4) | copy-start | bytes 2359300
  33.3 0.8 %copy-start.6 = (bf16[16,16,768]{2,1,0:T(8,128)(2,1)}, bf16[16,16,768]{2,1,0:T(8,128)(2,1)S(1)}, u32[]{:S(2)}) copy-start(bf16[16,16,768]{2,1,0:T(8,128)(2,1)S(1)} %get-tuple-element.25) | copy-start | bytes 1179652
  34.0 28.3 %all-to-all-start.1 = ((bf16[16,16,768]{2,1,0:T(8,128)(2,1)}), bf16[16,16,768]{2,1,0:T(8,128)(2,1)S(1)}, u32[]{:S(2)}, u32[]{:S(2)}) async-start(bf16[16,16,768]{2,1,0:T(8,128)(2,1)} %copy-done.6), calls=%async_computation.1 | async-start | bytes 786432 | tf_op jit(solution)/shard_map/all_to_all | solution.py:363
  42.8 17.7 %copy-start.7 = (bf16[16,5120]{1,0:T(8,128)(2,1)}, bf16[16,5120]{1,0:T(8,128)(2,1)S(1)}, u32[]{:S(2)}) copy-start(bf16[16,5120]{1,0:T(8,128)(2,1)S(1)} %get-tuple-element.32.refs_0_) | copy-start | bytes 491524
  42.8 12.7 %collective-permute-start.6 = (bf16[64,3072]{1,0:T(8,128)(2,1)S(1)}, bf16[64,3072]{1,0:T(8,128)(2,1)S(1)}, u32[]{:S(2)}, u32[]{:S(2)}) collective-permute-start(bf16[64,3072]{1,0:T(8,128)(2,1)S(1)} %get-tuple-element.37), channel_id=1, source_target_pairs={{0,2},{1,3},{2,0},{3,1},{4,6},{5,7},{6,4},{7,5},{8,10},{9,11},{10,... | collective-permute-start | bytes 1179656 | tf_op jit(solution)/shard_map/ppermute | solution.py:297
  45.1 13.9 %collective-permute-start.3 = (bf16[16,5120]{1,0:T(8,128)(2,1)S(1)}, bf16[16,5120]{1,0:T(8,128)(2,1)S(1)}, u32[]{:S(2)}, u32[]{:S(2)}) collective-permute-start(bf16[16,5120]{1,0:T(8,128)(2,1)S(1)} %get-tuple-element.33), channel_id=1, source_target_pairs={{0,4},{1,5},{2,6},{3,7},{4,0},{5,1},{6,2},{7,3},{8,12},{9,13},{10,... | collective-permute-start | bytes 491528 | tf_op jit(solution)/shard_map/ppermute | solution.py:297
  46.7 17.7 %collective-permute-start.4 = (bf16[16,5120]{1,0:T(8,128)(2,1)}, bf16[16,5120]{1,0:T(8,128)(2,1)S(1)}, u32[]{:S(2)}, u32[]{:S(2)}) collective-permute-start(bf16[16,5120]{1,0:T(8,128)(2,1)} %get-tuple-element.34), channel_id=1, source_target_pairs={{0,8},{1,9},{2,10},{3,11},{4,12},{5,13},{6,14},{7,15},{8,0},{9,1},... | collective-permute-start | bytes 491528 | tf_op jit(solution)/shard_map/ppermute | solution.py:297
  48.5 15.9 %collective-permute-start.5 = (bf16[16,5120]{1,0:T(8,128)(2,1)}, bf16[16,5120]{1,0:T(8,128)(2,1)S(1)}, u32[]{:S(2)}, u32[]{:S(2)}) collective-permute-start(bf16[16,5120]{1,0:T(8,128)(2,1)} %get-tuple-element.35), channel_id=1, source_target_pairs={{0,12},{1,13},{2,14},{3,15},{4,8},{5,9},{6,10},{7,11},{8,4},{9,5},... | collective-permute-start | bytes 491528 | tf_op jit(solution)/shard_map/ppermute | solution.py:297
  56.1 8.2 %collective-permute-start.7 = (bf16[16,3072]{1,0:T(8,128)(2,1)}, bf16[16,3072]{1,0:T(8,128)(2,1)S(1)}, u32[]{:S(2)}, u32[]{:S(2)}) collective-permute-start(bf16[16,3072]{1,0:T(8,128)(2,1)} %get-tuple-element.39), channel_id=1, source_target_pairs={{0,4},{1,5},{2,6},{3,7},{4,0},{5,1},{6,2},{7,3},{8,12},{9,13},{10,... | collective-permute-start | bytes 294920 | tf_op jit(solution)/shard_map/ppermute | solution.py:297
  58.0 13.2 %collective-permute-start.8 = (bf16[16,3072]{1,0:T(8,128)(2,1)S(1)}, bf16[16,3072]{1,0:T(8,128)(2,1)S(1)}, u32[]{:S(2)}, u32[]{:S(2)}) collective-permute-start(bf16[16,3072]{1,0:T(8,128)(2,1)S(1)} %get-tuple-element.40), channel_id=1, source_target_pairs={{0,8},{1,9},{2,10},{3,11},{4,12},{5,13},{6,14},{7,15},{8,0},{9,1},... | collective-permute-start | bytes 294920 | tf_op jit(solution)/shard_map/ppermute | solution.py:297
  59.0 12.2 %collective-permute-start.9 = (bf16[16,3072]{1,0:T(8,128)(2,1)S(1)}, bf16[16,3072]{1,0:T(8,128)(2,1)S(1)}, u32[]{:S(2)}, u32[]{:S(2)}) collective-permute-start(bf16[16,3072]{1,0:T(8,128)(2,1)S(1)} %get-tuple-element.41), channel_id=1, source_target_pairs={{0,12},{1,13},{2,14},{3,15},{4,8},{5,9},{6,10},{7,11},{8,4},{9,5},... | collective-permute-start | bytes 294920 | tf_op jit(solution)/shard_map/ppermute | solution.py:297
  60.5 1.8 %copy-start.2 = (bf16[640,256]{1,0:T(8,128)(2,1)S(1)}, bf16[640,256]{1,0:T(8,128)(2,1)}, u32[]{:S(2)}) copy-start(bf16[640,256]{1,0:T(8,128)(2,1)} %cot_ref.1) | copy-start | bytes 983044
  62.3 8.9 %copy-start.8 = (bf16[16,5120]{1,0:T(8,128)(2,1)S(1)}, bf16[16,5120]{1,0:T(8,128)(2,1)}, u32[]{:S(2)}) copy-start(bf16[16,5120]{1,0:T(8,128)(2,1)} %copy-done.7) | copy-start | bytes 491524

commit v6 on v5

--- a/solution.py
+++ b/solution.py
@@ -81,13 +81,14 @@
 
 
 def multiply(cotp, wbuf, copies, block, parts):
-    each = parts[0].shape[0]
     for i, copy in enumerate(copies):
         copy.wait()
         columns = pl.ds(i * block, block)
         out = jnp.dot(cotp, wbuf[:, columns], preferred_element_type=F32)
-        for k, part in enumerate(parts):
-            part[:, columns] = out[k * each : (k + 1) * each].astype(BF)
+        at = 0
+        for part in parts:
+            part[:, columns] = out[at : at + part.shape[0]].astype(BF)
+            at += part.shape[0]
 
 
 def first_kernel(order, own, block, me_ref, cot_hbm, weight_hbm, cotp_ref, *refs):
@@ -106,8 +107,15 @@
     multiply(cotp_ref[...], wbuf, copies, block, parts)
 
 
-def second_kernel(order, rank, first, block, me_ref, lens_ref, slots_ref, cotp_ref, tok_hbm, up_hbm, weight_hbm, send_hbm, *refs):
-    *parts, send_ref, tokv, up, wbuf, back_rows, sem, sems = refs
+def second_kernel(first, block, cotp_ref, after_hbm, weight_hbm, *refs):
+    *parts, wbuf, sems = refs
+    copies = fetch_weight(weight_hbm, wbuf, sems, first, block)
+    for copy in copies:
+        copy.start()
+    multiply(cotp_ref[...], wbuf, copies, block, parts)
+
+
+def adapter_kernel(order, rank, me_ref, lens_ref, slots_ref, cotp_ref, tok_hbm, up_hbm, send_hbm, send_ref, tokv, up, back_rows, sem):
     tp, own, _ = send_ref.shape
     width = tokv.shape[1]
     share = width // tp
@@ -116,9 +124,6 @@
     tok_copy.start()
     up_copy = pltpu.make_async_copy(up_hbm, up, sem.at[1])
     up_copy.start()
-    copies = fetch_weight(weight_hbm, wbuf, sems, first, block)
-    for copy in copies:
-        copy.start()
     member, match = membership(lens_ref, slots_ref, rows)
     chosen = lax.dot_general(member, match, NT, preferred_element_type=F32).astype(BF)
     slots = match.shape[0]
@@ -148,7 +153,6 @@
         send_ref[q, :, share:] = back
     send_copy = pltpu.make_async_copy(send_ref, send_hbm, sem.at[2])
     send_copy.start()
-    multiply(cotp_ref[...], wbuf, copies, block, parts)
     send_copy.wait()
 
 
@@ -166,7 +170,14 @@
     for n, m in groups:
         each = terms[at].shape[0] // m
         for i in range(m):
-            outs[to + i][...] = total_of(terms[at : at + n], i, each)
+            if n > 2 and terms[at + 1].shape[0] * (n - 1) == terms[at].shape[0]:
+                small = terms[at + 1].shape[0]
+                for k in range(each // small):
+                    here = terms[at][i * each + k * small : i * each + (k + 1) * small].astype(F32)
+                    there = terms[at + 1 + i * (each // small) + k][...].astype(F32)
+                    outs[to + i][k * small : (k + 1) * small] = (here + there).astype(BF)
+            else:
+                outs[to + i][...] = total_of(terms[at : at + n], i, each)
         at, to = at + n, to + m
 
 
@@ -268,8 +279,9 @@
     lens = lengths.reshape(1, count)
     slot = slots.reshape(1, count)
     down_flat = down_maps.reshape(count * rank, share)
-
-    half = width * 5 // 8
+    weight = pltpu.with_memory_space_constraint(weight, pltpu.HBM)
+
+    half = width * 4 // 8
     block = 1024
     m = len(stages[0])
     each = rows // m
@@ -285,7 +297,7 @@
             dma,
             dma((half // block,)),
         ],
-        vmem=48,
+        vmem=20,
         flops=2 * rows * columns * half,
         nbytes=2 * columns * half,
     )(me, cotangent, weight)
@@ -317,31 +329,34 @@
             at += c
         return cut, list(res[at:])
 
-    send, *parts_b = call(
-        functools.partial(second_kernel, order, rank, half, block),
-        [shape((tp, own, share + rows))] + [shape((each, width - half))] * m,
-        [SMEM, VMEM, VMEM, VMEM, HBM, HBM, HBM],
+    packet = (tp, own, share + rows)
+    (send,) = call(
+        functools.partial(adapter_kernel, order, rank),
+        [shape(packet)],
+        [SMEM, VMEM, VMEM, VMEM, HBM, HBM],
         scratch=[
-            pltpu.VMEM((tp, own, share + rows), BF),
+            pltpu.VMEM(packet, BF),
             pltpu.VMEM((own, width), BF),
             pltpu.VMEM((columns, count * rank), BF),
-            pltpu.VMEM((columns, width - half), BF),
             pltpu.VMEM((rows, count * rank), F32),
             dma((3,)),
-            dma(((width - half) // block,)),
         ],
-        out_specs=[HBM] + [VMEM] * m,
-        vmem=48,
-        flops=2 * rows * columns * (half + count * rank),
-        nbytes=2 * columns * (half + count * rank),
-    )(me, lens, slot, cotp, tokens, up_maps, weight)
+        out_specs=[HBM],
+    )(me, lens, slot, cotp, tokens, up_maps)
 
     last = len(stages) - 1
     held_a = exchange(0, parts_a)
-    held_b = exchange(0, parts_b)
     (cut_a,), _ = summed([held_a], [1])
     (mask,) = call(functools.partial(mask_kernel, rank), [shape((count * rank, rows))], [VMEM, VMEM])(lens, slot)
     recv = lax.all_to_all(send, "tp", split_axis=0, concat_axis=0, tiled=True)
+    cut = 2 * len(stages[1])
+    parts_b = call(
+        functools.partial(second_kernel, half, block),
+        [shape((each, width - half))] + [shape((each // cut, width - half))] * cut,
+        [VMEM, HBM, HBM],
+        scratch=[pltpu.VMEM((columns, width - half), BF), dma(((width - half) // block,))],
+    )(cotp, cut_a[0], weight)
+    held_b = [parts_b[0]] + [lax.ppermute(part, "tp", pairs(stages[0][1])) for part in parts_b[1:]]
     for stage in range(1, last + 1):
         held_a = exchange(stage, cut_a)
         if stage < last:

time: 72.8 us -> 72 us (0.989)
  waiting for transfers between devices: 23.2 us -> 17.5 us
  Pallas kernels: 19.4 us -> 22.8 us
  starting transfers between devices: 24.3 us -> 25.3 us
    all_to_all x1, waiting for transfers between devices: 7.24 us -> 0.86 us  [body(): recv = lax.all_to_all(send, 'tp', split_axis=0, concat_axis=0, tiled=True)]
    pallas_call x1 -> x2, Pallas kernels: 3.38 us -> 6.95 us  [the longest x1 4.6 us: body(): call(functools.partial(second_kernel, half, block), [shape((each, width -...]
    pallas_call x3, Pallas kernels: 5.08 us -> 3.89 us  [summed(): call(functools.partial(sum_kernel, [(len(g), c) for g, c in zip(groups, c...]
    ppermute x0 -> x4, starting transfers between devices: none -> 1.08 us  [body(): lax.ppermute(part, 'tp', pairs(stages[0][1]))]
    ppermute x10 -> x9, waiting for transfers between devices: 16 us -> 16.6 us  [exchange(): lax.ppermute(part, 'tp', pairs(m))]
    unnamed x26 -> x22, local copies, waits for them, and re-layouts: 4.74 us -> 5.19 us
    ppermute x10 -> x9, starting transfers between devices: 13.7 us -> 13.4 us  [exchange(): lax.ppermute(part, 'tp', pairs(m))]
  transfers between devices with their start and end apart: 12 -> 15, of which waited for: 4 -> 3; matrix products, arithmetic and copies ran while one was open for 0% -> 0% of each run, Pallas kernels for 19% -> 23%
where the time goes in v6:
time: 72 us; the launch traced here: 71.6 us
  starting transfers between devices  25.3 us (35%)
  Pallas kernels  22.8 us (32%)
  waiting for transfers between devices  17.5 us (24%)
  local copies, waits for them, and re-layouts  5.19 us (7%)
  between operations  0.81 us (1%)
    ppermute x9, waiting for transfers between devices, exchange(): lax.ppermute(part, 'tp', pairs(m))  16.6 us
    ppermute x9, starting transfers between devices, exchange(): lax.ppermute(part, 'tp', pairs(m))  13.4 us
    all_to_all x1, starting transfers between devices, body(): recv = lax.all_to_all(send, 'tp', split_axis=0, concat_axis=0, tiled=True)  7.06 us
    unnamed x22, local copies, waits for them, and re-layouts  5.19 us
    pallas_call x1, Pallas kernels, body(): call(functools.partial(first_kernel, order, own, block), [shape((rows, co...  4.84 us
    pallas_call x1, Pallas kernels, body(): call(functools.partial(second_kernel, half, block), [shape((each, width -...  4.6 us
    pallas_call x3, Pallas kernels, summed(): call(functools.partial(sum_kernel, [(len(g), c) for g, c in zip(groups, c...  3.89 us
    all_to_all x1, starting transfers between devices, body(): recv2 = lax.all_to_all(send2, 'tp', split_axis=0, concat_axis=0, tiled=True)  3.81 us
  transfers between devices with their start and end apart: 15, of which 3 were waited for; matrix products, arithmetic and copies ran while one was open for 0% of the time, Pallas kernels for 23%

profile of v6, /device:TPU:0, one launch (start us, length us, event | category | flops | bytes accessed | tf_op | source)
XLA Modules:
  0.0 71.6 jit_solution(11593703125241233453)
XLA Ops:
  0.6 0.0 copy-start
  0.6 1.0 %copy-done = bf16[640,256]{1,0:T(8,128)(2,1)S(1)} copy-done((bf16[640,256]{1,0:T(8,128)(2,1)S(1)}, bf16[640,256]{1,0:T(8,128)(2,1)}, u32[]{:S(2)}) %copy-start) | copy-done | bytes 327704
  1.6 0.0 copy-start.2
  1.6 0.0 copy-start.3
  1.6 0.0 copy-start.8
  1.6 0.0 copy-start.9
  1.6 4.8 %shard_map.95 = (bf16[256,640]{1,0:T(8,128)(2,1)S(1)}, bf16[128,4096]{1,0:T(8,128)(2,1)S(1)}, bf16[128,4096]{1,0:T(8,128)(2,1)}) custom-call(s32[1]{0:T(128)} %bitcast.2.me_ref, bf16[640,256]{1,0:T(8,128)(2,1)S(1)} %copy-done, bf16[640,8192]{1,0:T(8,128)(2,1)} %weight_hbm.3), custom_call_target="tpu_custom_call" | custom-call | flops 1342177280 | bytes 5242880 | tf_op jit(solution)/shard_map/pallas_call | solution.py:289
  6.5 0.5 collective-permute-start
  7.0 0.0 copy-done.2
  7.0 0.0 copy-done.3
  7.0 0.0 copy-done.8
  7.0 0.0 copy-done.9
  7.0 2.4 %shard_map.96 = bf16[16,16,768]{2,1,0:T(8,128)(2,1)} custom-call(s32[1]{0:T(128)} %bitcast.2.me_ref, s32[1,64]{1,0:T(1,128)S(1)} %bitcast.5, s32[1,64]{1,0:T(1,128)S(1)} %bitcast.7, bf16[256,640]{1,0:T(8,128)(2,1)S(1)} %get-tuple-element.25.cotp_ref, bf16[16,8192]{1,0:T(8,128)(2,1)S(1)} %copy-done.3, bf16[640,1024]{1,0:T(8,128)(2,1)S(1)} %copy-done.2), custom_call_target="tpu_custom_call" | custom-call | tf_op jit(solution)/shard_map/pallas_call | solution.py:333
  9.4 7.1 %all-to-all-start = ((bf16[16,16,768]{2,1,0:T(8,128)(2,1)}), bf16[16,16,768]{2,1,0:T(8,128)(2,1)S(1)}, u32[]{:S(2)}, u32[]{:S(2)}) async-start(bf16[16,16,768]{2,1,0:T(8,128)(2,1)} %shard_map.96), calls=%async_computation | async-start | bytes 786432 | tf_op jit(solution)/shard_map/all_to_all | solution.py:351
  16.4 0.0 collective-permute-done.refs_1_
  16.4 0.0 copy-start.4
  16.5 1.0 %copy-done.4 = bf16[128,4096]{1,0:T(8,128)(2,1)} copy-done((bf16[128,4096]{1,0:T(8,128)(2,1)}, bf16[128,4096]{1,0:T(8,128)(2,1)S(1)}, u32[]{:S(2)}) %copy-start.4) | copy-done | bytes 1048600
  17.4 0.0 copy-start.5
  17.4 1.2 %copy-done.5 = bf16[128,4096]{1,0:T(8,128)(2,1)S(1)} copy-done((bf16[128,4096]{1,0:T(8,128)(2,1)S(1)}, bf16[128,4096]{1,0:T(8,128)(2,1)}, u32[]{:S(2)}) %copy-start.5) | copy-done | bytes 1048600
  18.6 1.0 %shard_map.98 = (bf16[64,4096]{1,0:T(8,128)(2,1)S(1)}, bf16[64,4096]{1,0:T(8,128)(2,1)}) custom-call(bf16[128,4096]{1,0:T(8,128)(2,1)S(1)} %get-tuple-element.27.refs_0_, bf16[128,4096]{1,0:T(8,128)(2,1)S(1)} %copy-done.5), custom_call_target="tpu_custom_call" | custom-call | bytes 4194304 | tf_op jit(solution)/shard_map/pallas_call | solution.py:318
  19.6 1.9 %collective-permute-start.1 = (bf16[64,4096]{1,0:T(8,128)(2,1)}, bf16[64,4096]{1,0:T(8,128)(2,1)}, u32[]{:S(2)}, u32[]{:S(2)}) collective-permute-start(bf16[64,4096]{1,0:T(8,128)(2,1)} %get-tuple-element.30), channel_id=1, source_target_pairs={{0,2},{1,3},{2,0},{3,1},{4,6},{5,7},{6,4},{7,5},{8,10},{9,11},{10,... | collective-permute-start | bytes 1572872 | tf_op jit(solution)/shard_map/ppermute | solution.py:309
  21.5 4.6 %shard_map.99 = (bf16[128,4096]{1,0:T(8,128)(2,1)S(1)}, bf16[32,4096]{1,0:T(8,128)(2,1)}, bf16[32,4096]{1,0:T(8,128)(2,1)}, bf16[32,4096]{1,0:T(8,128)(2,1)}, bf16[32,4096]{1,0:T(8,128)(2,1)}) custom-call(bf16[256,640]{1,0:T(8,128)(2,1)S(1)} %get-tuple-element.25.cotp_ref, bf16[64,4096]{1,0:T(8,128)(2,1)S(1)} %get-tuple-element.29.after_hbm.refs_0_, ...), custom_call_target="tpu_custom_call" | custom-call | tf_op jit(solution)/shard_map/pallas_call | solution.py:353
  26.1 0.1 collective-permute-start.2
  26.2 0.5 collective-permute-start.3
  26.7 0.1 collective-permute-start.4
  26.8 0.4 collective-permute-start.5
  27.2 0.6 shard_map.94.mask_ref
  27.8 0.9 %all-to-all-done.recv_ref = bf16[16,16,768]{2,1,0:T(8,128)(2,1)S(1)} async-done(((bf16[16,16,768]{2,1,0:T(8,128)(2,1)}), bf16[16,16,768]{2,1,0:T(8,128)(2,1)S(1)}, u32[]{:S(2)}, u32[]{:S(2)}) %all-to-all-start) | async-done | bytes 393248 | tf_op jit(solution)/shard_map/all_to_all | solution.py:351
  28.7 0.0 copy-start.10
  28.7 1.2 %copy-done.10 = bf16[64,16,512]{2,1,0:T(8,128)(2,1)S(1)} copy-done((bf16[64,16,512]{2,1,0:T(8,128)(2,1)S(1)}, bf16[64,16,512]{2,1,0:T(8,128)(2,1)}, u32[]{:S(2)}) %copy-start.10) | copy-done | bytes 1048600
  29.9 1.5 %shard_map.97 = (bf16[16,16,768]{2,1,0:T(8,128)(2,1)}, bf16[1024,256]{1,0:T(8,128)(2,1)S(1)}) custom-call(bf16[1024,256]{1,0:T(8,128)(2,1)S(1)} %shard_map.94.mask_ref, bf16[16,16,768]{2,1,0:T(8,128)(2,1)S(1)} %all-to-all-done.recv_ref, bf16[1024,512]{1,0:T(8,128)(2,1)S(1)} %bitcast.9), custom_call_target="tpu_custom_call" | custom-call | flops 536870912 | bytes 3145728 | tf_op jit(solution)/shard_map/pallas_call | solution.py:369
  31.4 0.0 copy-start.6
  31.4 0.8 %copy-done.6 = bf16[1024,256]{1,0:T(8,128)(2,1)} copy-done((bf16[1024,256]{1,0:T(8,128)(2,1)}, bf16[1024,256]{1,0:T(8,128)(2,1)S(1)}, u32[]{:S(2)}) %copy-start.6) | copy-done | bytes 524312
  32.2 3.8 %all-to-all-start.1 = ((bf16[16,16,768]{2,1,0:T(8,128)(2,1)}), bf16[16,16,768]{2,1,0:T(8,128)(2,1)S(1)}, u32[]{:S(2)}, u32[]{:S(2)}) async-start(bf16[16,16,768]{2,1,0:T(8,128)(2,1)} %get-tuple-element.26), calls=%async_computation.1 | async-start | bytes 786432 | tf_op jit(solution)/shard_map/all_to_all | solution.py:378
  36.0 0.0 copy-start.7
  36.0 0.0 collective-permute-done.2.refs_3_
  36.0 0.0 collective-permute-done.3.refs_4_
  36.1 0.0 collective-permute-done.4.refs_5_
  36.1 0.0 collective-permute-done.5.refs_6_
  36.1 0.0 collective-permute-done.1.refs_1_
  36.1 2.1 %shard_map.100 = (bf16[16,4096]{1,0:T(8,128)(2,1)S(1)}, bf16[16,4096]{1,0:T(8,128)(2,1)S(1)}, bf16[16,4096]{1,0:T(8,128)(2,1)}, bf16[16,4096]{1,0:T(8,128)(2,1)}...) custom-call(bf16[64,4096]{1,0:T(8,128)(2,1)S(1)} %get-tuple-element.29.after_hbm.refs_0_, ...), custom_call_target="tpu_custom_call" | custom-call | bytes 6291456 | tf_op jit(solution)/shard_map/pallas_call | solution.py:318
  38.2 0.0 copy-start.1
  38.2 1.9 %collective-permute-start.9 = (bf16[64,4096]{1,0:T(8,128)(2,1)S(1)}, bf16[64,4096]{1,0:T(8,128)(2,1)S(1)}, u32[]{:S(2)}, u32[]{:S(2)}) collective-permute-start(bf16[64,4096]{1,0:T(8,128)(2,1)S(1)} %get-tuple-element.41), channel_id=1, source_target_pairs={{0,2},{1,3},{2,0},{3,1},{4,6},{5,7},{6,4},{7,5},{8,10},{9,11},{10,... | collective-permute-start | bytes 1572872 | tf_op jit(solution)/shard_map/ppermute | solution.py:309
  40.2 1.5 %collective-permute-start.6 = (bf16[16,4096]{1,0:T(8,128)(2,1)S(1)}, bf16[16,4096]{1,0:T(8,128)(2,1)S(1)}, u32[]{:S(2)}, u32[]{:S(2)}) collective-permute-start(bf16[16,4096]{1,0:T(8,128)(2,1)S(1)} %get-tuple-element.37), channel_id=1, source_target_pairs={{0,4},{1,5},{2,6},{3,7},{4,0},{5,1},{6,2},{7,3},{8,12},{9,13},{10,... | collective-permute-start | bytes 393224 | tf_op jit(solution)/shard_map/ppermute | solution.py:309
  41.6 2.4 %collective-permute-start.7 = (bf16[16,4096]{1,0:T(8,128)(2,1)}, bf16[16,4096]{1,0:T(8,128)(2,1)S(1)}, u32[]{:S(2)}, u32[]{:S(2)}) collective-permute-start(bf16[16,4096]{1,0:T(8,128)(2,1)} %get-tuple-element.38), channel_id=1, source_target_pairs={{0,8},{1,9},{2,10},{3,11},{4,12},{5,13},{6,14},{7,15},{8,0},{9,1},... | collective-permute-start | bytes 393224 | tf_op jit(solution)/shard_map/ppermute | solution.py:309
  44.0 0.6 collective-permute-start.8
  44.5 10.2 %collective-permute-done.9.refs_1_ = bf16[64,4096]{1,0:T(8,128)(2,1)S(1)} collective-permute-done((bf16[64,4096]{1,0:T(8,128)(2,1)S(1)}, bf16[64,4096]{1,0:T(8,128)(2,1)S(1)}, u32[]{:S(2)}, u32[]{:S(2)}) %collective-permute-start.9) | collective-permute-done | bytes 524320 | tf_op jit(solution)/shard_map/ppermute | solution.py:309
  54.7 0.8 %shard_map.101 = (bf16[16,4096]{1,0:T(8,128)(2,1)S(1)}, bf16[16,4096]{1,0:T(8,128)(2,1)}, bf16[16,4096]{1,0:T(8,128)(2,1)}, bf16[16,4096]{1,0:T(8,128)(2,1)}) custom-call(bf16[64,4096]{1,0:T(8,128)(2,1)S(1)} %get-tuple-element.40.refs_0_, bf16[64,4096]{1,0:T(8,128)(2,1)S(1)} %collective-permute-done.9.refs_1_), custom_call_target="tpu_custom_call" | custom-call | bytes 2097152 | tf_op jit(solution)/shard_map/pallas_call | solution.py:318
  55.5 2.2 %collective-permute-start.10 = (bf16[16,4096]{1,0:T(8,128)(2,1)}, bf16[16,4096]{1,0:T(8,128)(2,1)S(1)}, u32[]{:S(2)}, u32[]{:S(2)}) collective-permute-start(bf16[16,4096]{1,0:T(8,128)(2,1)} %get-tuple-element.43), channel_id=1, source_target_pairs={{0,4},{1,5},{2,6},{3,7},{4,0},{5,1},{6,2},{7,3},{8,12},{9,13},{10,... | collective-permute-start | bytes 393224 | tf_op jit(solution)/shard_map/ppermute | solution.py:309
  57.7 1.5 %collective-permute-start.11 = (bf16[16,4096]{1,0:T(8,128)(2,1)}, bf16[16,4096]{1,0:T(8,128)(2,1)S(1)}, u32[]{:S(2)}, u32[]{:S(2)}) collective-permute-start(bf16[16,4096]{1,0:T(8,128)(2,1)} %get-tuple-element.44), channel_id=1, source_target_pairs={{0,8},{1,9},{2,10},{3,11},{4,12},{5,13},{6,14},{7,15},{8,0},{9,1},... | collective-permute-start | bytes 393224 | tf_op jit(solution)/shard_map/ppermute | solution.py:309
  59.2 0.0 collective-permute-done.6.refs_1_
  59.2 0.9 %collective-permute-start.12 = (bf16[16,4096]{1,0:T(8,128)(2,1)}, bf16[16,4096]{1,0:T(8,128)(2,1)S(1)}, u32[]{:S(2)}, u32[]{:S(2)}) collective-permute-start(bf16[16,4096]{1,0:T(8,128)(2,1)} %get-tuple-element.45), channel_id=1, source_target_pairs={{0,12},{1,13},{2,14},{3,15},{4,8},{5,9},{6,10},{7,11},{8,4},{9,5},... | collective-permute-start | bytes 393224 | tf_op jit(solution)/shard_map/ppermute | solution.py:309
  60.1 0.0 copy-done.7
  60.1 1.8 %shard_map.103 = f32[1024,512]{1,0:T(8,128)} custom-call(bf16[1024,256]{1,0:T(8,128)(2,1)S(1)} %copy-done.7, bf16[16,16,768]{2,1,0:T(8,128)(2,1)S(1)} %all-to-all-done.recv_ref), custom_call_target="tpu_custom_call" | custom-call | flops 268435456 | bytes 3145728 | tf_op jit(solution)/shard_map/pallas_call | solution.py:379
  61.9 0.0 all-to-all-done.1.recv_ref
  61.9 0.0 copy-done.1
  61.9 2.1 %shard_map.104 = f32[640,1024]{1,0:T(8,128)} custom-call(bf16[1024,256]{1,0:T(8,128)(2,1)S(1)} %shard_map.94.mask_ref, bf16[16,16,768]{2,1,0:T(8,128)(2,1)S(1)} %all-to-all-done.1.recv_ref, bf16[640,256]{1,0:T(8,128)(2,1)S(1)} %copy-done.1), custom_call_target="tpu_custom_call" | custom-call | flops 335544320 | bytes 3145728 | tf_op jit(solution)/shard_map/pallas_call | solution.py:386
  63.9 0.0 collective-permute-done.7.refs_2_
  63.9 0.0 collective-permute-done.8.refs_3_
  63.9 0.0 collective-permute-done.10.refs_5_
  64.0 6.4 %collective-permute-done.11.refs_6_ = bf16[16,4096]{1,0:T(8,128)(2,1)S(1)} collective-permute-done((bf16[16,4096]{1,0:T(8,128)(2,1)}, bf16[16,4096]{1,0:T(8,128)(2,1)S(1)}, u32[]{:S(2)}, u32[]{:S(2)}) %collective-permute-start.11) | collective-permute-done | bytes 131104 | tf_op jit(solution)/shard_map/ppermute | solution.py:309
  70.4 0.0 collective-permute-done.12.refs_7_
  70.4 1.2 %shard_map.102 = bf16[16,8192]{1,0:T(8,128)(2,1)} custom-call(bf16[16,16,768]{2,1,0:T(8,128)(2,1)S(1)} %all-to-all-done.1.recv_ref, bf16[16,8192]{1,0:T(8,128)(2,1)S(1)} %copy-done.3, bf16[16,4096]{1,0:T(8,128)(2,1)S(1)} %get-tuple-element.36.refs_0_, bf16[16,4096]{1,0:T(8,128)(2,1)S(1)} %collective-permute-done.6.refs_1_, ...), custom_call_target="tpu_custom_call" | custom-call | bytes 2097152 | tf_op jit(solution)/shard_map/pallas_call | solution.py:394
Async XLA Ops:
  0.6 1.0 %copy-start = (bf16[640,256]{1,0:T(8,128)(2,1)S(1)}, bf16[640,256]{1,0:T(8,128)(2,1)}, u32[]{:S(2)}) copy-start(bf16[640,256]{1,0:T(8,128)(2,1)} %cot_ref.1) | copy-start | bytes 983044
  1.6 5.4 %copy-start.2 = (bf16[640,1024]{1,0:T(8,128)(2,1)S(1)}, bf16[640,1024]{1,0:T(8,128)(2,1)}, u32[]{:S(2)}) copy-start(bf16[640,1024]{1,0:T(8,128)(2,1)} %up_hbm.1) | copy-start | bytes 3932164
  1.6 5.4 %copy-start.3 = (bf16[16,8192]{1,0:T(8,128)(2,1)S(1)}, bf16[16,8192]{1,0:T(8,128)(2,1)}, u32[]{:S(2)}) copy-start(bf16[16,8192]{1,0:T(8,128)(2,1)} %tok_ref.1) | copy-start | bytes 786436
  1.6 5.4 %copy-start.8 = (s32[64]{0:T(128)S(1)}, s32[64]{0:T(128)}, u32[]{:S(2)}) copy-start(s32[64]{0:T(128)} %param.12) | copy-start | bytes 772
  1.6 5.4 %copy-start.9 = (s32[64]{0:T(128)S(1)}, s32[64]{0:T(128)}, u32[]{:S(2)}) copy-start(s32[64]{0:T(128)} %param.13) | copy-start | bytes 772
  6.5 10.0 %collective-permute-start = (bf16[128,4096]{1,0:T(8,128)(2,1)}, bf16[128,4096]{1,0:T(8,128)(2,1)S(1)}, u32[]{:S(2)}, u32[]{:S(2)}) collective-permute-start(bf16[128,4096]{1,0:T(8,128)(2,1)} %get-tuple-element.28), channel_id=1, source_target_pairs={{0,1},{1,0},{2,3},{3,2},{4,5},{5,4},{6,7},{7,6},{8,9},{9,8},{10,11... | collective-permute-start | bytes 3145736 | tf_op jit(solution)/shard_map/ppermute | solution.py:309
  9.4 19.3 %all-to-all-start = ((bf16[16,16,768]{2,1,0:T(8,128)(2,1)}), bf16[16,16,768]{2,1,0:T(8,128)(2,1)S(1)}, u32[]{:S(2)}, u32[]{:S(2)}) async-start(bf16[16,16,768]{2,1,0:T(8,128)(2,1)} %shard_map.96), calls=%async_computation | async-start | bytes 786432 | tf_op jit(solution)/shard_map/all_to_all | solution.py:351
  16.4 1.0 %copy-start.4 = (bf16[128,4096]{1,0:T(8,128)(2,1)}, bf16[128,4096]{1,0:T(8,128)(2,1)S(1)}, u32[]{:S(2)}) copy-start(bf16[128,4096]{1,0:T(8,128)(2,1)S(1)} %collective-permute-done.refs_1_) | copy-start | bytes 3145732
  17.4 1.2 %copy-start.5 = (bf16[128,4096]{1,0:T(8,128)(2,1)S(1)}, bf16[128,4096]{1,0:T(8,128)(2,1)}, u32[]{:S(2)}) copy-start(bf16[128,4096]{1,0:T(8,128)(2,1)} %copy-done.4) | copy-start | bytes 3145732
  19.6 16.5 %collective-permute-start.1 = (bf16[64,4096]{1,0:T(8,128)(2,1)}, bf16[64,4096]{1,0:T(8,128)(2,1)}, u32[]{:S(2)}, u32[]{:S(2)}) collective-permute-start(bf16[64,4096]{1,0:T(8,128)(2,1)} %get-tuple-element.30), channel_id=1, source_target_pairs={{0,2},{1,3},{2,0},{3,1},{4,6},{5,7},{6,4},{7,5},{8,10},{9,11},{10,... | collective-permute-start | bytes 1572872 | tf_op jit(solution)/shard_map/ppermute | solution.py:309
  26.1 9.9 %collective-permute-start.2 = (bf16[32,4096]{1,0:T(8,128)(2,1)}, bf16[32,4096]{1,0:T(8,128)(2,1)S(1)}, u32[]{:S(2)}, u32[]{:S(2)}) collective-permute-start(bf16[32,4096]{1,0:T(8,128)(2,1)} %get-tuple-element.32), channel_id=1, source_target_pairs={{0,1},{1,0},{2,3},{3,2},{4,5},{5,4},{6,7},{7,6},{8,9},{9,8},{10,11... | collective-permute-start | bytes 786440 | tf_op jit(solution)/shard_map/ppermute | solution.py:359
  26.2 9.8 %collective-permute-start.3 = (bf16[32,4096]{1,0:T(8,128)(2,1)}, bf16[32,4096]{1,0:T(8,128)(2,1)}, u32[]{:S(2)}, u32[]{:S(2)}) collective-permute-start(bf16[32,4096]{1,0:T(8,128)(2,1)} %get-tuple-element.33), channel_id=1, source_target_pairs={{0,1},{1,0},{2,3},{3,2},{4,5},{5,4},{6,7},{7,6},{8,9},{9,8},{10,11... | collective-permute-start | bytes 786440 | tf_op jit(solution)/shard_map/ppermute | solution.py:359
  26.7 9.4 %collective-permute-start.4 = (bf16[32,4096]{1,0:T(8,128)(2,1)}, bf16[32,4096]{1,0:T(8,128)(2,1)}, u32[]{:S(2)}, u32[]{:S(2)}) collective-permute-start(bf16[32,4096]{1,0:T(8,128)(2,1)} %get-tuple-element.34), channel_id=1, source_target_pairs={{0,1},{1,0},{2,3},{3,2},{4,5},{5,4},{6,7},{7,6},{8,9},{9,8},{10,11... | collective-permute-start | bytes 786440 | tf_op jit(solution)/shard_map/ppermute | solution.py:359
  26.8 9.3 %collective-permute-start.5 = (bf16[32,4096]{1,0:T(8,128)(2,1)}, bf16[32,4096]{1,0:T(8,128)(2,1)}, u32[]{:S(2)}, u32[]{:S(2)}) collective-permute-start(bf16[32,4096]{1,0:T(8,128)(2,1)} %get-tuple-element.35), channel_id=1, source_target_pairs={{0,1},{1,0},{2,3},{3,2},{4,5},{5,4},{6,7},{7,6},{8,9},{9,8},{10,11... | collective-permute-start | bytes 786440 | tf_op jit(solution)/shard_map/ppermute | solution.py:359
  28.7 1.2 %copy-start.10 = (bf16[64,16,512]{2,1,0:T(8,128)(2,1)S(1)}, bf16[64,16,512]{2,1,0:T(8,128)(2,1)}, u32[]{:S(2)}) copy-start(bf16[64,16,512]{2,1,0:T(8,128)(2,1)} %param.10) | copy-start | bytes 3145732
  31.4 0.8 %copy-start.6 = (bf16[1024,256]{1,0:T(8,128)(2,1)}, bf16[1024,256]{1,0:T(8,128)(2,1)S(1)}, u32[]{:S(2)}) copy-start(bf16[1024,256]{1,0:T(8,128)(2,1)S(1)} %get-tuple-element.46.left_ref) | copy-start | bytes 1572868
  32.2 29.7 %all-to-all-start.1 = ((bf16[16,16,768]{2,1,0:T(8,128)(2,1)}), bf16[16,16,768]{2,1,0:T(8,128)(2,1)S(1)}, u32[]{:S(2)}, u32[]{:S(2)}) async-start(bf16[16,16,768]{2,1,0:T(8,128)(2,1)} %get-tuple-element.26), calls=%async_computation.1 | async-start | bytes 786432 | tf_op jit(solution)/shard_map/all_to_all | solution.py:378
  36.0 24.1 %copy-start.7 = (bf16[1024,256]{1,0:T(8,128)(2,1)S(1)}, bf16[1024,256]{1,0:T(8,128)(2,1)}, u32[]{:S(2)}) copy-start(bf16[1024,256]{1,0:T(8,128)(2,1)} %copy-done.6) | copy-start | bytes 1572868
  38.2 23.6 %copy-start.1 = (bf16[640,256]{1,0:T(8,128)(2,1)S(1)}, bf16[640,256]{1,0:T(8,128)(2,1)}, u32[]{:S(2)}) copy-start(bf16[640,256]{1,0:T(8,128)(2,1)} %cot_ref.1) | copy-start | bytes 983044
  38.2 16.5 %collective-permute-start.9 = (bf16[64,4096]{1,0:T(8,128)(2,1)S(1)}, bf16[64,4096]{1,0:T(8,128)(2,1)S(1)}, u32[]{:S(2)}, u32[]{:S(2)}) collective-permute-start(bf16[64,4096]{1,0:T(8,128)(2,1)S(1)} %get-tuple-element.41), channel_id=1, source_target_pairs={{0,2},{1,3},{2,0},{3,1},{4,6},{5,7},{6,4},{7,5},{8,10},{9,11},{10,... | collective-permute-start | bytes 1572872 | tf_op jit(solution)/shard_map/ppermute | solution.py:309
  40.2 19.1 %collective-permute-start.6 = (bf16[16,4096]{1,0:T(8,128)(2,1)S(1)}, bf16[16,4096]{1,0:T(8,128)(2,1)S(1)}, u32[]{:S(2)}, u32[]{:S(2)}) collective-permute-start(bf16[16,4096]{1,0:T(8,128)(2,1)S(1)} %get-tuple-element.37), channel_id=1, source_target_pairs={{0,4},{1,5},{2,6},{3,7},{4,0},{5,1},{6,2},{7,3},{8,12},{9,13},{10,... | collective-permute-start | bytes 393224 | tf_op jit(solution)/shard_map/ppermute | solution.py:309
  41.6 22.3 %collective-permute-start.7 = (bf16[16,4096]{1,0:T(8,128)(2,1)}, bf16[16,4096]{1,0:T(8,128)(2,1)S(1)}, u32[]{:S(2)}, u32[]{:S(2)}) collective-permute-start(bf16[16,4096]{1,0:T(8,128)(2,1)} %get-tuple-element.38), channel_id=1, source_target_pairs={{0,8},{1,9},{2,10},{3,11},{4,12},{5,13},{6,14},{7,15},{8,0},{9,1},... | collective-permute-start | bytes 393224 | tf_op jit(solution)/shard_map/ppermute | solution.py:309
  44.0 20.0 %collective-permute-start.8 = (bf16[16,4096]{1,0:T(8,128)(2,1)}, bf16[16,4096]{1,0:T(8,128)(2,1)S(1)}, u32[]{:S(2)}, u32[]{:S(2)}) collective-permute-start(bf16[16,4096]{1,0:T(8,128)(2,1)} %get-tuple-element.39), channel_id=1, source_target_pairs={{0,12},{1,13},{2,14},{3,15},{4,8},{5,9},{6,10},{7,11},{8,4},{9,5},... | collective-permute-start | bytes 393224 | tf_op jit(solution)/shard_map/ppermute | solution.py:309
  55.5 8.4 %collective-permute-start.10 = (bf16[16,4096]{1,0:T(8,128)(2,1)}, bf16[16,4096]{1,0:T(8,128)(2,1)S(1)}, u32[]{:S(2)}, u32[]{:S(2)}) collective-permute-start(bf16[16,4096]{1,0:T(8,128)(2,1)} %get-tuple-element.43), channel_id=1, source_target_pairs={{0,4},{1,5},{2,6},{3,7},{4,0},{5,1},{6,2},{7,3},{8,12},{9,13},{10,... | collective-permute-start | bytes 393224 | tf_op jit(solution)/shard_map/ppermute | solution.py:309
  57.7 12.6 %collective-permute-start.11 = (bf16[16,4096]{1,0:T(8,128)(2,1)}, bf16[16,4096]{1,0:T(8,128)(2,1)S(1)}, u32[]{:S(2)}, u32[]{:S(2)}) collective-permute-start(bf16[16,4096]{1,0:T(8,128)(2,1)} %get-tuple-element.44), channel_id=1, source_target_pairs={{0,8},{1,9},{2,10},{3,11},{4,12},{5,13},{6,14},{7,15},{8,0},{9,1},... | collective-permute-start | bytes 393224 | tf_op jit(solution)/shard_map/ppermute | solution.py:309
  59.2 11.2 %collective-permute-start.12 = (bf16[16,4096]{1,0:T(8,128)(2,1)}, bf16[16,4096]{1,0:T(8,128)(2,1)S(1)}, u32[]{:S(2)}, u32[]{:S(2)}) collective-permute-start(bf16[16,4096]{1,0:T(8,128)(2,1)} %get-tuple-element.45), channel_id=1, source_target_pairs={{0,12},{1,13},{2,14},{3,15},{4,8},{5,9},{6,10},{7,11},{8,4},{9,5},... | collective-permute-start | bytes 393224 | tf_op jit(solution)/shard_map/ppermute | solution.py:309

commit v7 on v6

--- a/solution.py
+++ b/solution.py
@@ -185,18 +185,21 @@
     mask_ref[...] = mask_by_column(lens_ref, slots_ref, mask_ref.shape[1], rank).astype(BF)
 
 
-def middle_kernel(rank, mask_ref, recv_ref, down_ref, send_hbm, left_ref, send_ref, sem):
+def middle_kernel(rank, mask_ref, recv_ref, down_hbm, send_hbm, back_ref, send_ref, down_ref, sem):
+    fetch = pltpu.make_async_copy(down_hbm, down_ref, sem)
+    fetch.start()
     tp, own, wide = recv_ref.shape
     rows = tp * own
     share = wide - rows
     mask = mask_ref[...].astype(F32)
     normed = recv_ref[:, :, :share].reshape(rows, share)
-    every = lax.dot_general(down_ref[...], normed, NT, preferred_element_type=F32) * mask
-    slots = every.shape[0] // rank
-    low = jnp.sum(every.reshape(slots, rank, rows), axis=0).astype(BF)
+    slots = mask.shape[0] // rank
     back = jnp.sum(recv_ref[:, :, share:].astype(F32), axis=0).astype(BF).astype(F32)
     left = (mask.reshape(slots, rank, rows) * back[None]).reshape(slots * rank, rows).astype(BF)
-    left_ref[...] = left
+    back_ref[...] = back
+    fetch.wait()
+    every = lax.dot_general(down_ref[...], normed, NT, preferred_element_type=F32) * mask
+    low = jnp.sum(every.reshape(slots, rank, rows), axis=0).astype(BF)
     term = SCALE * lax.dot_general(left, down_ref[...], TN, preferred_element_type=F32)
     send_ref[:, :, :share] = term.astype(BF).reshape(tp, own, share)
     for q in range(tp):
@@ -206,12 +209,15 @@
     copy.wait()
 
 
-def down_kernel(left_ref, recv_ref, out_ref):
+def down_kernel(rank, mask_ref, back_ref, recv_ref, out_ref):
     tp, own, wide = recv_ref.shape
     rows = tp * own
     share = wide - rows
     normed = recv_ref[:, :, :share].reshape(rows, share)
-    out_ref[...] = SCALE * jnp.dot(left_ref[...], normed, preferred_element_type=F32)
+    mask = mask_ref[...].astype(F32)
+    slots = mask.shape[0] // rank
+    left = (mask.reshape(slots, rank, rows) * back_ref[...][None]).reshape(slots * rank, rows).astype(BF)
+    out_ref[...] = SCALE * jnp.dot(left, normed, preferred_element_type=F32)
 
 
 def up_kernel(rank, mask_ref, recv_ref, cot_ref, out_ref):
@@ -346,7 +352,8 @@
 
     last = len(stages) - 1
     held_a = exchange(0, parts_a)
-    (cut_a,), _ = summed([held_a], [1])
+    total = sum(x.astype(F32) for x in held_a).astype(BF)
+    cut_a = jnp.split(total, len(stages[1]), axis=0)
     (mask,) = call(functools.partial(mask_kernel, rank), [shape((count * rank, rows))], [VMEM, VMEM])(lens, slot)
     recv = lax.all_to_all(send, "tp", split_axis=0, concat_axis=0, tiled=True)
     cut = 2 * len(stages[1])
@@ -366,23 +373,23 @@
         held_b = exchange(stage, cut_b)
     chunks = [held_a, held_b]
 
-    send2, left = call(
+    send2, back = call(
         functools.partial(middle_kernel, rank),
-        (shape((tp, own, share + rows)), shape((count * rank, rows))),
-        [VMEM] * 3,
-        scratch=[pltpu.VMEM((tp, own, share + rows), BF), dma],
+        (shape((tp, own, share + rows)), shape((rank, rows), F32)),
+        [VMEM, VMEM, HBM],
+        scratch=[pltpu.VMEM((tp, own, share + rows), BF), pltpu.VMEM((count * rank, share), BF), dma],
         out_specs=[HBM, VMEM],
         flops=4 * rows * share * count * rank,
         nbytes=3 << 20,
-    )(mask, recv, down_flat)
+    )(mask, recv, pltpu.with_memory_space_constraint(down_flat, pltpu.HBM))
     recv2 = lax.all_to_all(send2, "tp", split_axis=0, concat_axis=0, tiled=True)
     down_grad = call(
-        down_kernel,
+        functools.partial(down_kernel, rank),
         shape((count * rank, share), F32),
-        [VMEM] * 2,
+        [VMEM] * 3,
         flops=2 * rows * share * count * rank,
         nbytes=3 << 20,
-    )(left, recv)
+    )(mask, back, recv)
     up_grad = call(
         functools.partial(up_kernel, rank),
         shape((columns, count * rank), F32),

time: 72 us -> 70.7 us (0.982)
  local copies, waits for them, and re-layouts: 5.19 us -> 1.86 us
  other arithmetic: 0 us -> 1.47 us
  waiting for transfers between devices: 17.5 us -> 18.3 us
    unnamed x22 -> x12, local copies, waits for them, and re-layouts: 5.19 us -> 0.99 us
    convert_element_type x0 -> x1, other arithmetic: none -> 1.47 us  [body(): total = sum((x.astype(F32) for x in held_a)).astype(BF)]
    pallas_call x1, Pallas kernels: 1.52 us -> 2.72 us  [body(): call(functools.partial(middle_kernel, rank), (shape((tp, own, share + row...]
    pallas_call x3 -> x2, Pallas kernels: 3.89 us -> 2.9 us  [summed(): call(functools.partial(sum_kernel, [(len(g), c) for g, c in zip(groups, c...]
    split x0 -> x1, local copies, waits for them, and re-layouts: none -> 0.88 us  [body(): cut_a = jnp.split(total, len(stages[1]), axis=0)]
    all_to_all x1, waiting for transfers between devices: 0.86 us -> 1.68 us  [body(): recv = lax.all_to_all(send, 'tp', split_axis=0, concat_axis=0, tiled=True)]
  transfers between devices with their start and end apart: 15 -> 15, of which waited for: 3 -> 4; matrix products, arithmetic and copies ran while one was open for 0% -> 3% of each run, Pallas kernels for 23% -> 24%
where the time goes in v7:
time: 70.7 us; the launch traced here: 70.2 us
  starting transfers between devices  24.9 us (35%)
  Pallas kernels  23 us (33%)
  waiting for transfers between devices  18.3 us (26%)
  local copies, waits for them, and re-layouts  1.86 us (3%)
  other arithmetic  1.47 us (2%)
  between operations  0.78 us (1%)
    ppermute x9, waiting for transfers between devices, exchange(): lax.ppermute(part, 'tp', pairs(m))  16.6 us
    ppermute x9, starting transfers between devices, exchange(): lax.ppermute(part, 'tp', pairs(m))  13.2 us
    all_to_all x1, starting transfers between devices, body(): recv = lax.all_to_all(send, 'tp', split_axis=0, concat_axis=0, tiled=True)  7.06 us
    pallas_call x1, Pallas kernels, body(): call(functools.partial(first_kernel, order, own, block), [shape((rows, co...  4.84 us
    pallas_call x1, Pallas kernels, body(): call(functools.partial(second_kernel, half, block), [shape((each, width -...  4.58 us
    all_to_all x1, starting transfers between devices, body(): recv2 = lax.all_to_all(send2, 'tp', split_axis=0, concat_axis=0, tiled=True)  3.57 us
    pallas_call x2, Pallas kernels, summed(): call(functools.partial(sum_kernel, [(len(g), c) for g, c in zip(groups, c...  2.9 us
    pallas_call x1, Pallas kernels, body(): call(functools.partial(middle_kernel, rank), (shape((tp, own, share + row...  2.72 us
  transfers between devices with their start and end apart: 15, of which 4 were waited for; matrix products, arithmetic and copies ran while one was open for 3% of the time, Pallas kernels for 24%

profile of v7, /device:TPU:0, one launch (start us, length us, event | category | flops | bytes accessed | tf_op | source)
XLA Modules:
  0.0 70.2 jit_solution(5754632737231923258)
XLA Ops:
  0.6 0.0 copy-start
  0.6 1.0 %copy-done = bf16[640,256]{1,0:T(8,128)(2,1)S(1)} copy-done((bf16[640,256]{1,0:T(8,128)(2,1)S(1)}, bf16[640,256]{1,0:T(8,128)(2,1)}, u32[]{:S(2)}) %copy-start) | copy-done | bytes 327704
  1.6 0.0 copy-start.2
  1.6 0.0 copy-start.3
  1.6 0.0 copy-start.4
  1.6 0.0 copy-start.5
  1.6 4.8 %shard_map.95 = (bf16[256,640]{1,0:T(8,128)(2,1)S(1)}, bf16[128,4096]{1,0:T(8,128)(2,1)S(1)}, bf16[128,4096]{1,0:T(8,128)(2,1)}) custom-call(s32[1]{0:T(128)} %bitcast.2.me_ref, bf16[640,256]{1,0:T(8,128)(2,1)S(1)} %copy-done, bf16[640,8192]{1,0:T(8,128)(2,1)} %weight_hbm.3), custom_call_target="tpu_custom_call" | custom-call | flops 1342177280 | bytes 5242880 | tf_op jit(solution)/shard_map/pallas_call | solution.py:295
  6.5 0.5 collective-permute-start
  7.0 0.0 copy-done.2
  7.0 0.0 copy-done.3
  7.0 0.0 copy-done.4
  7.0 0.0 copy-done.5
  7.0 2.4 %shard_map.96 = bf16[16,16,768]{2,1,0:T(8,128)(2,1)} custom-call(s32[1]{0:T(128)} %bitcast.2.me_ref, s32[1,64]{1,0:T(1,128)S(1)} %bitcast.5, s32[1,64]{1,0:T(1,128)S(1)} %bitcast.7, bf16[256,640]{1,0:T(8,128)(2,1)S(1)} %get-tuple-element.23.cotp_ref, bf16[16,8192]{1,0:T(8,128)(2,1)S(1)} %copy-done.3, bf16[640,1024]{1,0:T(8,128)(2,1)S(1)} %copy-done.2), custom_call_target="tpu_custom_call" | custom-call | tf_op jit(solution)/shard_map/pallas_call | solution.py:339
  9.4 7.1 %all-to-all-start = ((bf16[16,16,768]{2,1,0:T(8,128)(2,1)}), bf16[16,16,768]{2,1,0:T(8,128)(2,1)S(1)}, u32[]{:S(2)}, u32[]{:S(2)}) async-start(bf16[16,16,768]{2,1,0:T(8,128)(2,1)} %shard_map.96), calls=%async_computation | async-start | bytes 786432 | tf_op jit(solution)/shard_map/all_to_all | solution.py:358
  16.4 0.0 collective-permute-done
  16.4 1.5 %add_convert_fusion = bf16[128,4096]{1,0:T(8,128)(2,1)S(1)} fusion(bf16[128,4096]{1,0:T(8,128)(2,1)} %collective-permute-done, bf16[128,4096]{1,0:T(8,128)(2,1)S(1)} %get-tuple-element.25), kind=kLoop, calls=%fused_computation | loop fusion | flops 2097152 | bytes 3145728 | tf_op jit(solution)/shard_map/convert_element_type | solution.py:355
  17.9 0.9 %fusion = (bf16[64,4096]{1,0:T(8,128)(2,1)}, bf16[64,4096]{1,0:T(8,128)(2,1)S(1)}) fusion(bf16[128,4096]{1,0:T(8,128)(2,1)S(1)} %add_convert_fusion), kind=kLoop, calls=%fused_computation.1 | loop fusion | bytes 2097152 | tf_op jit(solution)/shard_map/split | solution.py:356
  18.8 1.9 %collective-permute-start.1 = (bf16[64,4096]{1,0:T(8,128)(2,1)}, bf16[64,4096]{1,0:T(8,128)(2,1)}, u32[]{:S(2)}, u32[]{:S(2)}) collective-permute-start(bf16[64,4096]{1,0:T(8,128)(2,1)} %get-tuple-element.43), channel_id=1, source_target_pairs={{0,2},{1,3},{2,0},{3,1},{4,6},{5,7},{6,4},{7,5},{8,10},{9,11},{10,... | collective-permute-start | bytes 1572872 | tf_op jit(solution)/shard_map/ppermute | solution.py:315
  20.7 4.6 %shard_map.98 = (bf16[128,4096]{1,0:T(8,128)(2,1)S(1)}, bf16[32,4096]{1,0:T(8,128)(2,1)}, bf16[32,4096]{1,0:T(8,128)(2,1)}, bf16[32,4096]{1,0:T(8,128)(2,1)}, bf16[32,4096]{1,0:T(8,128)(2,1)}) custom-call(bf16[256,640]{1,0:T(8,128)(2,1)S(1)} %get-tuple-element.23.cotp_ref, bf16[64,4096]{1,0:T(8,128)(2,1)S(1)} %get-tuple-element.44.after_hbm.refs_0_, ...), custom_call_target="tpu_custom_call" | custom-call | tf_op jit(solution)/shard_map/pallas_call | solution.py:360
  25.3 0.1 collective-permute-start.2
  25.4 0.5 collective-permute-start.3
  25.9 0.1 collective-permute-start.4
  26.0 0.4 collective-permute-start.5
  26.4 0.6 shard_map.94.mask_ref
  27.0 1.7 %all-to-all-done.recv_ref = bf16[16,16,768]{2,1,0:T(8,128)(2,1)S(1)} async-done(((bf16[16,16,768]{2,1,0:T(8,128)(2,1)}), bf16[16,16,768]{2,1,0:T(8,128)(2,1)S(1)}, u32[]{:S(2)}, u32[]{:S(2)}) %all-to-all-start) | async-done | bytes 393248 | tf_op jit(solution)/shard_map/all_to_all | solution.py:358
  28.7 2.7 %shard_map.97 = (bf16[16,16,768]{2,1,0:T(8,128)(2,1)}, f32[16,256]{1,0:T(8,128)S(1)}) custom-call(bf16[1024,256]{1,0:T(8,128)(2,1)S(1)} %shard_map.94.mask_ref, bf16[16,16,768]{2,1,0:T(8,128)(2,1)S(1)} %all-to-all-done.recv_ref, bf16[1024,512]{1,0:T(8,128)(2,1)} %bitcast.10), custom_call_target="tpu_custom_call" | custom-call | flops 536870912 | bytes 3145728 | tf_op jit(solution)/shard_map/pallas_call | solution.py:376
  31.4 3.6 %all-to-all-start.1 = ((bf16[16,16,768]{2,1,0:T(8,128)(2,1)}), bf16[16,16,768]{2,1,0:T(8,128)(2,1)S(1)}, u32[]{:S(2)}, u32[]{:S(2)}) async-start(bf16[16,16,768]{2,1,0:T(8,128)(2,1)} %get-tuple-element.24), calls=%async_computation.1 | async-start | bytes 786432 | tf_op jit(solution)/shard_map/all_to_all | solution.py:385
  35.0 0.0 collective-permute-done.2.refs_3_
  35.0 0.0 collective-permute-done.3.refs_4_
  35.0 0.0 collective-permute-done.4.refs_5_
  35.0 0.0 collective-permute-done.5.refs_6_
  35.0 0.5 collective-permute-done.1.refs_1_
  35.5 2.1 %shard_map.99 = (bf16[16,4096]{1,0:T(8,128)(2,1)S(1)}, bf16[16,4096]{1,0:T(8,128)(2,1)S(1)}, bf16[16,4096]{1,0:T(8,128)(2,1)}, bf16[16,4096]{1,0:T(8,128)(2,1)},...) custom-call(bf16[64,4096]{1,0:T(8,128)(2,1)S(1)} %get-tuple-element.44.after_hbm.refs_0_, ...), custom_call_target="tpu_custom_call" | custom-call | bytes 6291456 | tf_op jit(solution)/shard_map/pallas_call | solution.py:324
  37.6 0.0 copy-start.1
  37.6 1.8 %collective-permute-start.9 = (bf16[64,4096]{1,0:T(8,128)(2,1)S(1)}, bf16[64,4096]{1,0:T(8,128)(2,1)S(1)}, u32[]{:S(2)}, u32[]{:S(2)}) collective-permute-start(bf16[64,4096]{1,0:T(8,128)(2,1)S(1)} %get-tuple-element.37), channel_id=1, source_target_pairs={{0,2},{1,3},{2,0},{3,1},{4,6},{5,7},{6,4},{7,5},{8,10},{9,11},{10,... | collective-permute-start | bytes 1572872 | tf_op jit(solution)/shard_map/ppermute | solution.py:315
  39.3 1.5 %collective-permute-start.6 = (bf16[16,4096]{1,0:T(8,128)(2,1)S(1)}, bf16[16,4096]{1,0:T(8,128)(2,1)S(1)}, u32[]{:S(2)}, u32[]{:S(2)}) collective-permute-start(bf16[16,4096]{1,0:T(8,128)(2,1)S(1)} %get-tuple-element.33), channel_id=1, source_target_pairs={{0,4},{1,5},{2,6},{3,7},{4,0},{5,1},{6,2},{7,3},{8,12},{9,13},{10,... | collective-permute-start | bytes 393224 | tf_op jit(solution)/shard_map/ppermute | solution.py:315
  40.8 2.0 %collective-permute-start.7 = (bf16[16,4096]{1,0:T(8,128)(2,1)}, bf16[16,4096]{1,0:T(8,128)(2,1)S(1)}, u32[]{:S(2)}, u32[]{:S(2)}) collective-permute-start(bf16[16,4096]{1,0:T(8,128)(2,1)} %get-tuple-element.34), channel_id=1, source_target_pairs={{0,8},{1,9},{2,10},{3,11},{4,12},{5,13},{6,14},{7,15},{8,0},{9,1},... | collective-permute-start | bytes 393224 | tf_op jit(solution)/shard_map/ppermute | solution.py:315
  42.8 0.9 %collective-permute-start.8 = (bf16[16,4096]{1,0:T(8,128)(2,1)}, bf16[16,4096]{1,0:T(8,128)(2,1)S(1)}, u32[]{:S(2)}, u32[]{:S(2)}) collective-permute-start(bf16[16,4096]{1,0:T(8,128)(2,1)} %get-tuple-element.35), channel_id=1, source_target_pairs={{0,12},{1,13},{2,14},{3,15},{4,8},{5,9},{6,10},{7,11},{8,4},{9,5},... | collective-permute-start | bytes 393224 | tf_op jit(solution)/shard_map/ppermute | solution.py:315
  43.7 9.9 %collective-permute-done.9.refs_1_ = bf16[64,4096]{1,0:T(8,128)(2,1)S(1)} collective-permute-done((bf16[64,4096]{1,0:T(8,128)(2,1)S(1)}, bf16[64,4096]{1,0:T(8,128)(2,1)S(1)}, u32[]{:S(2)}, u32[]{:S(2)}) %collective-permute-start.9) | collective-permute-done | bytes 524320 | tf_op jit(solution)/shard_map/ppermute | solution.py:315
  53.6 0.8 %shard_map.100 = (bf16[16,4096]{1,0:T(8,128)(2,1)S(1)}, bf16[16,4096]{1,0:T(8,128)(2,1)}, bf16[16,4096]{1,0:T(8,128)(2,1)}, bf16[16,4096]{1,0:T(8,128)(2,1)}) custom-call(bf16[64,4096]{1,0:T(8,128)(2,1)S(1)} %get-tuple-element.36.refs_0_, bf16[64,4096]{1,0:T(8,128)(2,1)S(1)} %collective-permute-done.9.refs_1_), custom_call_target="tpu_custom_call" | custom-call | bytes 2097152 | tf_op jit(solution)/shard_map/pallas_call | solution.py:324
  54.4 2.2 %collective-permute-start.10 = (bf16[16,4096]{1,0:T(8,128)(2,1)}, bf16[16,4096]{1,0:T(8,128)(2,1)S(1)}, u32[]{:S(2)}, u32[]{:S(2)}) collective-permute-start(bf16[16,4096]{1,0:T(8,128)(2,1)} %get-tuple-element.39), channel_id=1, source_target_pairs={{0,4},{1,5},{2,6},{3,7},{4,0},{5,1},{6,2},{7,3},{8,12},{9,13},{10,... | collective-permute-start | bytes 393224 | tf_op jit(solution)/shard_map/ppermute | solution.py:315
  56.7 1.5 %collective-permute-start.11 = (bf16[16,4096]{1,0:T(8,128)(2,1)}, bf16[16,4096]{1,0:T(8,128)(2,1)S(1)}, u32[]{:S(2)}, u32[]{:S(2)}) collective-permute-start(bf16[16,4096]{1,0:T(8,128)(2,1)} %get-tuple-element.40), channel_id=1, source_target_pairs={{0,8},{1,9},{2,10},{3,11},{4,12},{5,13},{6,14},{7,15},{8,0},{9,1},... | collective-permute-start | bytes 393224 | tf_op jit(solution)/shard_map/ppermute | solution.py:315
  58.2 0.0 collective-permute-done.6.refs_1_
  58.2 0.9 %collective-permute-start.12 = (bf16[16,4096]{1,0:T(8,128)(2,1)}, bf16[16,4096]{1,0:T(8,128)(2,1)S(1)}, u32[]{:S(2)}, u32[]{:S(2)}) collective-permute-start(bf16[16,4096]{1,0:T(8,128)(2,1)} %get-tuple-element.41), channel_id=1, source_target_pairs={{0,12},{1,13},{2,14},{3,15},{4,8},{5,9},{6,10},{7,11},{8,4},{9,5},... | collective-permute-start | bytes 393224 | tf_op jit(solution)/shard_map/ppermute | solution.py:315
  59.0 1.8 %shard_map.102 = f32[1024,512]{1,0:T(8,128)} custom-call(bf16[1024,256]{1,0:T(8,128)(2,1)S(1)} %shard_map.94.mask_ref, f32[16,256]{1,0:T(8,128)S(1)} %get-tuple-element.42.back_ref, bf16[16,16,768]{2,1,0:T(8,128)(2,1)S(1)} %all-to-all-done.recv_ref), custom_call_target="tpu_custom_call" | custom-call | flops 268435456 | bytes 3145728 | tf_op jit(solution)/shard_map/pallas_call | solution.py:386
  60.8 0.0 all-to-all-done.1.recv_ref
  60.8 0.0 copy-done.1
  60.8 2.1 %shard_map.103 = f32[640,1024]{1,0:T(8,128)} custom-call(bf16[1024,256]{1,0:T(8,128)(2,1)S(1)} %shard_map.94.mask_ref, bf16[16,16,768]{2,1,0:T(8,128)(2,1)S(1)} %all-to-all-done.1.recv_ref, bf16[640,256]{1,0:T(8,128)(2,1)S(1)} %copy-done.1), custom_call_target="tpu_custom_call" | custom-call | flops 335544320 | bytes 3145728 | tf_op jit(solution)/shard_map/pallas_call | solution.py:393
  62.9 0.0 collective-permute-done.7.refs_2_
  62.9 0.0 collective-permute-done.8.refs_3_
  62.9 0.0 collective-permute-done.10.refs_5_
  62.9 6.2 %collective-permute-done.11.refs_6_ = bf16[16,4096]{1,0:T(8,128)(2,1)S(1)} collective-permute-done((bf16[16,4096]{1,0:T(8,128)(2,1)}, bf16[16,4096]{1,0:T(8,128)(2,1)S(1)}, u32[]{:S(2)}, u32[]{:S(2)}) %collective-permute-start.11) | collective-permute-done | bytes 131104 | tf_op jit(solution)/shard_map/ppermute | solution.py:315
  69.1 0.0 collective-permute-done.12.refs_7_
  69.1 1.2 %shard_map.101 = bf16[16,8192]{1,0:T(8,128)(2,1)} custom-call(bf16[16,16,768]{2,1,0:T(8,128)(2,1)S(1)} %all-to-all-done.1.recv_ref, bf16[16,8192]{1,0:T(8,128)(2,1)S(1)} %copy-done.3, bf16[16,4096]{1,0:T(8,128)(2,1)S(1)} %get-tuple-element.32.refs_0_, bf16[16,4096]{1,0:T(8,128)(2,1)S(1)} %collective-permute-done.6.refs_1_, ...), custom_call_target="tpu_custom_call" | custom-call | bytes 2097152 | tf_op jit(solution)/shard_map/pallas_call | solution.py:401
Async XLA Ops:
  0.6 1.0 %copy-start = (bf16[640,256]{1,0:T(8,128)(2,1)S(1)}, bf16[640,256]{1,0:T(8,128)(2,1)}, u32[]{:S(2)}) copy-start(bf16[640,256]{1,0:T(8,128)(2,1)} %cot_ref.1) | copy-start | bytes 983044
  1.6 5.4 %copy-start.2 = (bf16[640,1024]{1,0:T(8,128)(2,1)S(1)}, bf16[640,1024]{1,0:T(8,128)(2,1)}, u32[]{:S(2)}) copy-start(bf16[640,1024]{1,0:T(8,128)(2,1)} %up_hbm.1) | copy-start | bytes 3932164
  1.6 5.4 %copy-start.3 = (bf16[16,8192]{1,0:T(8,128)(2,1)S(1)}, bf16[16,8192]{1,0:T(8,128)(2,1)}, u32[]{:S(2)}) copy-start(bf16[16,8192]{1,0:T(8,128)(2,1)} %tok_ref.1) | copy-start | bytes 786436
  1.6 5.4 %copy-start.4 = (s32[64]{0:T(128)S(1)}, s32[64]{0:T(128)}, u32[]{:S(2)}) copy-start(s32[64]{0:T(128)} %param.12) | copy-start | bytes 772
  1.6 5.4 %copy-start.5 = (s32[64]{0:T(128)S(1)}, s32[64]{0:T(128)}, u32[]{:S(2)}) copy-start(s32[64]{0:T(128)} %param.13) | copy-start | bytes 772
  6.5 10.0 %collective-permute-start = (bf16[128,4096]{1,0:T(8,128)(2,1)}, bf16[128,4096]{1,0:T(8,128)(2,1)}, u32[]{:S(2)}, u32[]{:S(2)}) collective-permute-start(bf16[128,4096]{1,0:T(8,128)(2,1)} %get-tuple-element.26), channel_id=1, source_target_pairs={{0,1},{1,0},{2,3},{3,2},{4,5},{5,4},{6,7},{7,6},{8,9},{9,8},{10,11... | collective-permute-start | bytes 3145736 | tf_op jit(solution)/shard_map/ppermute | solution.py:315
  9.4 19.3 %all-to-all-start = ((bf16[16,16,768]{2,1,0:T(8,128)(2,1)}), bf16[16,16,768]{2,1,0:T(8,128)(2,1)S(1)}, u32[]{:S(2)}, u32[]{:S(2)}) async-start(bf16[16,16,768]{2,1,0:T(8,128)(2,1)} %shard_map.96), calls=%async_computation | async-start | bytes 786432 | tf_op jit(solution)/shard_map/all_to_all | solution.py:358
  18.8 16.7 %collective-permute-start.1 = (bf16[64,4096]{1,0:T(8,128)(2,1)}, bf16[64,4096]{1,0:T(8,128)(2,1)}, u32[]{:S(2)}, u32[]{:S(2)}) collective-permute-start(bf16[64,4096]{1,0:T(8,128)(2,1)} %get-tuple-element.43), channel_id=1, source_target_pairs={{0,2},{1,3},{2,0},{3,1},{4,6},{5,7},{6,4},{7,5},{8,10},{9,11},{10,... | collective-permute-start | bytes 1572872 | tf_op jit(solution)/shard_map/ppermute | solution.py:315
  25.3 9.7 %collective-permute-start.2 = (bf16[32,4096]{1,0:T(8,128)(2,1)}, bf16[32,4096]{1,0:T(8,128)(2,1)S(1)}, u32[]{:S(2)}, u32[]{:S(2)}) collective-permute-start(bf16[32,4096]{1,0:T(8,128)(2,1)} %get-tuple-element.28), channel_id=1, source_target_pairs={{0,1},{1,0},{2,3},{3,2},{4,5},{5,4},{6,7},{7,6},{8,9},{9,8},{10,11... | collective-permute-start | bytes 786440 | tf_op jit(solution)/shard_map/ppermute | solution.py:366
  25.4 9.6 %collective-permute-start.3 = (bf16[32,4096]{1,0:T(8,128)(2,1)}, bf16[32,4096]{1,0:T(8,128)(2,1)}, u32[]{:S(2)}, u32[]{:S(2)}) collective-permute-start(bf16[32,4096]{1,0:T(8,128)(2,1)} %get-tuple-element.29), channel_id=1, source_target_pairs={{0,1},{1,0},{2,3},{3,2},{4,5},{5,4},{6,7},{7,6},{8,9},{9,8},{10,11... | collective-permute-start | bytes 786440 | tf_op jit(solution)/shard_map/ppermute | solution.py:366
  25.9 9.1 %collective-permute-start.4 = (bf16[32,4096]{1,0:T(8,128)(2,1)}, bf16[32,4096]{1,0:T(8,128)(2,1)}, u32[]{:S(2)}, u32[]{:S(2)}) collective-permute-start(bf16[32,4096]{1,0:T(8,128)(2,1)} %get-tuple-element.30), channel_id=1, source_target_pairs={{0,1},{1,0},{2,3},{3,2},{4,5},{5,4},{6,7},{7,6},{8,9},{9,8},{10,11... | collective-permute-start | bytes 786440 | tf_op jit(solution)/shard_map/ppermute | solution.py:366
  26.0 9.0 %collective-permute-start.5 = (bf16[32,4096]{1,0:T(8,128)(2,1)}, bf16[32,4096]{1,0:T(8,128)(2,1)}, u32[]{:S(2)}, u32[]{:S(2)}) collective-permute-start(bf16[32,4096]{1,0:T(8,128)(2,1)} %get-tuple-element.31), channel_id=1, source_target_pairs={{0,1},{1,0},{2,3},{3,2},{4,5},{5,4},{6,7},{7,6},{8,9},{9,8},{10,11... | collective-permute-start | bytes 786440 | tf_op jit(solution)/shard_map/ppermute | solution.py:366
  31.4 29.4 %all-to-all-start.1 = ((bf16[16,16,768]{2,1,0:T(8,128)(2,1)}), bf16[16,16,768]{2,1,0:T(8,128)(2,1)S(1)}, u32[]{:S(2)}, u32[]{:S(2)}) async-start(bf16[16,16,768]{2,1,0:T(8,128)(2,1)} %get-tuple-element.24), calls=%async_computation.1 | async-start | bytes 786432 | tf_op jit(solution)/shard_map/all_to_all | solution.py:385
  37.6 23.2 %copy-start.1 = (bf16[640,256]{1,0:T(8,128)(2,1)S(1)}, bf16[640,256]{1,0:T(8,128)(2,1)}, u32[]{:S(2)}) copy-start(bf16[640,256]{1,0:T(8,128)(2,1)} %cot_ref.1) | copy-start | bytes 983044
  37.6 16.0 %collective-permute-start.9 = (bf16[64,4096]{1,0:T(8,128)(2,1)S(1)}, bf16[64,4096]{1,0:T(8,128)(2,1)S(1)}, u32[]{:S(2)}, u32[]{:S(2)}) collective-permute-start(bf16[64,4096]{1,0:T(8,128)(2,1)S(1)} %get-tuple-element.37), channel_id=1, source_target_pairs={{0,2},{1,3},{2,0},{3,1},{4,6},{5,7},{6,4},{7,5},{8,10},{9,11},{10,... | collective-permute-start | bytes 1572872 | tf_op jit(solution)/shard_map/ppermute | solution.py:315
  39.3 18.8 %collective-permute-start.6 = (bf16[16,4096]{1,0:T(8,128)(2,1)S(1)}, bf16[16,4096]{1,0:T(8,128)(2,1)S(1)}, u32[]{:S(2)}, u32[]{:S(2)}) collective-permute-start(bf16[16,4096]{1,0:T(8,128)(2,1)S(1)} %get-tuple-element.33), channel_id=1, source_target_pairs={{0,4},{1,5},{2,6},{3,7},{4,0},{5,1},{6,2},{7,3},{8,12},{9,13},{10,... | collective-permute-start | bytes 393224 | tf_op jit(solution)/shard_map/ppermute | solution.py:315
  40.8 22.0 %collective-permute-start.7 = (bf16[16,4096]{1,0:T(8,128)(2,1)}, bf16[16,4096]{1,0:T(8,128)(2,1)S(1)}, u32[]{:S(2)}, u32[]{:S(2)}) collective-permute-start(bf16[16,4096]{1,0:T(8,128)(2,1)} %get-tuple-element.34), channel_id=1, source_target_pairs={{0,8},{1,9},{2,10},{3,11},{4,12},{5,13},{6,14},{7,15},{8,0},{9,1},... | collective-permute-start | bytes 393224 | tf_op jit(solution)/shard_map/ppermute | solution.py:315
  42.8 20.0 %collective-permute-start.8 = (bf16[16,4096]{1,0:T(8,128)(2,1)}, bf16[16,4096]{1,0:T(8,128)(2,1)S(1)}, u32[]{:S(2)}, u32[]{:S(2)}) collective-permute-start(bf16[16,4096]{1,0:T(8,128)(2,1)} %get-tuple-element.35), channel_id=1, source_target_pairs={{0,12},{1,13},{2,14},{3,15},{4,8},{5,9},{6,10},{7,11},{8,4},{9,5},... | collective-permute-start | bytes 393224 | tf_op jit(solution)/shard_map/ppermute | solution.py:315
  54.4 8.5 %collective-permute-start.10 = (bf16[16,4096]{1,0:T(8,128)(2,1)}, bf16[16,4096]{1,0:T(8,128)(2,1)S(1)}, u32[]{:S(2)}, u32[]{:S(2)}) collective-permute-start(bf16[16,4096]{1,0:T(8,128)(2,1)} %get-tuple-element.39), channel_id=1, source_target_pairs={{0,4},{1,5},{2,6},{3,7},{4,0},{5,1},{6,2},{7,3},{8,12},{9,13},{10,... | collective-permute-start | bytes 393224 | tf_op jit(solution)/shard_map/ppermute | solution.py:315
  56.7 12.4 %collective-permute-start.11 = (bf16[16,4096]{1,0:T(8,128)(2,1)}, bf16[16,4096]{1,0:T(8,128)(2,1)S(1)}, u32[]{:S(2)}, u32[]{:S(2)}) collective-permute-start(bf16[16,4096]{1,0:T(8,128)(2,1)} %get-tuple-element.40), channel_id=1, source_target_pairs={{0,8},{1,9},{2,10},{3,11},{4,12},{5,13},{6,14},{7,15},{8,0},{9,1},... | collective-permute-start | bytes 393224 | tf_op jit(solution)/shard_map/ppermute | solution.py:315
  58.2 10.9 %collective-permute-start.12 = (bf16[16,4096]{1,0:T(8,128)(2,1)}, bf16[16,4096]{1,0:T(8,128)(2,1)S(1)}, u32[]{:S(2)}, u32[]{:S(2)}) collective-permute-start(bf16[16,4096]{1,0:T(8,128)(2,1)} %get-tuple-element.41), channel_id=1, source_target_pairs={{0,12},{1,13},{2,14},{3,15},{4,8},{5,9},{6,10},{7,11},{8,4},{9,5},... | collective-permute-start | bytes 393224 | tf_op jit(solution)/shard_map/ppermute | solution.py:315

commit v8 on v7

--- a/solution.py
+++ b/solution.py
@@ -352,8 +352,10 @@
 
     last = len(stages) - 1
     held_a = exchange(0, parts_a)
-    total = sum(x.astype(F32) for x in held_a).astype(BF)
-    cut_a = jnp.split(total, len(stages[1]), axis=0)
+    rows_cut = each // len(stages[1])
+    cut_a = [
+        sum(x[i * rows_cut : (i + 1) * rows_cut].astype(F32) for x in held_a).astype(BF) for i in range(len(stages[1]))
+    ]
     (mask,) = call(functools.partial(mask_kernel, rank), [shape((count * rank, rows))], [VMEM, VMEM])(lens, slot)
     recv = lax.all_to_all(send, "tp", split_axis=0, concat_axis=0, tiled=True)
     cut = 2 * len(stages[1])

time: 70.7 us -> 70.7 us (level)
  local copies, waits for them, and re-layouts: 1.86 us -> 0.99 us
  other arithmetic: 1.47 us -> 2.24 us
    split x1 -> x0, local copies, waits for them, and re-layouts: 0.88 us -> none  [body(): cut_a = jnp.split(total, len(stages[1]), axis=0)]
    convert_element_type x1, other arithmetic: 1.47 us -> 2.24 us  [body(): sum((x[i * rows_cut:(i + 1) * rows_cut].astype(F32) for x in held_a))]
where the time goes in v8:
time: 70.7 us; the launch traced here: 70.3 us
  starting transfers between devices  24.9 us (35%)
  Pallas kernels  23 us (33%)
  waiting for transfers between devices  18.4 us (26%)
  other arithmetic  2.24 us (3%)
  local copies, waits for them, and re-layouts  0.99 us (1%)
  between operations  0.77 us (1%)
    ppermute x9, waiting for transfers between devices, exchange(): lax.ppermute(part, 'tp', pairs(m))  16.6 us
    ppermute x9, starting transfers between devices, exchange(): lax.ppermute(part, 'tp', pairs(m))  13.2 us
    all_to_all x1, starting transfers between devices, body(): recv = lax.all_to_all(send, 'tp', split_axis=0, concat_axis=0, tiled=True)  7.06 us
    pallas_call x1, Pallas kernels, body(): call(functools.partial(first_kernel, order, own, block), [shape((rows, co...  4.84 us
    pallas_call x1, Pallas kernels, body(): call(functools.partial(second_kernel, half, block), [shape((each, width -...  4.58 us
    all_to_all x1, starting transfers between devices, body(): recv2 = lax.all_to_all(send2, 'tp', split_axis=0, concat_axis=0, tiled=True)  3.57 us
    pallas_call x2, Pallas kernels, summed(): call(functools.partial(sum_kernel, [(len(g), c) for g, c in zip(groups, c...  2.9 us
    pallas_call x1, Pallas kernels, body(): call(functools.partial(middle_kernel, rank), (shape((tp, own, share + row...  2.72 us
  transfers between devices with their start and end apart: 15, of which 4 were waited for; matrix products, arithmetic and copies ran while one was open for 3% of the time, Pallas kernels for 24%

profile of v8, /device:TPU:0, one launch (start us, length us, event | category | flops | bytes accessed | tf_op | source)
XLA Modules:
  0.0 70.3 jit_solution(11870678901664758803)
XLA Ops:
  0.6 0.0 copy-start
  0.6 1.0 %copy-done = bf16[640,256]{1,0:T(8,128)(2,1)S(1)} copy-done((bf16[640,256]{1,0:T(8,128)(2,1)S(1)}, bf16[640,256]{1,0:T(8,128)(2,1)}, u32[]{:S(2)}) %copy-start) | copy-done | bytes 327704
  1.6 0.0 copy-start.2
  1.6 0.0 copy-start.3
  1.6 0.0 copy-start.4
  1.6 0.0 copy-start.5
  1.6 4.8 %shard_map.95 = (bf16[256,640]{1,0:T(8,128)(2,1)S(1)}, bf16[128,4096]{1,0:T(8,128)(2,1)S(1)}, bf16[128,4096]{1,0:T(8,128)(2,1)}) custom-call(s32[1]{0:T(128)} %bitcast.2.me_ref, bf16[640,256]{1,0:T(8,128)(2,1)S(1)} %copy-done, bf16[640,8192]{1,0:T(8,128)(2,1)} %weight_hbm.3), custom_call_target="tpu_custom_call" | custom-call | flops 1342177280 | bytes 5242880 | tf_op jit(solution)/shard_map/pallas_call | solution.py:295
  6.5 0.5 collective-permute-start
  7.0 0.0 copy-done.2
  7.0 0.0 copy-done.3
  7.0 0.0 copy-done.4
  7.0 0.0 copy-done.5
  7.0 2.4 %shard_map.96 = bf16[16,16,768]{2,1,0:T(8,128)(2,1)} custom-call(s32[1]{0:T(128)} %bitcast.2.me_ref, s32[1,64]{1,0:T(1,128)S(1)} %bitcast.5, s32[1,64]{1,0:T(1,128)S(1)} %bitcast.7, bf16[256,640]{1,0:T(8,128)(2,1)S(1)} %get-tuple-element.23.cotp_ref, bf16[16,8192]{1,0:T(8,128)(2,1)S(1)} %copy-done.3, bf16[640,1024]{1,0:T(8,128)(2,1)S(1)} %copy-done.2), custom_call_target="tpu_custom_call" | custom-call | tf_op jit(solution)/shard_map/pallas_call | solution.py:339
  9.4 7.1 %all-to-all-start = ((bf16[16,16,768]{2,1,0:T(8,128)(2,1)}), bf16[16,16,768]{2,1,0:T(8,128)(2,1)S(1)}, u32[]{:S(2)}, u32[]{:S(2)}) async-start(bf16[16,16,768]{2,1,0:T(8,128)(2,1)} %shard_map.96), calls=%async_computation | async-start | bytes 786432 | tf_op jit(solution)/shard_map/all_to_all | solution.py:360
  16.4 0.0 collective-permute-done
  16.4 2.2 %add_convert_fusion = (bf16[64,4096]{1,0:T(8,128)(2,1)}, bf16[64,4096]{1,0:T(8,128)(2,1)S(1)}) fusion(bf16[128,4096]{1,0:T(8,128)(2,1)} %collective-permute-done, bf16[128,4096]{1,0:T(8,128)(2,1)S(1)} %get-tuple-element.25), kind=kLoop, calls=%fused_computation | loop fusion | flops 2097152 | bytes 3145728 | tf_op jit(solution)/shard_map/convert_element_type | solution.py:357
  18.7 1.9 %collective-permute-start.1 = (bf16[64,4096]{1,0:T(8,128)(2,1)}, bf16[64,4096]{1,0:T(8,128)(2,1)}, u32[]{:S(2)}, u32[]{:S(2)}) collective-permute-start(bf16[64,4096]{1,0:T(8,128)(2,1)} %get-tuple-element.43), channel_id=1, source_target_pairs={{0,2},{1,3},{2,0},{3,1},{4,6},{5,7},{6,4},{7,5},{8,10},{9,11},{10,... | collective-permute-start | bytes 1572872 | tf_op jit(solution)/shard_map/ppermute | solution.py:315
  20.6 4.6 %shard_map.98 = (bf16[128,4096]{1,0:T(8,128)(2,1)S(1)}, bf16[32,4096]{1,0:T(8,128)(2,1)}, bf16[32,4096]{1,0:T(8,128)(2,1)}, bf16[32,4096]{1,0:T(8,128)(2,1)}, bf16[32,4096]{1,0:T(8,128)(2,1)}) custom-call(bf16[256,640]{1,0:T(8,128)(2,1)S(1)} %get-tuple-element.23.cotp_ref, bf16[64,4096]{1,0:T(8,128)(2,1)S(1)} %get-tuple-element.44.after_hbm.refs_0_, ...), custom_call_target="tpu_custom_call" | custom-call | tf_op jit(solution)/shard_map/pallas_call | solution.py:362
  25.2 0.1 collective-permute-start.2
  25.3 0.5 collective-permute-start.3
  25.8 0.1 collective-permute-start.4
  25.8 0.4 collective-permute-start.5
  26.3 0.6 shard_map.94.mask_ref
  26.9 1.8 %all-to-all-done.recv_ref = bf16[16,16,768]{2,1,0:T(8,128)(2,1)S(1)} async-done(((bf16[16,16,768]{2,1,0:T(8,128)(2,1)}), bf16[16,16,768]{2,1,0:T(8,128)(2,1)S(1)}, u32[]{:S(2)}, u32[]{:S(2)}) %all-to-all-start) | async-done | bytes 393248 | tf_op jit(solution)/shard_map/all_to_all | solution.py:360
  28.7 2.7 %shard_map.97 = (bf16[16,16,768]{2,1,0:T(8,128)(2,1)}, f32[16,256]{1,0:T(8,128)S(1)}) custom-call(bf16[1024,256]{1,0:T(8,128)(2,1)S(1)} %shard_map.94.mask_ref, bf16[16,16,768]{2,1,0:T(8,128)(2,1)S(1)} %all-to-all-done.recv_ref, bf16[1024,512]{1,0:T(8,128)(2,1)} %bitcast.10), custom_call_target="tpu_custom_call" | custom-call | flops 536870912 | bytes 3145728 | tf_op jit(solution)/shard_map/pallas_call | solution.py:378
  31.4 3.6 %all-to-all-start.1 = ((bf16[16,16,768]{2,1,0:T(8,128)(2,1)}), bf16[16,16,768]{2,1,0:T(8,128)(2,1)S(1)}, u32[]{:S(2)}, u32[]{:S(2)}) async-start(bf16[16,16,768]{2,1,0:T(8,128)(2,1)} %get-tuple-element.24), calls=%async_computation.1 | async-start | bytes 786432 | tf_op jit(solution)/shard_map/all_to_all | solution.py:387
  35.0 0.0 collective-permute-done.2.refs_3_
  35.0 0.0 collective-permute-done.3.refs_4_
  35.0 0.0 collective-permute-done.4.refs_5_
  35.0 0.0 collective-permute-done.5.refs_6_
  35.0 0.4 collective-permute-done.1.refs_1_
  35.4 2.1 %shard_map.99 = (bf16[16,4096]{1,0:T(8,128)(2,1)S(1)}, bf16[16,4096]{1,0:T(8,128)(2,1)S(1)}, bf16[16,4096]{1,0:T(8,128)(2,1)}, bf16[16,4096]{1,0:T(8,128)(2,1)},...) custom-call(bf16[64,4096]{1,0:T(8,128)(2,1)S(1)} %get-tuple-element.44.after_hbm.refs_0_, ...), custom_call_target="tpu_custom_call" | custom-call | bytes 6291456 | tf_op jit(solution)/shard_map/pallas_call | solution.py:324
  37.5 0.0 copy-start.1
  37.5 1.8 %collective-permute-start.9 = (bf16[64,4096]{1,0:T(8,128)(2,1)S(1)}, bf16[64,4096]{1,0:T(8,128)(2,1)S(1)}, u32[]{:S(2)}, u32[]{:S(2)}) collective-permute-start(bf16[64,4096]{1,0:T(8,128)(2,1)S(1)} %get-tuple-element.37), channel_id=1, source_target_pairs={{0,2},{1,3},{2,0},{3,1},{4,6},{5,7},{6,4},{7,5},{8,10},{9,11},{10,... | collective-permute-start | bytes 1572872 | tf_op jit(solution)/shard_map/ppermute | solution.py:315
  39.3 1.6 %collective-permute-start.6 = (bf16[16,4096]{1,0:T(8,128)(2,1)S(1)}, bf16[16,4096]{1,0:T(8,128)(2,1)S(1)}, u32[]{:S(2)}, u32[]{:S(2)}) collective-permute-start(bf16[16,4096]{1,0:T(8,128)(2,1)S(1)} %get-tuple-element.33), channel_id=1, source_target_pairs={{0,4},{1,5},{2,6},{3,7},{4,0},{5,1},{6,2},{7,3},{8,12},{9,13},{10,... | collective-permute-start | bytes 393224 | tf_op jit(solution)/shard_map/ppermute | solution.py:315
  40.8 2.0 %collective-permute-start.7 = (bf16[16,4096]{1,0:T(8,128)(2,1)}, bf16[16,4096]{1,0:T(8,128)(2,1)S(1)}, u32[]{:S(2)}, u32[]{:S(2)}) collective-permute-start(bf16[16,4096]{1,0:T(8,128)(2,1)} %get-tuple-element.34), channel_id=1, source_target_pairs={{0,8},{1,9},{2,10},{3,11},{4,12},{5,13},{6,14},{7,15},{8,0},{9,1},... | collective-permute-start | bytes 393224 | tf_op jit(solution)/shard_map/ppermute | solution.py:315
  42.8 0.8 %collective-permute-start.8 = (bf16[16,4096]{1,0:T(8,128)(2,1)}, bf16[16,4096]{1,0:T(8,128)(2,1)S(1)}, u32[]{:S(2)}, u32[]{:S(2)}) collective-permute-start(bf16[16,4096]{1,0:T(8,128)(2,1)} %get-tuple-element.35), channel_id=1, source_target_pairs={{0,12},{1,13},{2,14},{3,15},{4,8},{5,9},{6,10},{7,11},{8,4},{9,5},... | collective-permute-start | bytes 393224 | tf_op jit(solution)/shard_map/ppermute | solution.py:315
  43.7 10.0 %collective-permute-done.9.refs_1_ = bf16[64,4096]{1,0:T(8,128)(2,1)S(1)} collective-permute-done((bf16[64,4096]{1,0:T(8,128)(2,1)S(1)}, bf16[64,4096]{1,0:T(8,128)(2,1)S(1)}, u32[]{:S(2)}, u32[]{:S(2)}) %collective-permute-start.9) | collective-permute-done | bytes 524320 | tf_op jit(solution)/shard_map/ppermute | solution.py:315
  53.6 0.8 %shard_map.100 = (bf16[16,4096]{1,0:T(8,128)(2,1)S(1)}, bf16[16,4096]{1,0:T(8,128)(2,1)}, bf16[16,4096]{1,0:T(8,128)(2,1)}, bf16[16,4096]{1,0:T(8,128)(2,1)}) custom-call(bf16[64,4096]{1,0:T(8,128)(2,1)S(1)} %get-tuple-element.36.refs_0_, bf16[64,4096]{1,0:T(8,128)(2,1)S(1)} %collective-permute-done.9.refs_1_), custom_call_target="tpu_custom_call" | custom-call | bytes 2097152 | tf_op jit(solution)/shard_map/pallas_call | solution.py:324
  54.4 2.2 %collective-permute-start.10 = (bf16[16,4096]{1,0:T(8,128)(2,1)}, bf16[16,4096]{1,0:T(8,128)(2,1)S(1)}, u32[]{:S(2)}, u32[]{:S(2)}) collective-permute-start(bf16[16,4096]{1,0:T(8,128)(2,1)} %get-tuple-element.39), channel_id=1, source_target_pairs={{0,4},{1,5},{2,6},{3,7},{4,0},{5,1},{6,2},{7,3},{8,12},{9,13},{10,... | collective-permute-start | bytes 393224 | tf_op jit(solution)/shard_map/ppermute | solution.py:315
  56.7 1.5 %collective-permute-start.11 = (bf16[16,4096]{1,0:T(8,128)(2,1)}, bf16[16,4096]{1,0:T(8,128)(2,1)S(1)}, u32[]{:S(2)}, u32[]{:S(2)}) collective-permute-start(bf16[16,4096]{1,0:T(8,128)(2,1)} %get-tuple-element.40), channel_id=1, source_target_pairs={{0,8},{1,9},{2,10},{3,11},{4,12},{5,13},{6,14},{7,15},{8,0},{9,1},... | collective-permute-start | bytes 393224 | tf_op jit(solution)/shard_map/ppermute | solution.py:315
  58.2 0.0 collective-permute-done.6.refs_1_
  58.2 0.9 %collective-permute-start.12 = (bf16[16,4096]{1,0:T(8,128)(2,1)}, bf16[16,4096]{1,0:T(8,128)(2,1)S(1)}, u32[]{:S(2)}, u32[]{:S(2)}) collective-permute-start(bf16[16,4096]{1,0:T(8,128)(2,1)} %get-tuple-element.41), channel_id=1, source_target_pairs={{0,12},{1,13},{2,14},{3,15},{4,8},{5,9},{6,10},{7,11},{8,4},{9,5},... | collective-permute-start | bytes 393224 | tf_op jit(solution)/shard_map/ppermute | solution.py:315
  59.0 1.8 %shard_map.102 = f32[1024,512]{1,0:T(8,128)} custom-call(bf16[1024,256]{1,0:T(8,128)(2,1)S(1)} %shard_map.94.mask_ref, f32[16,256]{1,0:T(8,128)S(1)} %get-tuple-element.42.back_ref, bf16[16,16,768]{2,1,0:T(8,128)(2,1)S(1)} %all-to-all-done.recv_ref), custom_call_target="tpu_custom_call" | custom-call | flops 268435456 | bytes 3145728 | tf_op jit(solution)/shard_map/pallas_call | solution.py:388
  60.8 0.0 all-to-all-done.1.recv_ref
  60.8 0.0 copy-done.1
  60.8 2.1 %shard_map.103 = f32[640,1024]{1,0:T(8,128)} custom-call(bf16[1024,256]{1,0:T(8,128)(2,1)S(1)} %shard_map.94.mask_ref, bf16[16,16,768]{2,1,0:T(8,128)(2,1)S(1)} %all-to-all-done.1.recv_ref, bf16[640,256]{1,0:T(8,128)(2,1)S(1)} %copy-done.1), custom_call_target="tpu_custom_call" | custom-call | flops 335544320 | bytes 3145728 | tf_op jit(solution)/shard_map/pallas_call | solution.py:395
  62.9 0.0 collective-permute-done.7.refs_2_
  62.9 0.0 collective-permute-done.8.refs_3_
  62.9 0.0 collective-permute-done.10.refs_5_
  62.9 6.2 %collective-permute-done.11.refs_6_ = bf16[16,4096]{1,0:T(8,128)(2,1)S(1)} collective-permute-done((bf16[16,4096]{1,0:T(8,128)(2,1)}, bf16[16,4096]{1,0:T(8,128)(2,1)S(1)}, u32[]{:S(2)}, u32[]{:S(2)}) %collective-permute-start.11) | collective-permute-done | bytes 131104 | tf_op jit(solution)/shard_map/ppermute | solution.py:315
  69.1 0.0 collective-permute-done.12.refs_7_
  69.1 1.2 %shard_map.101 = bf16[16,8192]{1,0:T(8,128)(2,1)} custom-call(bf16[16,16,768]{2,1,0:T(8,128)(2,1)S(1)} %all-to-all-done.1.recv_ref, bf16[16,8192]{1,0:T(8,128)(2,1)S(1)} %copy-done.3, bf16[16,4096]{1,0:T(8,128)(2,1)S(1)} %get-tuple-element.32.refs_0_, bf16[16,4096]{1,0:T(8,128)(2,1)S(1)} %collective-permute-done.6.refs_1_, ...), custom_call_target="tpu_custom_call" | custom-call | bytes 2097152 | tf_op jit(solution)/shard_map/pallas_call | solution.py:403
Async XLA Ops:
  0.6 1.0 %copy-start = (bf16[640,256]{1,0:T(8,128)(2,1)S(1)}, bf16[640,256]{1,0:T(8,128)(2,1)}, u32[]{:S(2)}) copy-start(bf16[640,256]{1,0:T(8,128)(2,1)} %cot_ref.1) | copy-start | bytes 983044
  1.6 5.4 %copy-start.2 = (bf16[640,1024]{1,0:T(8,128)(2,1)S(1)}, bf16[640,1024]{1,0:T(8,128)(2,1)}, u32[]{:S(2)}) copy-start(bf16[640,1024]{1,0:T(8,128)(2,1)} %up_hbm.1) | copy-start | bytes 3932164
  1.6 5.4 %copy-start.3 = (bf16[16,8192]{1,0:T(8,128)(2,1)S(1)}, bf16[16,8192]{1,0:T(8,128)(2,1)}, u32[]{:S(2)}) copy-start(bf16[16,8192]{1,0:T(8,128)(2,1)} %tok_ref.1) | copy-start | bytes 786436
  1.6 5.4 %copy-start.4 = (s32[64]{0:T(128)S(1)}, s32[64]{0:T(128)}, u32[]{:S(2)}) copy-start(s32[64]{0:T(128)} %param.12) | copy-start | bytes 772
  1.6 5.4 %copy-start.5 = (s32[64]{0:T(128)S(1)}, s32[64]{0:T(128)}, u32[]{:S(2)}) copy-start(s32[64]{0:T(128)} %param.13) | copy-start | bytes 772
  6.5 10.0 %collective-permute-start = (bf16[128,4096]{1,0:T(8,128)(2,1)}, bf16[128,4096]{1,0:T(8,128)(2,1)}, u32[]{:S(2)}, u32[]{:S(2)}) collective-permute-start(bf16[128,4096]{1,0:T(8,128)(2,1)} %get-tuple-element.26), channel_id=1, source_target_pairs={{0,1},{1,0},{2,3},{3,2},{4,5},{5,4},{6,7},{7,6},{8,9},{9,8},{10,11... | collective-permute-start | bytes 3145736 | tf_op jit(solution)/shard_map/ppermute | solution.py:315
  9.4 19.3 %all-to-all-start = ((bf16[16,16,768]{2,1,0:T(8,128)(2,1)}), bf16[16,16,768]{2,1,0:T(8,128)(2,1)S(1)}, u32[]{:S(2)}, u32[]{:S(2)}) async-start(bf16[16,16,768]{2,1,0:T(8,128)(2,1)} %shard_map.96), calls=%async_computation | async-start | bytes 786432 | tf_op jit(solution)/shard_map/all_to_all | solution.py:360
  18.7 16.7 %collective-permute-start.1 = (bf16[64,4096]{1,0:T(8,128)(2,1)}, bf16[64,4096]{1,0:T(8,128)(2,1)}, u32[]{:S(2)}, u32[]{:S(2)}) collective-permute-start(bf16[64,4096]{1,0:T(8,128)(2,1)} %get-tuple-element.43), channel_id=1, source_target_pairs={{0,2},{1,3},{2,0},{3,1},{4,6},{5,7},{6,4},{7,5},{8,10},{9,11},{10,... | collective-permute-start | bytes 1572872 | tf_op jit(solution)/shard_map/ppermute | solution.py:315
  25.2 9.8 %collective-permute-start.2 = (bf16[32,4096]{1,0:T(8,128)(2,1)}, bf16[32,4096]{1,0:T(8,128)(2,1)S(1)}, u32[]{:S(2)}, u32[]{:S(2)}) collective-permute-start(bf16[32,4096]{1,0:T(8,128)(2,1)} %get-tuple-element.28), channel_id=1, source_target_pairs={{0,1},{1,0},{2,3},{3,2},{4,5},{5,4},{6,7},{7,6},{8,9},{9,8},{10,11... | collective-permute-start | bytes 786440 | tf_op jit(solution)/shard_map/ppermute | solution.py:368
  25.3 9.7 %collective-permute-start.3 = (bf16[32,4096]{1,0:T(8,128)(2,1)}, bf16[32,4096]{1,0:T(8,128)(2,1)}, u32[]{:S(2)}, u32[]{:S(2)}) collective-permute-start(bf16[32,4096]{1,0:T(8,128)(2,1)} %get-tuple-element.29), channel_id=1, source_target_pairs={{0,1},{1,0},{2,3},{3,2},{4,5},{5,4},{6,7},{7,6},{8,9},{9,8},{10,11... | collective-permute-start | bytes 786440 | tf_op jit(solution)/shard_map/ppermute | solution.py:368
  25.8 9.2 %collective-permute-start.4 = (bf16[32,4096]{1,0:T(8,128)(2,1)}, bf16[32,4096]{1,0:T(8,128)(2,1)}, u32[]{:S(2)}, u32[]{:S(2)}) collective-permute-start(bf16[32,4096]{1,0:T(8,128)(2,1)} %get-tuple-element.30), channel_id=1, source_target_pairs={{0,1},{1,0},{2,3},{3,2},{4,5},{5,4},{6,7},{7,6},{8,9},{9,8},{10,11... | collective-permute-start | bytes 786440 | tf_op jit(solution)/shard_map/ppermute | solution.py:368
  25.8 9.2 %collective-permute-start.5 = (bf16[32,4096]{1,0:T(8,128)(2,1)}, bf16[32,4096]{1,0:T(8,128)(2,1)}, u32[]{:S(2)}, u32[]{:S(2)}) collective-permute-start(bf16[32,4096]{1,0:T(8,128)(2,1)} %get-tuple-element.31), channel_id=1, source_target_pairs={{0,1},{1,0},{2,3},{3,2},{4,5},{5,4},{6,7},{7,6},{8,9},{9,8},{10,11... | collective-permute-start | bytes 786440 | tf_op jit(solution)/shard_map/ppermute | solution.py:368
  31.4 29.4 %all-to-all-start.1 = ((bf16[16,16,768]{2,1,0:T(8,128)(2,1)}), bf16[16,16,768]{2,1,0:T(8,128)(2,1)S(1)}, u32[]{:S(2)}, u32[]{:S(2)}) async-start(bf16[16,16,768]{2,1,0:T(8,128)(2,1)} %get-tuple-element.24), calls=%async_computation.1 | async-start | bytes 786432 | tf_op jit(solution)/shard_map/all_to_all | solution.py:387
  37.5 23.3 %copy-start.1 = (bf16[640,256]{1,0:T(8,128)(2,1)S(1)}, bf16[640,256]{1,0:T(8,128)(2,1)}, u32[]{:S(2)}) copy-start(bf16[640,256]{1,0:T(8,128)(2,1)} %cot_ref.1) | copy-start | bytes 983044
  37.5 16.1 %collective-permute-start.9 = (bf16[64,4096]{1,0:T(8,128)(2,1)S(1)}, bf16[64,4096]{1,0:T(8,128)(2,1)S(1)}, u32[]{:S(2)}, u32[]{:S(2)}) collective-permute-start(bf16[64,4096]{1,0:T(8,128)(2,1)S(1)} %get-tuple-element.37), channel_id=1, source_target_pairs={{0,2},{1,3},{2,0},{3,1},{4,6},{5,7},{6,4},{7,5},{8,10},{9,11},{10,... | collective-permute-start | bytes 1572872 | tf_op jit(solution)/shard_map/ppermute | solution.py:315
  39.3 18.9 %collective-permute-start.6 = (bf16[16,4096]{1,0:T(8,128)(2,1)S(1)}, bf16[16,4096]{1,0:T(8,128)(2,1)S(1)}, u32[]{:S(2)}, u32[]{:S(2)}) collective-permute-start(bf16[16,4096]{1,0:T(8,128)(2,1)S(1)} %get-tuple-element.33), channel_id=1, source_target_pairs={{0,4},{1,5},{2,6},{3,7},{4,0},{5,1},{6,2},{7,3},{8,12},{9,13},{10,... | collective-permute-start | bytes 393224 | tf_op jit(solution)/shard_map/ppermute | solution.py:315
  40.8 22.0 %collective-permute-start.7 = (bf16[16,4096]{1,0:T(8,128)(2,1)}, bf16[16,4096]{1,0:T(8,128)(2,1)S(1)}, u32[]{:S(2)}, u32[]{:S(2)}) collective-permute-start(bf16[16,4096]{1,0:T(8,128)(2,1)} %get-tuple-element.34), channel_id=1, source_target_pairs={{0,8},{1,9},{2,10},{3,11},{4,12},{5,13},{6,14},{7,15},{8,0},{9,1},... | collective-permute-start | bytes 393224 | tf_op jit(solution)/shard_map/ppermute | solution.py:315
  42.8 20.0 %collective-permute-start.8 = (bf16[16,4096]{1,0:T(8,128)(2,1)}, bf16[16,4096]{1,0:T(8,128)(2,1)S(1)}, u32[]{:S(2)}, u32[]{:S(2)}) collective-permute-start(bf16[16,4096]{1,0:T(8,128)(2,1)} %get-tuple-element.35), channel_id=1, source_target_pairs={{0,12},{1,13},{2,14},{3,15},{4,8},{5,9},{6,10},{7,11},{8,4},{9,5},... | collective-permute-start | bytes 393224 | tf_op jit(solution)/shard_map/ppermute | solution.py:315
  54.4 8.5 %collective-permute-start.10 = (bf16[16,4096]{1,0:T(8,128)(2,1)}, bf16[16,4096]{1,0:T(8,128)(2,1)S(1)}, u32[]{:S(2)}, u32[]{:S(2)}) collective-permute-start(bf16[16,4096]{1,0:T(8,128)(2,1)} %get-tuple-element.39), channel_id=1, source_target_pairs={{0,4},{1,5},{2,6},{3,7},{4,0},{5,1},{6,2},{7,3},{8,12},{9,13},{10,... | collective-permute-start | bytes 393224 | tf_op jit(solution)/shard_map/ppermute | solution.py:315
  56.7 12.4 %collective-permute-start.11 = (bf16[16,4096]{1,0:T(8,128)(2,1)}, bf16[16,4096]{1,0:T(8,128)(2,1)S(1)}, u32[]{:S(2)}, u32[]{:S(2)}) collective-permute-start(bf16[16,4096]{1,0:T(8,128)(2,1)} %get-tuple-element.40), channel_id=1, source_target_pairs={{0,8},{1,9},{2,10},{3,11},{4,12},{5,13},{6,14},{7,15},{8,0},{9,1},... | collective-permute-start | bytes 393224 | tf_op jit(solution)/shard_map/ppermute | solution.py:315
  58.2 10.9 %collective-permute-start.12 = (bf16[16,4096]{1,0:T(8,128)(2,1)}, bf16[16,4096]{1,0:T(8,128)(2,1)S(1)}, u32[]{:S(2)}, u32[]{:S(2)}) collective-permute-start(bf16[16,4096]{1,0:T(8,128)(2,1)} %get-tuple-element.41), channel_id=1, source_target_pairs={{0,12},{1,13},{2,14},{3,15},{4,8},{5,9},{6,10},{7,11},{8,4},{9,5},... | collective-permute-start | bytes 393224 | tf_op jit(solution)/shard_map/ppermute | solution.py:315
